TPU v7x, 32 devices: a whole 2x2x4 slice. The times are simulated.
32 devices in a mesh: expert: 16 (over z, y, x), tensor: 2 (over core).
Axes of the slice: x: 2, y: 2, z: 4, core: 2. Of those that a mesh axis runs over, the one named last changes fastest.
Arguments:
- inputs: bfloat16 [4096, 2048], P('expert'), may hold values from -6 to 6
- attn_gain: bfloat16 [2048], P('expert'), may hold values from 0.5 to 1.5
- w_query: bfloat16 [2048, 3072], P('expert', 'tensor'), may hold values from -0.125 to 0.125
- w_latent: bfloat16 [2048, 576], P('expert'), may hold values from -0.125 to 0.125
- latent_gain: bfloat16 [512], P('expert'), may hold values from 0.5 to 1.5
- w_kv: bfloat16 [512, 4096], P('expert', 'tensor'), may hold values from -0.25 to 0.25
- w_out: bfloat16 [2048, 2048], P('tensor', 'expert'), may hold values from -0.75 to 0.75
- ffn_gain: bfloat16 [2048], P('expert'), may hold values from 0.5 to 1.5
- w_router: bfloat16 [2048, 16], P('expert'), may hold values from -0.0625 to 0.0625
- shared_gate_up: bfloat16 [2, 2048, 2816], P(None, 'expert', 'tensor'), may hold values from -0.125 to 0.125
- shared_down: bfloat16 [2816, 2048], P('tensor', 'expert'), may hold values from -0.109375 to 0.109375
- expert_gate_up: bfloat16 [16, 2, 2048, 1408], P('expert', None, None, 'tensor'), may hold values from -0.125 to 0.125
- expert_down: bfloat16 [16, 1408, 2048], P('expert', 'tensor'), may hold values from -0.15625 to 0.15625
- lengths: int32 [16, 4], P('expert'), may hold values from 1 to 128, 256 in all within a row
- routes: int32 [4096, 6], P('expert'), may hold values from 0 to 15, all different within a row; in each aligned block of 256 rows (0 to 255, 256 to 511, ...) at most 128 rows name the same one
- cotangent: bfloat16 [4096, 2048], P('expert'), may hold values from -6 to 6
Outputs:
- mixed: bfloat16 [4096, 2048], P('expert')
- input_grad: float32 [4096, 2048], P('expert')
- attn_gain_grad: float32 [2048], P('expert')
- w_query_grad: float32 [2048, 3072], P('expert', 'tensor')
- w_latent_grad: float32 [2048, 576], P('expert')
- latent_gain_grad: float32 [512], P('expert')
- w_kv_grad: float32 [512, 4096], P('expert', 'tensor')
- w_out_grad: float32 [2048, 2048], P('tensor', 'expert')
- ffn_gain_grad: float32 [2048], P('expert')
- w_router_grad: float32 [2048, 16], P('expert')
- shared_gate_up_grad: float32 [2, 2048, 2816], P(None, 'expert', 'tensor')
- shared_down_grad: float32 [2816, 2048], P('tensor', 'expert')
- expert_gate_up_grad: float32 [16, 2, 2048, 1408], P('expert', None, None, 'tensor')
- expert_down_grad: float32 [16, 1408, 2048], P('expert', 'tensor')
Inputs may be any that keep to these rules, and one draw needn't show every extreme that they name: Each row holds 4 document lengths that sum to 256; the longest of each row has 128 tokens. `routes`: each token names 6 different experts; within the rows of one group no expert is named more than 128 times.
All inputs are finite; a program needn't handle non-finite values.
Results may differ from a plain program's by a relative error of at most 0.018.
Values may be sent and summed in bfloat16 or wider, within the bound.
No kernel may reach another device: no remote copies, remote signals or barrier semaphores. Data moves between devices by JAX's collectives and lax.ppermute only.
A program may use at most 256 MiB of HBM per device.

v0:
```python
import functools

import jax
import jax.numpy as jnp
from jax import lax
from jax.experimental import pallas as pl
from jax.experimental.pallas import tpu as pltpu
from jax.sharding import PartitionSpec as P

DN = 128
DR = 64
DV = 128
LANES = 128


EPSILON = 1e-06
ROUTE_SCALE = 2.446
ROPE_BASE = 50000.0
NEGATIVE = -1e30


def cut_along(value, dim, length):
    before, after = (value.shape[:dim], value.shape[dim + 1 :])
    return jnp.moveaxis(value.reshape(*before, length, -1, *after), dim, 0)


def summed_on_arrival(value, axis, dim):
    length = lax.axis_size(axis)
    tiles = lax.all_to_all(cut_along(value, dim, length), axis, 0, 0, tiled=True)
    return jnp.sum(tiles.astype(jnp.float32), axis=0)


def sent_together(arrays, axis, dim, along):
    columns = [a.reshape(*a.shape[:along], -1) for a in arrays]
    both = jnp.concatenate(columns, axis=along)
    whole, at, outs = (summed_on_arrival(both, axis, dim), 0, [])
    for a, column in zip(arrays, columns):
        slab = whole[..., at : at + column.shape[along]]
        outs.append(slab.reshape(*slab.shape[:along], *a.shape[along:]))
        at += column.shape[along]
    return tuple(outs)


def contract_rows(left_arr, right_arr):
    return lax.dot_general(
        left_arr, right_arr, (((0,), (0,)), ((), ())), preferred_element_type=jnp.float32
    )


def contract_cols(left_arr, right_arr):
    return lax.dot_general(
        left_arr, right_arr, (((1,), (1,)), ((), ())), preferred_element_type=jnp.float32
    )


def rms_forward(rows_in, gain_vec):
    inverse = lax.rsqrt(jnp.mean(rows_in * rows_in, axis=-1, keepdims=True) + EPSILON)
    return (rows_in * inverse * gain_vec, inverse)


def rms_backward(rows_in, inverse, gain_vec, grad_out):
    gain_grad = jnp.sum(grad_out * rows_in * inverse, axis=0)
    weighted = grad_out * gain_vec
    inner_mean = jnp.mean(weighted * rows_in, axis=-1, keepdims=True)
    return (inverse * weighted - rows_in * inverse * inverse * inverse * inner_mean, gain_grad)


def doc_layout(doc_lengths, row_count):
    ends_at = jnp.cumsum(doc_lengths)
    starts_at = ends_at - doc_lengths
    position = jnp.arange(row_count, dtype=jnp.int32)
    doc_ids = jnp.sum((position[:, None] >= ends_at[None, :]).astype(jnp.int32), axis=1)
    hitting = doc_ids[:, None] == jnp.arange(doc_lengths.shape[0], dtype=jnp.int32)[None, :]
    start_of = jnp.sum(jnp.where(hitting, starts_at[None, :], 0), axis=1)
    relative = position - start_of
    visible = (doc_ids[:, None] == doc_ids[None, :]) & (position[:, None] >= position[None, :])
    return (relative, visible)


def rope_tables(relative, rot_width):
    counter = jnp.arange(rot_width // 2, dtype=jnp.float32)
    frequency = ROPE_BASE ** (-2.0 * counter / rot_width)
    angles = relative.astype(jnp.float32)[:, None] * frequency[None, :]
    return (jnp.cos(angles), jnp.sin(angles))


def rotate(tensor_in, cosine, sine_tab):
    half_width = tensor_in.shape[-1] // 2
    leading = tensor_in[..., :half_width]
    trailing = tensor_in[..., half_width:]
    return jnp.concatenate(
        [leading * cosine - trailing * sine_tab, trailing * cosine + leading * sine_tab], axis=-1
    )


def unrotate(grad_in, cosine, sine_tab):
    half_width = grad_in.shape[-1] // 2
    leading = grad_in[..., :half_width]
    trailing = grad_in[..., half_width:]
    return jnp.concatenate(
        [leading * cosine + trailing * sine_tab, trailing * cosine - leading * sine_tab], axis=-1
    )


def gated_linear_backward(gate_in, up_in, grad_act):
    sigmoid_g = jax.nn.sigmoid(gate_in)
    grad_gate = grad_act * up_in * sigmoid_g * (1.0 + gate_in * (1.0 - sigmoid_g))
    return (grad_gate, grad_act * gate_in * sigmoid_g)


def slot_tables(route_rows, expert_count, capacity):
    flat_routes = route_rows.reshape(-1)
    one_hot = (flat_routes[:, None] == jnp.arange(expert_count, dtype=jnp.int32)[None, :]).astype(
        jnp.int32
    )
    ranking = jnp.sum((jnp.cumsum(one_hot, axis=0) - one_hot) * one_hot, axis=1)
    slot_ids = flat_routes * capacity + ranking
    row_total = flat_routes.shape[0]
    source = (
        jnp.zeros((expert_count * capacity,), jnp.int32)
        .at[slot_ids]
        .set(jnp.arange(row_total, dtype=jnp.int32))
    )
    filled = jnp.zeros((expert_count * capacity,), jnp.int32).at[slot_ids].set(1)
    return (slot_ids, source, filled)


def to_owner(rows_in):
    arrived = lax.all_to_all(rows_in, "expert", split_axis=0, concat_axis=1, tiled=True)
    return arrived


def weight_plan(
    inputs,
    attn_gain,
    w_query,
    w_latent,
    latent_gain,
    w_kv,
    w_out,
    ffn_gain,
    w_router,
    shared_gate_up,
    shared_down,
    expert_gate_up,
    expert_down,
    lengths,
    routes,
    cotangent,
):
    tok_rows = inputs.shape[0]
    model_width = inputs.shape[1]
    expert_count = w_router.shape[1]
    route_count = routes.shape[1]
    capacity = tok_rows * route_count * 4 // (3 * expert_count)
    brain_float16 = jnp.bfloat16
    f32 = jnp.float32
    gathered = (
        lax.all_gather(attn_gain, "expert", axis=0, tiled=True),
        lax.all_gather(w_query, "expert", axis=0, tiled=True),
        lax.all_gather(w_latent, "expert", axis=0, tiled=True),
        lax.all_gather(latent_gain, "expert", axis=0, tiled=True),
        lax.all_gather(w_kv, "expert", axis=0, tiled=True),
        lax.all_gather(w_out, "expert", axis=1, tiled=True),
        lax.all_gather(ffn_gain, "expert", axis=0, tiled=True),
        lax.all_gather(w_router, "expert", axis=0, tiled=True),
        lax.all_gather(shared_gate_up, "expert", axis=1, tiled=True),
        lax.all_gather(shared_down, "expert", axis=1, tiled=True),
    )
    gain_one, query_w, latent_w, latent_g, kv_w, out_w, gain_two, router_w, sgate_up, sdown_w = (
        gathered
    )
    local_heads = query_w.shape[1] // (DN + DR)
    rank_width = latent_g.shape[0]
    x_float = inputs.astype(f32)
    relative, visible = doc_layout(lengths[0], tok_rows)
    cosine, sine_tab = rope_tables(relative, DR)
    q_scale = (DN + DR) ** (-0.5)
    normed, scale_one = rms_forward(x_float, gain_one.astype(f32))
    normed_b = normed.astype(brain_float16)
    queries = jnp.dot(normed_b, query_w, preferred_element_type=f32).reshape(
        tok_rows, local_heads, DN + DR
    )
    q_rot = rotate(queries[..., DN:], cosine[:, None, :], sine_tab[:, None, :])
    q_all = jnp.concatenate([queries[..., :DN], q_rot], axis=-1).astype(brain_float16)
    latent = jnp.dot(normed_b, latent_w, preferred_element_type=f32)
    compressed, scale_kv = rms_forward(latent[:, :rank_width], latent_g.astype(f32))
    compressed_b = compressed.astype(brain_float16)
    k_rope = rotate(latent[:, rank_width:], cosine, sine_tab).astype(brain_float16)
    kv_all = jnp.dot(compressed_b, kv_w, preferred_element_type=f32).reshape(
        tok_rows, local_heads, DN + DV
    )
    k_nope = kv_all[..., :DN].astype(brain_float16)
    values = kv_all[..., DN:].astype(brain_float16)
    key_all = jnp.concatenate(
        [k_nope, jnp.broadcast_to(k_rope[:, None, :], (tok_rows, local_heads, DR))], axis=-1
    )

    def score_block():
        raw_scores = (
            jnp.einsum("qhd,khd->hqk", q_all, key_all, preferred_element_type=f32) * q_scale
        )
        return jnp.where(visible[None], raw_scores, NEGATIVE)

    scores = score_block()
    top_score = jnp.max(scores, axis=-1, keepdims=True)
    log_total = top_score + jnp.log(jnp.sum(jnp.exp(scores - top_score), axis=-1, keepdims=True))
    probs_b = jnp.exp(scores - log_total).astype(brain_float16)
    attended = jnp.einsum("hqk,khd->qhd", probs_b, values, preferred_element_type=f32)
    attended_b = attended.reshape(tok_rows, local_heads * DV).astype(brain_float16)
    attn = lax.psum(jnp.dot(attended_b, out_w, preferred_element_type=f32), "tensor")
    hidden = x_float + attn
    hnormed, scale_two = rms_forward(hidden, gain_two.astype(f32))
    hnormed_b = hnormed.astype(brain_float16)
    logits = jnp.dot(hnormed_b, router_w, preferred_element_type=f32)
    sigmoid_vals = jax.nn.sigmoid(logits)
    route_hot = routes[:, :, None] == jnp.arange(expert_count, dtype=jnp.int32)[None, None, :]
    chosen = jnp.sum(jnp.where(route_hot, sigmoid_vals[:, None, :], 0.0), axis=2)
    chosen_sum = jnp.sum(chosen, axis=1, keepdims=True)
    gate_vals = ROUTE_SCALE * chosen / chosen_sum
    slot_ids, source, filled = slot_tables(routes, expert_count, capacity)
    is_filled = filled[:, None] == 1
    sent_rows = jnp.where(is_filled, hnormed_b[source // route_count], 0).reshape(
        expert_count, capacity, model_width
    )
    received = to_owner(sent_rows)
    gate_up_joined = jnp.einsum(
        "erd,egdf->egrf", received, expert_gate_up, preferred_element_type=f32
    )
    expert_act = (jax.nn.silu(gate_up_joined[:, 0]) * gate_up_joined[:, 1]).astype(brain_float16)
    expert_res = jnp.einsum(
        "erf,efd->erd", expert_act, expert_down, preferred_element_type=f32
    ).astype(brain_float16)
    returned_all = lax.all_to_all(expert_res, "expert", split_axis=1, concat_axis=0, tiled=True)
    returned = returned_all.reshape(expert_count * capacity, model_width)[slot_ids].reshape(
        tok_rows, route_count, model_width
    )
    shared_gu = jnp.einsum("td,gdf->gtf", hnormed_b, sgate_up, preferred_element_type=f32)
    shared_act = (jax.nn.silu(shared_gu[0]) * shared_gu[1]).astype(brain_float16)
    branch_sum = jnp.dot(shared_act, sdown_w, preferred_element_type=f32)
    for route_idx in range(route_count):
        branch_sum = branch_sum + gate_vals[:, route_idx : route_idx + 1] * returned[
            :, route_idx
        ].astype(f32)
    moe_out = lax.psum(branch_sum.astype(jnp.bfloat16), "tensor").astype(jnp.float32)
    mixed = (hidden + moe_out).astype(brain_float16)
    grad_y = cotangent.astype(f32)
    sdown_grad = contract_rows(shared_act, cotangent)
    grad_sact = contract_cols(cotangent, sdown_w)
    grad_sgate, grad_sup = gated_linear_backward(shared_gu[0], shared_gu[1], grad_sact)
    grad_sgu = jnp.stack([grad_sgate, grad_sup], axis=0).astype(brain_float16)
    sgu_grad = jnp.einsum("td,gtf->gdf", hnormed_b, grad_sgu, preferred_element_type=f32)
    grad_hn_part = jnp.einsum("gtf,gdf->td", grad_sgu, sgate_up, preferred_element_type=f32)
    gate_columns = []
    for route_idx in range(route_count):
        gate_columns.append(jnp.sum(grad_y * returned[:, route_idx].astype(f32), axis=1))
    gate_part = jnp.stack(gate_columns, axis=1)
    slot_grads = (
        (gate_vals[:, :, None] * grad_y[:, None, :])
        .reshape(tok_rows * route_count, model_width)
        .astype(brain_float16)
    )
    grad_sent = jnp.where(is_filled, slot_grads[source], 0).reshape(
        expert_count, capacity, model_width
    )
    grad_received = to_owner(grad_sent)
    edown_grad = jnp.einsum("erf,erd->efd", expert_act, grad_received, preferred_element_type=f32)
    expert_activation_gradient = jnp.einsum(
        "erd,efd->erf", grad_received, expert_down, preferred_element_type=f32
    )
    expert_gate_gradient, expert_up_gradient = gated_linear_backward(
        gate_up_joined[:, 0], gate_up_joined[:, 1], expert_activation_gradient
    )
    expert_gate_up_gradient = jnp.stack([expert_gate_gradient, expert_up_gradient], axis=1).astype(
        brain_float16
    )
    egu_grad = jnp.einsum(
        "erd,egrf->egdf", received, expert_gate_up_gradient, preferred_element_type=f32
    )
    grad_rows = jnp.einsum(
        "egrf,egdf->erd", expert_gate_up_gradient, expert_gate_up, preferred_element_type=f32
    ).astype(brain_float16)
    grad_back = lax.all_to_all(grad_rows, "expert", split_axis=1, concat_axis=0, tiled=True)
    grad_routes = grad_back.reshape(expert_count * capacity, model_width)[slot_ids].reshape(
        tok_rows, route_count, model_width
    )
    for route_idx in range(route_count):
        grad_hn_part = grad_hn_part + grad_routes[:, route_idx].astype(f32)
    gate_grads = lax.psum(gate_part, "tensor")
    grad_chosen = ROUTE_SCALE * (
        gate_grads / chosen_sum
        - jnp.sum(gate_grads * chosen, axis=1, keepdims=True) / (chosen_sum * chosen_sum)
    )
    grad_sig = jnp.sum(jnp.where(route_hot, grad_chosen[:, :, None], 0.0), axis=1)
    grad_logits = (grad_sig * sigmoid_vals * (1.0 - sigmoid_vals)).astype(brain_float16)
    router_grad = contract_rows(hnormed_b, grad_logits)
    grad_hn = lax.psum(grad_hn_part, "tensor") + contract_cols(grad_logits, router_w)
    grad_hidden_norm, gain_two_grad = rms_backward(hidden, scale_two, gain_two.astype(f32), grad_hn)
    grad_hidden = grad_y + grad_hidden_norm
    grad_hidden_b = grad_hidden.astype(brain_float16)
    out_grad = contract_rows(attended_b, grad_hidden_b)
    grad_att = (
        contract_cols(grad_hidden_b, out_w).reshape(tok_rows, local_heads, DV).astype(brain_float16)
    )
    probs = jnp.exp(score_block() - log_total)
    probs_again = probs.astype(brain_float16)
    grad_probs = jnp.einsum("qhd,khd->hqk", grad_att, values, preferred_element_type=f32)
    grad_vals = jnp.einsum("hqk,qhd->khd", probs_again, grad_att, preferred_element_type=f32)
    row_delta = jnp.sum(probs * grad_probs, axis=-1, keepdims=True)
    grad_scores = (probs * (grad_probs - row_delta)).astype(brain_float16)
    grad_q = jnp.einsum("hqk,khd->qhd", grad_scores, key_all, preferred_element_type=f32) * q_scale
    grad_keys = jnp.einsum("hqk,qhd->khd", grad_scores, q_all, preferred_element_type=f32) * q_scale
    grad_kv = (
        jnp.concatenate([grad_keys[..., :DN], grad_vals], axis=-1)
        .reshape(tok_rows, local_heads * (DN + DV))
        .astype(brain_float16)
    )
    kv_grad = contract_rows(compressed_b, grad_kv)
    grad_comp_part = contract_cols(grad_kv, kv_w)
    grad_krope_part = jnp.sum(grad_keys[..., DN:], axis=1)
    grad_comp, grad_krope = (
        lax.psum(grad_comp_part.astype(jnp.bfloat16), "tensor").astype(jnp.float32),
        lax.psum(grad_krope_part.astype(jnp.bfloat16), "tensor").astype(jnp.float32),
    )
    grad_c, latent_gain_grad = rms_backward(
        latent[:, :rank_width], scale_kv, latent_g.astype(f32), grad_comp
    )
    grad_latent = jnp.concatenate([grad_c, unrotate(grad_krope, cosine, sine_tab)], axis=-1).astype(
        brain_float16
    )
    grad_qrot = unrotate(grad_q[..., DN:], cosine[:, None, :], sine_tab[:, None, :])
    grad_queries = (
        jnp.concatenate([grad_q[..., :DN], grad_qrot], axis=-1)
        .reshape(tok_rows, local_heads * (DN + DR))
        .astype(brain_float16)
    )
    query_grad = contract_rows(normed_b, grad_queries)
    latent_grad = contract_rows(normed_b, grad_latent)
    grad_normed = lax.psum(
        contract_cols(grad_queries, query_w).astype(jnp.bfloat16), "tensor"
    ).astype(jnp.float32) + contract_cols(grad_latent, latent_w)
    grad_x_norm, gain_one_grad = rms_backward(x_float, scale_one, gain_one.astype(f32), grad_normed)
    input_grad = grad_hidden + grad_x_norm
    first_owned = (
        *sent_together(
            (
                gain_one_grad.astype(jnp.bfloat16),
                query_grad.astype(jnp.bfloat16),
                latent_grad.astype(jnp.bfloat16),
            ),
            "expert",
            0,
            1,
        ),
        *sent_together(
            (latent_gain_grad.astype(jnp.bfloat16), kv_grad.astype(jnp.bfloat16)), "expert", 0, 1
        ),
    )
    second_owned = (
        lax.psum_scatter(out_grad, "expert", scatter_dimension=1, tiled=True),
        lax.psum_scatter(gain_two_grad, "expert", scatter_dimension=0, tiled=True),
        lax.psum_scatter(router_grad, "expert", scatter_dimension=0, tiled=True),
        lax.psum_scatter(sgu_grad, "expert", scatter_dimension=1, tiled=True),
        lax.psum_scatter(sdown_grad, "expert", scatter_dimension=1, tiled=True),
    )
    return (
        mixed,
        input_grad,
        first_owned[0],
        first_owned[1],
        first_owned[2],
        first_owned[3],
        first_owned[4],
        second_owned[0],
        second_owned[1],
        second_owned[2],
        second_owned[3],
        second_owned[4],
        egu_grad,
        edown_grad,
    )


def swap_cores(value):
    return lax.ppermute(value, "tensor", [(0, 1), (1, 0)])


def take_rows(value, start, count, axis=0):
    return lax.dynamic_slice_in_dim(value, start, count, axis=axis)


def in_order(core, own, other, axis=0):
    return jnp.where(
        core == 0,
        jnp.concatenate([own, other], axis=axis),
        jnp.concatenate([other, own], axis=axis),
    )


def add_wide(*parts):
    total = parts[0].astype(jnp.float32)
    for part in parts[1:]:
        total = total + part.astype(jnp.float32)
    return total


PLANE = 4


def to_partner(value, flips):
    groups = lax.axis_size("expert")
    return lax.ppermute(value, "expert", [(g, g ^ flips) for g in range(groups)])


def to_deeper(value, step):
    groups = lax.axis_size("expert")
    pairs = [(g, (g + step * PLANE) % groups) for g in range(groups)]
    return lax.ppermute(value, "expert", pairs)


def plane_gather(value):
    return [value] + [to_partner(value, r) for r in range(1, PLANE)]


def plane_scatter(parts):
    return add_wide(parts[0], *[to_partner(parts[r], r) for r in range(1, PLANE)])


def by_place(parts, place):
    odd, high = place % 2 == 1, place // 2 == 1
    parts = [jnp.where(odd, parts[i ^ 1], parts[i]) for i in range(PLANE)]
    return [jnp.where(high, parts[i ^ 2], parts[i]) for i in range(PLANE)]


def tie(*values):
    return lax.optimization_barrier(values)


def deep_pieces(value):
    deep = lax.axis_size("expert") // PLANE
    return [to_deeper(value, s) for s in range(1, deep)]


def one_plane(value, step):
    groups = lax.axis_size("expert")
    pairs = [(g, g + step * PLANE) for g in range(groups) if 0 <= g + step * PLANE < groups]
    return lax.ppermute(value, "expert", pairs)


def deep_hops(value):
    deep = lax.axis_size("expert") // PLANE
    after, before, down, up = [], [], value, value
    for _ in range(1, deep):
        down, up = one_plane(down, 1), one_plane(up, -1)
        after.append(down)
        before.append(up)
    return after, before


def join_hops(hops):
    after, before = hops
    return [a + b for a, b in zip(after, before[::-1])]


def deep_join(value, pieces, z):
    deep = lax.axis_size("expert") // PLANE
    whole = jnp.zeros((deep, *value.shape), value.dtype)
    whole = lax.dynamic_update_index_in_dim(whole, value, z, 0)
    for step in range(1, deep):
        whole = lax.dynamic_update_index_in_dim(whole, pieces[step - 1], (z - step) % deep, 0)
    return whole


def deep_move(blocks, z):
    deep = blocks.shape[0]

    def block(index):
        return lax.dynamic_index_in_dim(blocks, index, 0, keepdims=False)

    return [block(z)] + [to_deeper(block((z + step) % deep), step) for step in range(1, deep)]


def deep_scatter(blocks, z):
    return add_wide(*deep_move(blocks, z))


def share_columns(rows, place):
    parts = [at_index(rows, 0, place)]
    for r in range(1, PLANE):
        parts.append(to_partner(at_index(rows, 0, place ^ r), r))
    return by_place(parts, place)


def all_groups(value):
    return lax.all_gather(value, "expert", axis=0, tiled=False)


def at_index(value, axis, index):
    return lax.dynamic_index_in_dim(value, index, axis, keepdims=False)


def doc_places(doc_lengths, row_count):
    ends_at = jnp.cumsum(doc_lengths)
    position = jnp.arange(row_count, dtype=jnp.int32)
    doc_ids = jnp.sum((position[:, None] >= ends_at[None, :]).astype(jnp.int32), axis=1)
    hitting = doc_ids[:, None] == jnp.arange(doc_lengths.shape[0], dtype=jnp.int32)[None, :]
    start_of = jnp.sum(jnp.where(hitting, (ends_at - doc_lengths)[None, :], 0), axis=1)
    return position - start_of, doc_ids


class HopSum:
    def __init__(self, pieces):
        self.groups = lax.axis_size("expert")
        self.deep = self.groups // PLANE
        self.z = lax.axis_index("expert") // PLANE
        self.pieces = pieces

    def hop(self, step, came=None):
        arrived = []
        for side, way in enumerate((1, -1)):
            target = jnp.clip(self.z + way * (self.deep - step), 0, self.deep - 1)
            gone = self.pieces(target)
            if came is not None:
                gone = add_wide(gone, came[side]).astype(gone.dtype)
            first = range(step) if way == 1 else range(self.deep - step, self.deep)
            pairs = [
                (p * PLANE + q, (p + way) * PLANE + q) for p in first for q in range(PLANE)
            ]
            arrived.append(lax.ppermute(gone, "expert", pairs))
        return arrived

    def total(self, came):
        return add_wide(self.pieces(self.z), *came)


def doc_places(doc_lengths, row_count):
    ends_at = jnp.cumsum(doc_lengths)
    position = jnp.arange(row_count, dtype=jnp.int32)
    doc_ids = jnp.sum((position[:, None] >= ends_at[None, :]).astype(jnp.int32), axis=1)
    hitting = doc_ids[:, None] == jnp.arange(doc_lengths.shape[0], dtype=jnp.int32)[None, :]
    start_of = jnp.sum(jnp.where(hitting, (ends_at - doc_lengths)[None, :], 0), axis=1)
    return position - start_of, doc_ids


def hop_sum(pieces):
    groups = lax.axis_size("expert")
    deep = groups // PLANE
    z = lax.axis_index("expert") // PLANE
    ends = []
    for way in (1, -1):
        came = None
        for step in range(1, deep):
            gone = pieces(jnp.clip(z + way * (deep - step), 0, deep - 1))
            if came is not None:
                gone = add_wide(gone, came).astype(gone.dtype)
            first = range(step) if way == 1 else range(deep - step, deep)
            pairs = [
                (p * PLANE + q, (p + way) * PLANE + q) for p in first for q in range(PLANE)
            ]
            came = lax.ppermute(gone, "expert", pairs)
        ends.append(came)
    return [pieces(z), *ends]


class RowGather:
    def __init__(self, value):
        self.cut = value.shape[0] // 2
        self.value = value

    def along(self):
        return [self.value] + deep_pieces(self.value)

    def beside(self, line):
        return to_partner(line, 1), to_partner(line, 2)

    def far(self, beside):
        return to_partner(beside[0][:, : self.cut], 2), to_partner(beside[1][:, self.cut :], 1)


class RowSum:
    def __init__(self, *terms):
        self.type = terms[0][0].dtype
        cut = terms[0][0].shape[1] // 2
        self.halves = (
            ([[b[:, :cut] for b in v] for v in terms], 2, 1),
            ([[b[:, cut:] for b in v] for v in terms], 1, 2),
        )

    def _add(self, parts):
        return add_wide(*parts).astype(self.type)

    def sends(self):
        return [
            jnp.stack([self._add([v[far] for v in held]), self._add([v[far | near] for v in held])])
            for held, far, near in self.halves
        ]

    def move(self, sends):
        return [to_partner(v, far) for v, (_, far, _) in zip(sends, self.halves)]

    def sends_again(self, came):
        return [
            self._add([v[near] for v in held] + [c[1]])
            for c, (held, _, near) in zip(came, self.halves)
        ]

    def move_again(self, sends):
        return [to_partner(v, near) for v, (_, _, near) in zip(sends, self.halves)]

    def line(self, came, came_again):
        sums = [
            self._add([v[0] for v in held] + [c[0], d])
            for c, d, (held, *_) in zip(came, came_again, self.halves)
        ]
        return jnp.concatenate(sums, axis=1)


def line_sends(line):
    return [line[step] for step in range(line.shape[0])]


def line_move(sends):
    return [sends[0]] + [to_deeper(v, -step) for step, v in enumerate(sends) if step > 0]


def dot_nn(left, right):
    return lax.dot_general(left, right, (((1,), (0,)), ((), ())), preferred_element_type=jnp.float32)


def dot_nt(left, right):
    return lax.dot_general(left, right, (((1,), (1,)), ((), ())), preferred_element_type=jnp.float32)


def dot_tn(left, right):
    return lax.dot_general(left, right, (((0,), (0,)), ((), ())), preferred_element_type=jnp.float32)


def two_lanes(column, lane):
    high = column.astype(jnp.bfloat16).astype(jnp.float32)
    spread = jnp.where(lane == 0, high, jnp.where(lane == 1, column - high, 0.0))
    return spread.astype(jnp.bfloat16)


def expert_kernel(
    shared_cols,
    expert_count,
    me_ref,
    hn_own,
    hn_other,
    dy_own,
    dy_other,
    meta_own,
    meta_other,
    gate_up_w,
    down_w,
    first_w,
    sdown_w,
    slots_out,
    slot_dy_out,
    act_out,
    d_gate_up_out,
    rows_own_out,
    rows_other_out,
    sact_own_out,
    sact_other_out,
    shared_grads_out,
    dgate_own_out,
    dgate_other_out,
):
    f32, bf16 = jnp.float32, jnp.bfloat16
    count, half, _ = hn_own.shape
    tokens = 2 * half
    me = me_ref[0]
    lane = lax.broadcasted_iota(jnp.int32, (count * tokens, LANES), 1)
    is_router = (lane >= shared_cols) & (lane < shared_cols + expert_count)
    first = first_w[...]

    def joined(own, other):
        return jnp.concatenate([v[i] for i in range(count) for v in (own, other)], axis=0)

    rows, rows_dy = joined(hn_own, hn_other), joined(dy_own, dy_other)
    meta = joined(meta_own, meta_other)
    products = dot_nt(rows, first)
    gate, up = products[:, :LANES], products[:, LANES:]
    sig = jax.nn.sigmoid(gate)
    total = jnp.sum(jnp.where(is_router, sig * meta, 0.0), axis=1, keepdims=True)
    mine = jnp.sum(jnp.where(lane == shared_cols + me, sig, 0.0), axis=1, keepdims=True)
    token_gate = two_lanes(ROUTE_SCALE * mine / total, lane)
    sact = (gate * sig * up).astype(bf16)
    d_sact = dot_nt(rows_dy, sdown_w[...])
    d_sgate = d_sact * up * sig * (1.0 + gate * (1.0 - sig))
    dsh = jnp.concatenate([d_sgate, d_sact * gate * sig], axis=1).astype(bf16)
    pick = (meta[:, :1] == lane.astype(f32)).astype(bf16)
    groups = [slice(i * tokens, (i + 1) * tokens) for i in range(count)]
    for i in range(count):
        start = i * tokens
        sact_own_out[i] = sact[start : start + half]
        sact_other_out[i] = sact[start + half : start + tokens]
    slots = [dot_tn(pick[g], rows[g]).astype(bf16) for g in groups]
    slot_dys = [dot_tn(pick[g], rows_dy[g]).astype(bf16) for g in groups]
    slot_gates = [
        jnp.sum(dot_tn(pick[g], token_gate[g]), axis=1, keepdims=True) for g in groups
    ]

    @pl.when(pl.program_id(0) == 0)
    def _():
        shared_grads_out[...] = jnp.zeros_like(shared_grads_out)

    first_grad, sdown_grad = dot_tn(dsh, rows), dot_tn(sact, rows_dy)
    shared_grads_out[:shared_cols] += first_grad[:shared_cols]
    shared_grads_out[shared_cols : 2 * shared_cols] += first_grad[LANES : LANES + shared_cols]
    shared_grads_out[2 * shared_cols :] += sdown_grad[:shared_cols]
    slot_rows = jnp.concatenate(slots, axis=0)
    slot_dy = jnp.concatenate(slot_dys, axis=0)
    slot_gate = jnp.concatenate(slot_gates, axis=0)
    slots_out[...] = slot_rows
    slot_dy_out[...] = slot_dy
    gate = dot_nt(slot_rows, gate_up_w[0])
    up = dot_nt(slot_rows, gate_up_w[1])
    d_act = dot_nt(slot_dy, down_w[...])
    sig = jax.nn.sigmoid(gate)
    silu = gate * sig
    act = silu * up
    slot_dgate = jnp.sum(act * d_act, axis=1, keepdims=True)
    act_out[...] = (slot_gate * act).astype(bf16)
    d_act = slot_gate * d_act
    d_gate = (d_act * up * sig * (1.0 + gate * (1.0 - sig))).astype(bf16)
    d_up = (d_act * silu).astype(bf16)
    d_gate_up_out[0] = d_gate
    d_gate_up_out[1] = d_up
    d_slots = (dot_nn(d_gate, gate_up_w[0]) + dot_nn(d_up, gate_up_w[1])).astype(bf16)
    slot_lane = lax.broadcasted_iota(jnp.int32, (LANES, LANES), 1)
    d_shared = dot_nn(dsh, first)
    for i, g in enumerate(groups):
        here = slice(i * LANES, (i + 1) * LANES)
        d_rows = (dot_nn(pick[g], d_slots[here]) + d_shared[g]).astype(bf16)
        rows_own_out[i], rows_other_out[i] = d_rows[:half], d_rows[half:]
        dgate = dot_nn(pick[g], two_lanes(slot_dgate[here], slot_lane))
        dgate_own_out[i], dgate_other_out[i] = dgate[:half], dgate[half:]


def block_specs(per_step):
    def lead(*tail):
        return pl.BlockSpec((per_step, *tail), lambda i: (i,) + (0,) * len(tail))

    def flat(cols):
        return pl.BlockSpec((per_step * LANES, cols), lambda i: (i, 0))

    def whole(a):
        return pl.BlockSpec(a.shape, lambda i: (0,) * a.ndim, pipeline_mode=pl.Buffered(1))

    return lead, flat, whole


def experts(
    me,
    hn_own,
    hn_other,
    dy_own,
    dy_other,
    meta_own,
    meta_other,
    gate_up_w,
    down_w,
    first_w,
    sdown_w,
    shared_cols,
    expert_count,
    per_step=2,
):
    groups, half, width = hn_own.shape
    hidden = down_w.shape[0]
    slots = groups * LANES
    f32, bf16 = jnp.float32, jnp.bfloat16
    lead, flat, whole = block_specs(per_step)
    sds = jax.ShapeDtypeStruct
    return pl.pallas_call(
        functools.partial(expert_kernel, shared_cols, expert_count),
        grid=(groups // per_step,),
        in_specs=[
            pl.BlockSpec(memory_space=pltpu.SMEM),
            *[lead(half, width)] * 4,
            *[lead(half, LANES)] * 2,
            *[whole(a) for a in (gate_up_w, down_w, first_w, sdown_w)],
        ],
        out_specs=[
            flat(width),
            flat(width),
            flat(hidden),
            pl.BlockSpec((2, per_step * LANES, hidden), lambda i: (0, i, 0)),
            *[lead(half, width)] * 2,
            *[lead(half, LANES)] * 2,
            pl.BlockSpec((3 * shared_cols, width), lambda i: (0, 0)),
            *[lead(half, LANES)] * 2,
        ],
        out_shape=[
            sds((slots, width), bf16),
            sds((slots, width), bf16),
            sds((slots, hidden), bf16),
            sds((2, slots, hidden), bf16),
            *[sds((groups, half, width), bf16)] * 2,
            *[sds((groups, half, LANES), bf16)] * 2,
            sds((3 * shared_cols, width), f32),
            *[sds((groups, half, LANES), f32)] * 2,
        ],
        compiler_params=pltpu.CompilerParams(vmem_limit_bytes=58 * 1024 * 1024),
        cost_estimate=pl.CostEstimate(
            flops=groups * width, bytes_accessed=groups * width, transcendentals=0
        ),
    )(
        me,
        hn_own,
        hn_other,
        dy_own,
        dy_other,
        meta_own,
        meta_other,
        gate_up_w,
        down_w,
        first_w,
        sdown_w,
    )


def swap_halves(value, lane):
    low = lane % DR < DR // 2
    return jnp.where(low, pltpu.roll(value, LANES - DR // 2, 1), pltpu.roll(value, DR // 2, 1))


def by_core(core, first, second):
    return jnp.where(core == 0, first, second), jnp.where(core == 0, second, first)


def head_scores(q, kv, k_rope, visible, lane, head, heads):
    q_nope = q[:, head * DN : (head + 1) * DN]
    q_rope = jnp.where(lane // DR == head, q[:, heads * DN :], jnp.zeros((), q.dtype))
    at = head * (DN + DV)
    k_nope, value = kv[:, at : at + DN], kv[:, at + DN : at + DN + DV]
    scores = (dot_nt(q_nope, k_nope) + dot_nt(q_rope, k_rope)) * (DN + DR) ** -0.5
    return jnp.where(visible, scores, NEGATIVE), q_nope, q_rope, k_nope, value


def seen(doc_col, doc_row):
    rows = doc_col.shape[0]
    later = lax.broadcasted_iota(jnp.int32, (rows, rows), 0) >= lax.broadcasted_iota(
        jnp.int32, (rows, rows), 1
    )
    return (doc_col == doc_row) & later


def attention_kernel(
    heads,
    rank,
    core_ref,
    x_own,
    x_other,
    gain,
    latent_gain,
    head_w,
    small_w,
    kv_w,
    cosine,
    sine,
    doc_col,
    doc_row,
    normed_out,
    compressed_out,
    q_out,
    kv_out,
    k_rope_out,
    sums_out,
    attended_out,
    latent_out,
    part_own_out,
    part_other_out,
):
    f32, bf16 = jnp.float32, jnp.bfloat16
    core = core_ref[0]
    x = jnp.concatenate(by_core(core, x_own[0], x_other[0]), axis=0).astype(f32)
    rows = x.shape[0]
    half = rows // 2
    lane = lax.broadcasted_iota(jnp.int32, (rows, LANES), 1)
    inverse = lax.rsqrt(jnp.mean(x * x, axis=1, keepdims=True) + EPSILON)
    normed = (x * inverse * gain[...]).astype(bf16)
    normed_out[0] = normed
    q_cols = heads * (DN + DR)
    queries = dot_nn(normed, head_w[:, :q_cols])
    q_rope = queries[:, heads * DN :]
    q_rope = q_rope * cosine[0] + swap_halves(q_rope, lane) * sine[0]
    q = jnp.concatenate([queries[:, : heads * DN], q_rope], axis=1).astype(bf16)
    q_out[0] = q
    latent = dot_nn(normed, small_w[:, : rank + LANES])
    latent_out[0] = latent
    squeezed = latent[:, :rank]
    inverse = lax.rsqrt(jnp.mean(squeezed * squeezed, axis=1, keepdims=True) + EPSILON)
    compressed = (squeezed * inverse * latent_gain[...]).astype(bf16)
    compressed_out[0] = compressed
    k_rope = latent[:, rank:]
    k_rope = (k_rope * cosine[0] + swap_halves(k_rope, lane) * sine[0]).astype(bf16)
    k_rope_out[0] = k_rope
    kv = dot_nn(compressed, kv_w[...]).astype(bf16)
    kv_out[0] = kv
    visible = seen(doc_col[0], doc_row[0])
    attended, sums = [], jnp.zeros((rows, LANES), f32)
    for head in range(heads):
        scores, *_, value = head_scores(q, kv, k_rope, visible, lane, head, heads)
        top = jnp.max(scores, axis=1, keepdims=True)
        log_total = top + jnp.log(jnp.sum(jnp.exp(scores - top), axis=1, keepdims=True))
        sums = jnp.where(lane == head, log_total, sums)
        probs = jnp.exp(scores - log_total).astype(bf16)
        attended.append(dot_nn(probs, value).astype(bf16))
    sums_out[0] = sums
    attended = jnp.concatenate(attended, axis=1)
    attended_out[0] = attended
    part = dot_nt(attended, head_w[:, q_cols : q_cols + heads * DV]).astype(bf16)
    part_own_out[0], part_other_out[0] = by_core(core, part[:half], part[half:])


def attention_backward_kernel(
    heads,
    core_ref,
    d_own,
    d_other,
    normed_ref,
    compressed_ref,
    q_ref,
    kv_ref,
    k_rope_ref,
    sums_ref,
    attended_ref,
    head_w,
    kv_w,
    cosine,
    sine,
    doc_col,
    doc_row,
    head_grad_out,
    kv_grad_out,
    normed_own_out,
    normed_other_out,
    latent_own_out,
    latent_other_out,
    head_acc,
    kv_acc,
):
    f32, bf16 = jnp.float32, jnp.bfloat16
    core, step = core_ref[0], pl.program_id(0)
    scale = (DN + DR) ** -0.5
    d_rows = jnp.concatenate(by_core(core, d_own[0], d_other[0]), axis=0)
    rows = d_rows.shape[0]
    half = rows // 2
    lane = lax.broadcasted_iota(jnp.int32, (rows, LANES), 1)
    q_cols = heads * (DN + DR)
    q, kv, k_rope = q_ref[0], kv_ref[0], k_rope_ref[0]
    d_attended = dot_nn(d_rows, head_w[:, q_cols : q_cols + heads * DV]).astype(bf16)
    visible = seen(doc_col[0], doc_row[0])
    d_q, d_kv = [], []
    d_q_rope, d_k_rope = jnp.zeros((rows, LANES), f32), jnp.zeros((rows, LANES), f32)
    for head in range(heads):
        scores, q_nope, q_rope, k_nope, value = head_scores(
            q, kv, k_rope, visible, lane, head, heads
        )
        probs = jnp.exp(scores - sums_ref[0][:, head : head + 1])
        d_head = d_attended[:, head * DV : (head + 1) * DV]
        d_probs = dot_nt(d_head, value)
        d_value = dot_tn(probs.astype(bf16), d_head)
        delta = jnp.sum(probs * d_probs, axis=1, keepdims=True)
        d_scores = (probs * (d_probs - delta)).astype(bf16)
        d_q.append(dot_nn(d_scores, k_nope) * scale)
        d_q_rope = jnp.where(lane // DR == head, dot_nn(d_scores, k_rope) * scale, d_q_rope)
        d_kv += [dot_tn(d_scores, q_nope) * scale, d_value]
        d_k_rope += dot_tn(d_scores, q_rope) * scale
    d_q_rope = d_q_rope * cosine[0] - swap_halves(d_q_rope, lane) * sine[0]
    d_q = jnp.concatenate(d_q + [d_q_rope], axis=1).astype(bf16)
    d_kv = jnp.concatenate(d_kv, axis=1).astype(bf16)

    @pl.when(step == 0)
    def _():
        head_acc[...] = jnp.zeros_like(head_acc)
        kv_acc[...] = jnp.zeros_like(kv_acc)

    head_acc[:, :q_cols] += dot_tn(normed_ref[0], d_q)
    head_acc[:, q_cols:] += dot_tn(d_rows, attended_ref[0])
    kv_acc[...] += dot_tn(compressed_ref[0], d_kv)

    @pl.when(step == pl.num_programs(0) - 1)
    def _():
        head_grad_out[...] = head_acc[...].astype(bf16)
        kv_grad_out[...] = kv_acc[...].astype(bf16)

    part = dot_nt(d_q, head_w[:, :q_cols]).astype(bf16)
    normed_own_out[0], normed_other_out[0] = by_core(core, part[:half], part[half:])
    latent = jnp.concatenate([dot_nt(d_kv, kv_w[...]), d_k_rope], axis=1).astype(bf16)
    latent_own_out[0], latent_other_out[0] = by_core(core, latent[:half], latent[half:])


def one_each(*tail):
    return pl.BlockSpec((1, *tail), lambda i: (i,) + (0,) * len(tail))


def kept(value):
    return pl.BlockSpec(value.shape, lambda i: (0,) * value.ndim, pipeline_mode=pl.Buffered(1))


def attention(core, x_own, x_other, gain, latent_gain, head_w, small_w, kv_w, cosine, sine, doc):
    near, half, width = x_own.shape
    rows = 2 * half
    rank, kv_cols = kv_w.shape
    heads = kv_cols // (DN + DV)
    f32, bf16 = jnp.float32, jnp.bfloat16
    shapes = [
        ((rows, width), bf16),
        ((rows, rank), bf16),
        ((rows, heads * (DN + DR)), bf16),
        ((rows, kv_cols), bf16),
        ((rows, LANES), bf16),
        ((rows, LANES), f32),
        ((rows, heads * DV), bf16),
        ((rows, rank + LANES), f32),
        ((half, width), bf16),
        ((half, width), bf16),
    ]
    return pl.pallas_call(
        functools.partial(attention_kernel, heads, rank),
        grid=(near,),
        in_specs=[
            pl.BlockSpec(memory_space=pltpu.SMEM),
            *[one_each(half, width)] * 2,
            *[kept(a) for a in (gain, latent_gain, head_w, small_w, kv_w)],
            *[one_each(rows, LANES)] * 2,
            one_each(rows, 1),
            one_each(1, rows),
        ],
        out_specs=[one_each(*shape) for shape, _ in shapes],
        out_shape=[jax.ShapeDtypeStruct((near, *shape), kind) for shape, kind in shapes],
        compiler_params=pltpu.CompilerParams(vmem_limit_bytes=58 * 1024 * 1024),
        cost_estimate=pl.CostEstimate(
            flops=2 * near * rows * width * (rank + 3 * heads * DN),
            bytes_accessed=4 * near * rows * width,
            transcendentals=0,
        ),
    )(
        core,
        x_own,
        x_other,
        gain,
        latent_gain,
        head_w,
        small_w,
        kv_w,
        cosine,
        sine,
        doc[:, :, None],
        doc[:, None, :],
    )


def attention_backward(core, d_own, d_other, kept_rows, head_w, kv_w, cosine, sine, doc):
    near, half, width = d_own.shape
    rows = 2 * half
    rank, kv_cols = kv_w.shape
    heads = kv_cols // (DN + DV)
    head_cols = heads * (DN + DR + DV)
    f32, bf16 = jnp.float32, jnp.bfloat16
    sds = jax.ShapeDtypeStruct
    return pl.pallas_call(
        functools.partial(attention_backward_kernel, heads),
        grid=(near,),
        in_specs=[
            pl.BlockSpec(memory_space=pltpu.SMEM),
            *[one_each(half, width)] * 2,
            *[one_each(*v.shape[1:]) for v in kept_rows],
            *[kept(a) for a in (head_w, kv_w)],
            *[one_each(rows, LANES)] * 2,
            one_each(rows, 1),
            one_each(1, rows),
        ],
        out_specs=[
            pl.BlockSpec((width, head_cols), lambda i: (0, 0)),
            pl.BlockSpec((rank, kv_cols), lambda i: (0, 0)),
            *[one_each(half, width)] * 2,
            *[one_each(half, rank + LANES)] * 2,
        ],
        out_shape=[
            sds((width, head_cols), bf16),
            sds((rank, kv_cols), bf16),
            *[sds((near, half, width), bf16)] * 2,
            *[sds((near, half, rank + LANES), bf16)] * 2,
        ],
        scratch_shapes=[
            pltpu.VMEM((width, head_cols), f32),
            pltpu.VMEM((rank, kv_cols), f32),
        ],
        compiler_params=pltpu.CompilerParams(vmem_limit_bytes=58 * 1024 * 1024),
        cost_estimate=pl.CostEstimate(
            flops=near * rows * width * heads * DN,
            bytes_accessed=2 * near * rows * width,
            transcendentals=0,
        ),
    )(
        core,
        d_own,
        d_other,
        *kept_rows,
        head_w,
        kv_w,
        cosine,
        sine,
        doc[:, :, None],
        doc[:, None, :],
    )


def product_kernel(*refs):
    *operands, out_ref = refs
    count = len(operands) // 2
    total = 0.0
    for left_ref, right_ref in zip(operands[:count], operands[count:]):
        total += dot_tn(left_ref[0], right_ref[...])
    out_ref[0] = total


def column_products(lefts, rights, tile=512):
    count, _, height = lefts[0].shape
    width = rights[0].shape[1]
    return pl.pallas_call(
        product_kernel,
        grid=(width // tile, count),
        in_specs=[
            *[pl.BlockSpec((1, v.shape[1], height), lambda j, i: (i, 0, 0)) for v in lefts],
            *[pl.BlockSpec((v.shape[0], tile), lambda j, i: (0, j)) for v in rights],
        ],
        out_specs=pl.BlockSpec((1, height, tile), lambda j, i: (i, 0, j)),
        out_shape=jax.ShapeDtypeStruct((count, height, width), jnp.float32),
        compiler_params=pltpu.CompilerParams(vmem_limit_bytes=58 * 1024 * 1024),
        cost_estimate=pl.CostEstimate(flops=width, bytes_accessed=width, transcendentals=0),
    )(*lefts, *rights)


def output_kernel(act, sact_own, sact_other, meta_own, meta_other, down_w, sdown_w, own_out, other_out):
    f32, bf16 = jnp.float32, jnp.bfloat16
    count, half, _ = meta_own.shape
    lane = lax.broadcasted_iota(jnp.int32, (2 * half, LANES), 1).astype(f32)
    out = dot_nn(act[...], down_w[...]).astype(bf16)
    for i in range(count):
        meta = jnp.concatenate([meta_own[i], meta_other[i]], axis=0)
        pick = (meta[:, :1] == lane).astype(bf16)
        sact = jnp.concatenate([sact_own[i], sact_other[i]], axis=0)
        here = slice(i * LANES, (i + 1) * LANES)
        rows = (dot_nn(pick, out[here]) + dot_nn(sact, sdown_w[...])).astype(bf16)
        own_out[i], other_out[i] = rows[:half], rows[half:]


def outputs(act, sact_own, sact_other, meta_own, meta_other, down_w, sdown_w, per_step=4):
    groups, half, _ = meta_own.shape
    hidden, width = down_w.shape
    lead, flat, whole = block_specs(per_step)
    return pl.pallas_call(
        output_kernel,
        grid=(groups // per_step,),
        in_specs=[
            flat(hidden),
            *[lead(half, LANES)] * 4,
            *[whole(a) for a in (down_w, sdown_w)],
        ],
        out_specs=[lead(half, width)] * 2,
        out_shape=[jax.ShapeDtypeStruct((groups, half, width), jnp.bfloat16)] * 2,
        compiler_params=pltpu.CompilerParams(vmem_limit_bytes=58 * 1024 * 1024),
        cost_estimate=pl.CostEstimate(
            flops=groups * half * LANES * width,
            bytes_accessed=groups * half * width,
            transcendentals=0,
        ),
    )(act, sact_own, sact_other, meta_own, meta_other, down_w, sdown_w)


def token_plan(
    inputs,
    attn_gain,
    w_query,
    w_latent,
    latent_gain,
    w_kv,
    w_out,
    ffn_gain,
    w_router,
    shared_gate_up,
    shared_down,
    expert_gate_up,
    expert_down,
    lengths,
    routes,
    cotangent,
):
    f32, bf16 = jnp.float32, jnp.bfloat16
    core, me = lax.axis_index("tensor"), lax.axis_index("expert")
    groups = lax.axis_size("expert")
    deep, place, z = groups // PLANE, me % PLANE, me // PLANE
    tok_rows, width = inputs.shape
    half = tok_rows // 2
    own_at, other_at = core * half, (1 - core) * half
    expert_count = w_router.shape[1]
    route_count = routes.shape[1]
    capacity = tok_rows * route_count * 4 // (3 * expert_count)
    shared_cols = shared_gate_up.shape[2] // groups
    latent_cols, rank_width = w_latent.shape[1], latent_gain.shape[0] * groups
    block_rows = w_query.shape[0]
    kv_rows = w_kv.shape[0]

    query_cols = w_query.shape[1] // PLANE
    out_cols = w_out.shape[0] // PLANE
    small = jnp.concatenate(
        [
            w_latent,
            w_latent[:, rank_width:],
            w_router,
            attn_gain[:, None],
            ffn_gain[:, None],
            jnp.pad(latent_gain, (0, block_rows - kv_rows))[:, None],
        ],
        axis=1,
    )
    small_cols = small.shape[1]
    route_half = take_rows(routes, own_at, half).astype(bf16).reshape(block_rows // 2, -1)
    length_col = jnp.pad(lengths[0].astype(bf16), (0, block_rows // 2 - lengths.shape[1]))[:, None]
    route_cols = route_half.shape[1] + 1
    small_half = jnp.concatenate(
        [
            take_rows(small, core * (block_rows // 2), block_rows // 2),
            route_half,
            length_col,
            jnp.zeros((block_rows // 2, -(small_cols + route_cols) % (2 * LANES)), bf16),
        ],
        axis=1,
    )
    packed_cols = small_half.shape[1] // 2
    small_packed = jnp.concatenate([small_half[:, :packed_cols], small_half[:, packed_cols:]])
    kv_cols = w_kv.shape[1] // PLANE
    kv_parts = block_rows // kv_rows
    kv_piece = kv_cols // kv_parts
    w_out_t = w_out.T

    local_heads = query_cols // (DN + DR)

    def by_parts(block):
        heads = [block[:, h * (DN + DR) : (h + 1) * (DN + DR)] for h in range(local_heads)]
        return [h[:, :DN] for h in heads] + [h[:, DN:] for h in heads]

    def quarter(index):
        kv_here = take_rows(w_kv, index * kv_cols, kv_cols, axis=1)
        kv_here = [kv_here[:, p * kv_piece : (p + 1) * kv_piece] for p in range(kv_parts)]
        return jnp.concatenate(
            [
                *by_parts(take_rows(w_query, index * query_cols, query_cols, axis=1)),
                take_rows(w_out_t, index * out_cols, out_cols, axis=1),
                jnp.concatenate(kv_here, axis=0),
            ],
            axis=1,
        )

    near_w = [quarter(place)] + [to_partner(quarter(place ^ r), r) for r in range(1, PLANE)]
    small_line = deep_join(small_packed, deep_pieces(small_packed), z)
    near_w, small_line = tie(near_w, small_line)
    plane_w = jnp.stack(by_place(near_w, place))
    small_sent, x_sent, plane_w = tie(
        small_line.swapaxes(0, 1), take_rows(inputs, own_at, half), plane_w
    )
    small_sent = jnp.stack([small_sent, to_partner(small_sent, 1)])
    small_sent = jnp.concatenate([small_sent, to_partner(small_sent, 2)], axis=0)
    x_sent = jnp.stack([x_sent, to_partner(x_sent, 2)])
    x_came = to_partner(x_sent, 1)
    x_near_own = jnp.stack([x_sent[0], x_came[0], x_sent[1], x_came[1]])
    x_near_other = swap_cores(x_near_own)
    deep_w = deep_hops(plane_w)
    small_parts = [small_sent[r].swapaxes(0, 1) for r in range(PLANE)]
    small_own = jnp.stack(by_place(small_parts, place), axis=1)
    small_own = small_own.reshape(groups, block_rows, packed_cols)
    small_own = jnp.concatenate(
        [small_own[:, : block_rows // 2], small_own[:, block_rows // 2 :]], axis=2
    )
    small_other = swap_cores(small_own)
    small_all = in_order(core, small_own, small_other, axis=1)
    small_all, x_near_other, deep_w = tie(small_all, x_near_other, deep_w)
    head_w = deep_join(plane_w, join_hops(deep_w), z)
    length_at = small_cols + route_cols - 1
    lengths_near = take_rows(small_own, z * PLANE, PLANE)[:, : lengths.shape[1], length_at]
    lengths_near = lengths_near.astype(jnp.int32)
    lengths_near = jnp.stack(by_place([lengths_near[r] for r in range(PLANE)], place))
    shared_rows = jnp.concatenate(
        [shared_gate_up[0].T, shared_gate_up[1].T, shared_down], axis=0
    ).reshape(3, groups, shared_cols, block_rows)
    shared_rows = shared_rows.swapaxes(0, 1).reshape(groups, 3 * shared_cols, block_rows)
    dy_sent, head_w = tie(take_rows(cotangent, own_at, half), head_w)
    dy_own_rows = take_rows(cotangent, own_at, half)
    dy_gather = RowGather(dy_sent)
    dy_came = dy_gather.along()
    head_w = head_w.reshape(groups, block_rows, -1)
    flat_head = head_w.reshape(groups * block_rows, -1)
    at = query_cols + out_cols
    kv_w = head_w[:, :, at : at + kv_piece].reshape(groups, kv_parts, kv_rows, kv_piece)
    kv_w = kv_w.transpose(0, 2, 1, 3).reshape(groups * kv_rows, kv_cols)

    block_index = jnp.arange(groups)
    block_chip = (z - block_index % deep) % deep * PLANE + (place ^ (block_index // deep))
    in_blocks = (block_chip[:, None] == block_index[None, :]).astype(bf16)

    def routes_of(came):
        came = came[:, :, small_cols : small_cols + route_half.shape[1]].reshape(groups, -1)
        came = jnp.dot(in_blocks, came, preferred_element_type=f32)
        return came.astype(jnp.int32).reshape(groups, half, route_count)

    routes_own, routes_other = routes_of(small_own), routes_of(small_other)
    flat_small = small_all.reshape(groups * block_rows, -1)
    latent_w = flat_small[:, :latent_cols]
    at = rank_width + LANES
    router_w = flat_small[:, at : at + expert_count]
    at += expert_count
    gain_one, gain_two = flat_small[:, at], flat_small[:, at + 1]
    latent_g = small_all[:, :kv_rows, at + 2].reshape(-1)

    near_rows = PLANE * tok_rows
    relative, doc = jax.vmap(lambda one: doc_places(one, tok_rows))(lengths_near)
    cosine, sine_tab = rope_tables(relative.reshape(-1), DR)
    cosine, sine_tab = [v.reshape(PLANE, tok_rows, -1) for v in (cosine, sine_tab)]
    rope = (
        jnp.concatenate([cosine] * 4, axis=-1),
        jnp.concatenate([-sine_tab, sine_tab] * 2, axis=-1),
        doc.astype(f32),
    )
    core_index = core.reshape(1).astype(jnp.int32)
    *kept_rows, latent, part_own, part_other = attention(
        core_index,
        x_near_own,
        x_near_other,
        gain_one.astype(f32)[None],
        latent_g.astype(f32)[None],
        flat_head,
        flat_small,
        kv_w,
        *rope,
    )
    normed_b = kept_rows[0].reshape(near_rows, width)

    def sum_cores(own, other):
        return add_wide(own, swap_cores(other)).astype(bf16)

    def sum_plane(both):
        return plane_scatter([both[r] for r in range(PLANE)])

    part_own, part_other, dy_came = tie(part_own, part_other, dy_came)
    attn_own = sum_plane(sum_cores(part_own, part_other))
    x_own = take_rows(inputs, own_at, half).astype(f32)
    hidden = x_own + attn_own
    hnormed, scale_two = rms_forward(hidden, gain_two.astype(f32))
    hnormed_b = hnormed.astype(bf16)
    normed_cols = jnp.concatenate(
        [
            take_rows(normed_b, (k * PLANE + place) * block_rows, block_rows, axis=1)
            for k in range(deep)
        ],
        axis=1,
    )
    hnormed_b, normed_cols, shared_rows, routes_own, routes_other = tie(
        hnormed_b, normed_cols, shared_rows, routes_own, routes_other
    )
    dy_line = jnp.stack(dy_came)
    def membership(named):
        one_hot = named[..., None] == jnp.arange(expert_count, dtype=jnp.int32)
        return jnp.any(named == me, axis=-1), jnp.any(one_hot, axis=2)

    member_own, hot_own = membership(routes_own)
    member_other, hot_other = membership(routes_other)
    lower = (
        jnp.arange(half, dtype=jnp.int32)[:, None] <= jnp.arange(half, dtype=jnp.int32)[None, :]
    ).astype(bf16)

    def running(mask):
        counts = jnp.dot(mask.astype(bf16), lower, preferred_element_type=f32)
        return counts.astype(jnp.int32)

    count_own, count_other = running(member_own), running(member_other)
    place_own = jnp.where(member_own, count_own - 1, -1)
    place_other = jnp.where(member_other, count_own[:, -1:] + count_other - 1, -1)

    def metadata(slot, hot):
        return jnp.concatenate(
            [
                slot[..., None].astype(f32),
                jnp.zeros((groups, half, shared_cols - 1), f32),
                hot.astype(f32),
                jnp.zeros((groups, half, LANES - shared_cols - expert_count), f32),
            ],
            axis=-1,
        )

    meta_own, meta_other = metadata(place_own, hot_own), metadata(place_other, hot_other)
    hn_gather = RowGather(hnormed_b)
    shared_w = lax.all_to_all(shared_rows, "expert", split_axis=0, concat_axis=0, tiled=True)
    hn_came, dy_beside, dy_line_other, shared_w, meta_own, meta_other = tie(
        hn_gather.along(),
        dy_gather.beside(dy_line),
        swap_cores(dy_line),
        shared_w,
        meta_own,
        meta_other,
    )
    shared_w = shared_w.swapaxes(0, 1).reshape(3 * shared_cols, groups * block_rows)
    first_w = jnp.concatenate(
        [
            shared_w[:shared_cols],
            router_w.T,
            jnp.zeros((LANES - shared_cols - expert_count, width), bf16),
            shared_w[shared_cols : 2 * shared_cols],
            jnp.zeros((LANES - shared_cols, width), bf16),
        ],
        axis=0,
    )
    sdown_rows = jnp.pad(shared_w[2 * shared_cols :], ((0, LANES - shared_cols), (0, 0)))
    gate_up_w, down_w = jnp.swapaxes(expert_gate_up[0], 1, 2), expert_down[0]

    def run_experts(which, hn_part, hn_part_other):
        at, to = which[0] * deep, (which[-1] + 1) * deep
        return experts(
            me.reshape(1).astype(jnp.int32),
            hn_part,
            hn_part_other,
            *dy_parts[which],
            meta_own[at:to],
            meta_other[at:to],
            gate_up_w,
            down_w,
            first_w,
            sdown_rows,
            shared_cols,
            expert_count,
        )

    parts = ((0,), (1, 2), (3,))
    dy_parts = {parts[0]: (dy_line, dy_line_other)}
    hn_line, dy_beside = tie(jnp.stack(hn_came), dy_beside)
    dy_near = jnp.concatenate(dy_beside, axis=0)
    hn_beside, dy_far, done_line, *dy_parts[parts[1]] = tie(
        hn_gather.beside(hn_line),
        dy_gather.far(dy_beside),
        run_experts(parts[0], hn_line, swap_cores(hn_line)),
        dy_near,
        swap_cores(dy_near),
    )
    d_line_came = swap_cores(done_line[5])
    hn_near, dy_far = jnp.concatenate(hn_beside, axis=0), jnp.concatenate(dy_far, axis=1)
    hn_far, done_near, *dy_parts[parts[2]] = tie(
        hn_gather.far(hn_beside),
        run_experts(parts[1], hn_near, swap_cores(hn_near)),
        dy_far,
        swap_cores(dy_far),
    )
    d_near_came = swap_cores(done_near[5])
    hn_far = jnp.concatenate(hn_far, axis=1)
    done_far = run_experts(parts[2], hn_far, swap_cores(hn_far))
    done = (done_line, done_near, done_far)
    slot_rows, slot_dy, slot_act, d_gate_up = [[v[i] for v in done] for i in range(4)]
    shared_grads = add_wide(*[v[8] for v in done])

    def by_flips(line, near, far):
        return [line, near[:deep], near[deep:], far]

    d_rows_own = by_flips(*[v[4] for v in done])
    d_rows_came = by_flips(d_line_came, d_near_came, swap_cores(done_far[5]))

    def two_parts(value):
        return value[..., 0] + value[..., 1]

    dgate_own, dgate_other = [
        jnp.concatenate([two_parts(v[i]) for v in done], axis=0) for i in (9, 10)
    ]
    dgate_sent = dgate_own + swap_cores(dgate_other)
    dgate_high = dgate_sent.astype(bf16)
    dgate_low = (dgate_sent - dgate_high.astype(f32)).astype(bf16)
    d_rows_came, dgate_high, dgate_low = tie(d_rows_came, dgate_high, dgate_low)
    d_sum = RowSum(d_rows_own, d_rows_came)
    sends, shared_grads, slot_act = tie(d_sum.sends(), shared_grads, slot_act)
    came = d_sum.move(sends)
    gate_rows = jnp.stack([contract_rows(in_blocks, v).reshape(-1) for v in (dgate_high, dgate_low)])
    grads_sent = jnp.concatenate([shared_grads, gate_rows], axis=0).astype(bf16)
    grads_sent = grads_sent.reshape(-1, groups, block_rows)
    grads_came = lax.all_to_all(grads_sent, "expert", split_axis=1, concat_axis=1, tiled=True)
    out_done = [
        outputs(
            act,
            v[6],
            v[7],
            meta_own[p[0] * deep : (p[-1] + 1) * deep],
            meta_other[p[0] * deep : (p[-1] + 1) * deep],
            down_w,
            sdown_rows,
        )
        for act, v, p in zip(slot_act, done, parts)
    ]
    edown_grad = column_products([v[None] for v in slot_act], slot_dy)[0]
    came, out_done, edown_grad, grads_came = tie(came, out_done, edown_grad, grads_came)
    dgate = add_wide(grads_came[3 * shared_cols], grads_came[3 * shared_cols + 1]).T
    sends, slot_rows, out_done = tie(d_sum.sends_again(came), slot_rows, out_done)
    came_again = d_sum.move_again(sends)
    egu_grad = column_products(d_gate_up, slot_rows).swapaxes(1, 2)
    out_own = by_flips(*[v[0] for v in out_done])
    out_came = by_flips(*[swap_cores(v[1]) for v in out_done])
    out_sum = RowSum(out_own, out_came)
    out_sends = out_sum.sends()
    came_again, egu_grad, out_sends = tie(came_again, egu_grad, out_sends)
    z_sends, out_sends, dgate = tie(
        line_sends(d_sum.line(came, came_again)), out_sends, dgate
    )
    z_came = line_move(z_sends)
    out_first = out_sum.move(out_sends)
    hot_mine = take_rows(
        jnp.any(routes[..., None] == jnp.arange(expert_count, dtype=jnp.int32), axis=1), own_at, half
    )
    sig = jax.nn.sigmoid(jnp.dot(hnormed_b, router_w, preferred_element_type=f32))
    chosen = jnp.where(hot_mine, sig, 0.0)
    chosen_sum = jnp.sum(chosen, axis=1, keepdims=True)
    dgate = jnp.where(hot_mine, dgate, 0.0)
    inner = jnp.sum(dgate * chosen, axis=1, keepdims=True)
    d_chosen = ROUTE_SCALE * (dgate / chosen_sum - inner / (chosen_sum * chosen_sum))
    d_logits = (jnp.where(hot_mine, d_chosen, 0.0) * sig * (1.0 - sig)).astype(bf16)
    router_grad = contract_rows(d_logits, hnormed_b)
    z_came, d_logits, router_grad = tie(z_came, d_logits, router_grad)
    d_hn = add_wide(*z_came)
    d_hn = d_hn + contract_cols(d_logits, router_w)
    d_hidden_norm, gain_two_grad = rms_backward(hidden, scale_two, gain_two.astype(f32), d_hn)
    d_hidden = dy_own_rows.astype(f32) + d_hidden_norm
    d_parts, out_first = tie(plane_gather(d_hidden.astype(bf16)), out_first)
    d_near_own = jnp.stack(d_parts)
    d_near_other = swap_cores(d_near_own)
    out_sends, d_near_other = tie(out_sum.sends_again(out_first), d_near_other)
    out_second = out_sum.move_again(out_sends)

    (
        head_grad,
        kv_grad,
        normed_part_own,
        normed_part_other,
        latent_part_own,
        latent_part_other,
    ) = attention_backward(
        core_index, d_near_own, d_near_other, kept_rows, flat_head, kv_w, *rope
    )
    kv_grad = kv_grad.reshape(groups, kv_rows, kv_parts, kv_piece).transpose(0, 2, 1, 3)
    head_grad = jnp.concatenate([head_grad, kv_grad.reshape(-1, kv_piece)], axis=1)
    head_blocks = head_grad.reshape(deep, -1, head_grad.shape[1])
    head_hops = HopSum(lambda t: at_index(head_blocks, 0, t))
    came, latent_both, normed_both, out_second = tie(
        head_hops.hop(1),
        sum_cores(latent_part_own, latent_part_other),
        sum_cores(normed_part_own, normed_part_other),
        out_second,
    )
    out_line = out_sum.line(out_first, out_second)
    came, grad_both, out_line = tie(head_hops.hop(2, came), sum_plane(latent_both), out_line)
    grad_rope = grad_both[:, rank_width : rank_width + DR] + grad_both[:, rank_width + DR :]
    latent_own = take_rows(latent[0], own_at, half)
    cosine_own = take_rows(cosine[0], own_at, half)
    sine_own = take_rows(sine_tab[0], own_at, half)
    _, scale_kv = rms_forward(latent_own[:, :rank_width], latent_g.astype(f32))
    grad_c, latent_gain_grad = rms_backward(
        latent_own[:, :rank_width], scale_kv, latent_g.astype(f32), grad_both[:, :rank_width]
    )
    grad_latent = jnp.concatenate(
        [grad_c, unrotate(grad_rope, cosine_own, sine_own)], axis=-1
    ).astype(bf16)
    out_hops = HopSum(lambda t: at_index(out_line, 0, (z - t) % deep))
    came, latent_parts, grad_normed, out_z = tie(
        head_hops.hop(3, came), plane_gather(grad_latent), sum_plane(normed_both), out_hops.hop(1)
    )
    latent_near_own = jnp.stack(latent_parts)
    latent_near = in_order(core, latent_near_own, swap_cores(latent_near_own), axis=1)
    head_sums = head_hops.total(came).astype(bf16).reshape(PLANE, block_rows, -1)
    out_z, latent_near, head_shared, grads_came = tie(
        out_hops.hop(2, out_z), latent_near, share_columns(head_sums, place), grads_came
    )
    out_z = out_hops.hop(3, out_z)
    latent_cut = latent_cols // 2
    latent_near = latent_near.reshape(near_rows, latent_cols)
    latent_blocks = contract_rows(
        normed_cols,
        take_rows(latent_near, core * latent_cut, latent_cut, axis=1),
    )
    latent_half = deep_scatter(latent_blocks.astype(bf16).reshape(deep, -1, latent_cut), z)
    w_latent_grad = in_order(core, latent_half, swap_cores(latent_half), axis=1)


    def by_heads(block):
        rotary = local_heads * DN
        return [
            part
            for h in range(local_heads)
            for part in (
                block[:, h * DN : (h + 1) * DN],
                block[:, rotary + h * DR : rotary + (h + 1) * DR],
            )
        ]

    at_kv = query_cols + out_cols
    w_query_grad = jnp.concatenate([v for p in head_shared for v in by_heads(p)], axis=1)
    w_query_grad = w_query_grad.astype(f32)
    w_kv_grad = jnp.concatenate(
        [
            p[q * kv_rows : (q + 1) * kv_rows, at_kv:]
            for p in head_shared
            for q in range(kv_parts)
        ],
        axis=1,
    ).astype(f32)
    w_out_grad = jnp.concatenate([p[:, query_cols:at_kv] for p in head_shared], axis=1)
    w_out_grad = w_out_grad.astype(f32).T
    sgu_out = grads_came[: 2 * shared_cols].astype(f32)
    sgu_out = sgu_out.reshape(2, shared_cols, groups, block_rows)
    sgu_out = sgu_out.transpose(0, 3, 2, 1).reshape(2, block_rows, -1)
    sdown_out = grads_came[2 * shared_cols : 3 * shared_cols].astype(f32).swapaxes(0, 1).reshape(-1, block_rows)
    grad_normed = grad_normed + contract_cols(grad_latent, latent_w)
    moe_own = out_hops.total(out_z)
    mixed_own = (hidden + moe_own).astype(bf16)
    mixed = in_order(core, mixed_own, swap_cores(mixed_own))

    _, scale_own = rms_forward(x_own, gain_one.astype(f32))
    grad_x_norm, gain_one_grad = rms_backward(x_own, scale_own, gain_one.astype(f32), grad_normed)
    input_own = d_hidden + grad_x_norm
    input_grad = in_order(core, input_own, swap_cores(input_own))

    gain_lanes = jnp.pad(
        latent_gain_grad.reshape(groups, kv_rows), ((0, 0), (0, block_rows - kv_rows))
    )
    vectors = jnp.concatenate(
        [
            router_grad,
            gain_one_grad[None],
            gain_two_grad[None],
            gain_lanes.reshape(1, -1),
        ],
        axis=0,
    ).reshape(-1, groups, block_rows)
    arrived = lax.all_to_all(vectors, "expert", split_axis=1, concat_axis=1, tiled=True)
    sums = jnp.sum(arrived, axis=1)
    sums = sums + swap_cores(sums)
    return (
        mixed,
        input_grad,
        sums[expert_count],
        w_query_grad,
        w_latent_grad,
        sums[expert_count + 2, :kv_rows],
        w_kv_grad,
        w_out_grad,
        sums[expert_count + 1],
        sums[:expert_count].T,
        sgu_out,
        sdown_out,
        egu_grad[None],
        edown_grad[None],
    )


def solution(mesh):
    groups = mesh.shape["expert"]
    plan = token_plan if groups <= 16 else weight_plan
    return jax.shard_map(
        plan,
        mesh=mesh,
        in_specs=(
            P("expert", None),
            P("expert"),
            P("expert", "tensor"),
            P("expert", None),
            P("expert"),
            P("expert", "tensor"),
            P("tensor", "expert"),
            P("expert"),
            P("expert", None),
            P(None, "expert", "tensor"),
            P("tensor", "expert"),
            P("expert", None, None, "tensor"),
            P("expert", "tensor", None),
            P("expert", None),
            P("expert", None),
            P("expert", None),
        ),
        out_specs=(
            P("expert", None),
            P("expert", None),
            P("expert"),
            P("expert", "tensor"),
            P("expert", None),
            P("expert"),
            P("expert", "tensor"),
            P("tensor", "expert"),
            P("expert"),
            P("expert", None),
            P(None, "expert", "tensor"),
            P("tensor", "expert"),
            P("expert", None, None, "tensor"),
            P("expert", "tensor", None),
        ),
        check_vma=False,
    )
```

profile of v0, /device:TPU:1, one launch (start us, length us, event | category | flops | bytes accessed | tf_op | source)
XLA Modules:
  0.0 864.8 jit_solution(3643006148261286521)
XLA Ops:
  7.7 3.1 collective-permute-start.4
  21.5 3.7 collective-permute-done.2
  30.0 7.2 collective-permute-start.12
  41.9 8.7 %collective-permute-done.15 = bf16[4,128,768]{2,1,0:T(8,128)(2,1)} collective-permute-done((bf16[4,128,768]{2,1,0:T(8,128)(2,1)}, bf16[4,128,768]{2,1,0:T(8,128)(2,1)}, u32[]{:S(2)}, u32[]{:S(2)}) %collective-permute-start.15) | collective-permute-done | bytes 786464 | tf_op jit(solution)/shard_map/ppermute | solution.py:447
  52.0 5.6 collective-permute-start.13
  68.4 3.1 fusion.91
  72.8 6.8 collective-permute-start.14
  81.3 3.4 pad_maximum_fusion.19.cosine
  84.7 2.9 pad_maximum_fusion.20.sine
  90.2 4.6 collective-permute-done.17
  100.4 6.3 collective-permute-start.20
  113.3 18.4 %shard_map.263 = (bf16[4,256,2048]{2,1,0:T(8,128)(2,1)}, bf16[4,256,512]{2,1,0:T(8,128)(2,1)}, bf16[4,256,384]{2,1,0:T(8,128)(2,1)}, bf16[4,256,512]{2,1,0:T(8,1...) custom-call(s32[1]{0:T(128)} %bitcast.core_ref, ...), custom_call_target="tpu_custom_call" | custom-call | flops 5368709120 | bytes 8388608 | tf_op jit(solution)/shard_map/pallas_call | solution.py:1023
  131.7 18.8 %collective-permute-done.19 = bf16[128,2048]{1,0:T(8,128)(2,1)} collective-permute-done((bf16[128,2048]{1,0:T(8,128)(2,1)}, bf16[128,2048]{1,0:T(8,128)(2,1)}, u32[]{:S(2)}, u32[]{:S(2)}) %collective-permute-start.19) | collective-permute-done | bytes 524320 | tf_op jit(solution)/shard_map/ppermute | solution.py:418
  157.7 3.0 add_convert_fusion.1
  165.9 3.2 pad_maximum_fusion.1.dy_own
  171.2 3.3 collective-permute-done.22
  175.0 11.7 %collective-permute-done.24 = bf16[128,2048]{1,0:T(8,128)(2,1)S(1)} collective-permute-done((bf16[128,2048]{1,0:T(8,128)(2,1)S(1)}, bf16[128,2048]{1,0:T(8,128)(2,1)S(1)}, u32[]{:S(2)}, u32[]{:S(2)}) %collective-permute-start.24) | collective-permute-done | bytes 524320 | tf_op jit(solution)/shard_map/ppermute | solution.py:412
  188.3 5.0 all-to-all-start
  193.4 3.1 collective-permute-start.27
  204.4 3.8 maximum_maximum_fusion.1
  208.2 34.5 %collective-permute-done.29 = bf16[4,128,2048]{2,1,0:T(8,128)(2,1)} collective-permute-done((bf16[4,128,2048]{2,1,0:T(8,128)(2,1)}, bf16[4,128,2048]{2,1,0:T(8,128)(2,1)}, u32[]{:S(2)}, u32[]{:S(2)}) %collective-permute-start.29) | collective-permute-done | bytes 2097184 | tf_op jit(solution)/shard_map/ppermute | solution.py:412
  242.6 22.1 %collective-permute-done.26 = bf16[128,2048]{1,0:T(8,128)(2,1)} collective-permute-done((bf16[128,2048]{1,0:T(8,128)(2,1)S(1)}, bf16[128,2048]{1,0:T(8,128)(2,1)}, u32[]{:S(2)}, u32[]{:S(2)}) %collective-permute-start.26) | collective-permute-done | bytes 524320 | tf_op jit(solution)/shard_map/ppermute | solution.py:418
  264.8 2.9 pad_maximum_fusion.2.hn_own
  267.7 3.2 constant_dynamic-update-slice_fusion.2
  270.9 3.2 constant_dynamic-update-slice_fusion.1.dy_own
  288.3 27.1 %shard_map.264 = (bf16[512,2048]{1,0:T(8,128)(2,1)}, bf16[512,2048]{1,0:T(8,128)(2,1)}, bf16[512,704]{1,0:T(8,128)(2,1)}, bf16[2,512,704]{2,1,0:T(8,128)(2,1)}, ...) custom-call(s32[1]{0:T(128)} %bitcast.68.me_ref, ...), custom_call_target="tpu_custom_call" | custom-call | flops 8192 | bytes 8192 | tf_op jit(solution)/shard_map/pallas_call | solution.py:777
  315.4 35.7 %collective-permute-done.34 = bf16[4,64,2048]{2,1,0:T(8,128)(2,1)} collective-permute-done((bf16[4,64,2048]{2,1,0:T(8,128)(2,1)}, bf16[4,64,2048]{2,1,0:T(8,128)(2,1)}, u32[]{:S(2)}, u32[]{:S(2)}) %collective-permute-start.34) | collective-permute-done | bytes 1048608 | tf_op jit(solution)/shard_map/ppermute | solution.py:412
  368.0 45.7 %shard_map.265 = (bf16[1024,2048]{1,0:T(8,128)(2,1)}, bf16[1024,2048]{1,0:T(8,128)(2,1)}, bf16[1024,704]{1,0:T(8,128)(2,1)}, bf16[2,1024,704]{2,1,0:T(8,128)(2,1...) custom-call(s32[1]{0:T(128)} %bitcast.68.me_ref, ...), custom_call_target="tpu_custom_call" | custom-call | flops 16384 | bytes 16384 | tf_op jit(solution)/shard_map/pallas_call | solution.py:777
  418.7 10.1 %collective-permute-done.43.hn_other = bf16[4,128,2048]{2,1,0:T(8,128)(2,1)S(1)} collective-permute-done((bf16[4,128,2048]{2,1,0:T(8,128)(2,1)S(1)}, bf16[4,128,2048]{2,1,0:T(8,128)(2,1)S(1)}, u32[]{:S(2)}, u32[]{:S(2)}) %collective-permute-start.43) | collective-permute-done | bytes 2097184 | tf_op jit(solution)/shard_map/ppermute | solution.py:385
  430.1 27.5 %shard_map.266 = (bf16[512,2048]{1,0:T(8,128)(2,1)}, bf16[512,2048]{1,0:T(8,128)(2,1)}, bf16[512,704]{1,0:T(8,128)(2,1)}, bf16[2,512,704]{2,1,0:T(8,128)(2,1)}, ...) custom-call(s32[1]{0:T(128)} %bitcast.68.me_ref, ...), custom_call_target="tpu_custom_call" | custom-call | flops 8192 | bytes 8192 | tf_op jit(solution)/shard_map/pallas_call | solution.py:777
  463.4 2.9 fusion.118
  476.4 4.1 all-to-all-start.1
  480.6 11.2 %shard_map.270 = f32[1,704,2048]{2,1,0:T(8,128)} custom-call(bf16[1,512,704]{2,1,0:T(8,128)(2,1)} %bitcast.419, bf16[1,1024,704]{2,1,0:T(8,128)(2,1)} %bitcast.412, bf16[1,512,704]{2,1,0:T(8,128)(2,1)} %bitcast.420, bf16[512,2048]{1,0:T(8,128)(2,1)} %get-tuple-element.345.refs_3_, bf16[1024,2048]{1,0:T(8,128)(2,1)} %get-tuple-element.346.refs_4_, ...), custom_call_target="tpu_custom_call" | custom-call | flops 2048 | bytes 2048 | tf_op jit(solution)/shard_map/pallas_call | solution.py:1126
  491.7 8.4 shard_map.267
  500.1 8.4 shard_map.269
  508.5 12.5 %shard_map.268 = (bf16[8,128,2048]{2,1,0:T(8,128)(2,1)}, bf16[8,128,2048]{2,1,0:T(8,128)(2,1)}) custom-call(bf16[1024,704]{1,0:T(8,128)(2,1)} %get-tuple-element.335.act, bf16[8,128,128]{2,1,0:T(8,128)(2,1)} %get-tuple-element.336.sact_own, bf16[8,128,128]{2,1,0:T(8,128)(2,1)} %get-tuple-element.337.sact_other, f32[8,128,128]{2,1,0:T(8,128)} %slice.718.meta_own, ...), custom_call_target="tpu_custom_call" | custom-call | flops 268435456 | bytes 2097152 | tf_op jit(solution)/shard_map/pallas_call | solution.py:1158
  521.0 12.8 %all-to-all-done.1 = bf16[266,16,128]{2,0,1:T(8,128)(2,1)S(1)} async-done(((bf16[266,16,128]{2,0,1:T(8,128)(2,1)}), bf16[266,16,128]{2,0,1:T(8,128)(2,1)S(1)}, u32[]{:S(2)}, u32[]{:S(2)}) %all-to-all-start.1) | async-done | bytes 1089568 | tf_op jit(solution)/shard_map/all_to_all | solution.py:1486
  533.8 5.9 fusion.13
  542.8 22.8 %shard_map.271 = f32[2,704,2048]{2,1,0:T(8,128)} custom-call(bf16[2,512,704]{2,1,0:T(8,128)(2,1)} %get-tuple-element.364.refs_0_, bf16[2,1024,704]{2,1,0:T(8,128)(2,1)} %get-tuple-element.365.refs_1_, bf16[2,512,704]{2,1,0:T(8,128)(2,1)} %get-tuple-element.366.refs_2_, bf16[512,2048]{1,0:T(8,128)(2,1)} %get-tuple-element.367.refs_3_, ...), custom_call_target="tpu_custom_call" | custom-call | flops 2048 | bytes 2048 | tf_op jit(solution)/shard_map/pallas_call | solution.py:1126
  572.6 4.6 fusion.12
  582.9 7.5 collective-permute-done.52
  590.3 32.3 %collective-permute-done.53 = bf16[128,2048]{1,0:T(8,128)(2,1)S(1)} collective-permute-done((bf16[128,2048]{1,0:T(8,128)(2,1)S(1)}, bf16[128,2048]{1,0:T(8,128)(2,1)S(1)}, u32[]{:S(2)}, u32[]{:S(2)}) %collective-permute-start.53) | collective-permute-done | bytes 524320 | tf_op jit(solution)/shard_map/ppermute | solution.py:418
  627.5 10.1 %collective-permute-done.57 = bf16[128,2048]{1,0:T(8,128)(2,1)S(1)} collective-permute-done((bf16[128,2048]{1,0:T(8,128)(2,1)S(1)}, bf16[128,2048]{1,0:T(8,128)(2,1)S(1)}, u32[]{:S(2)}, u32[]{:S(2)}) %collective-permute-start.57) | collective-permute-done | bytes 524320 | tf_op jit(solution)/shard_map/ppermute | solution.py:412
  637.6 13.3 %collective-permute-done.56 = bf16[128,2048]{1,0:T(8,128)(2,1)S(1)} collective-permute-done((bf16[128,2048]{1,0:T(8,128)(2,1)S(1)}, bf16[128,2048]{1,0:T(8,128)(2,1)S(1)}, u32[]{:S(2)}, u32[]{:S(2)}) %collective-permute-start.56) | collective-permute-done | bytes 524320 | tf_op jit(solution)/shard_map/ppermute | solution.py:412
  653.0 4.1 fusion.9
  658.4 22.0 %shard_map.272 = (bf16[2048,640]{1,0:T(8,128)(2,1)}, bf16[512,512]{1,0:T(8,128)(2,1)}, bf16[4,128,2048]{2,1,0:T(8,128)(2,1)}, bf16[4,128,2048]{2,1,0:T(8,128)(2,...) custom-call(s32[1]{0:T(128)} %bitcast.core_ref, bf16[4,128,2048]{2,1,0:T(8,128)(2,1)} %copy-done.22, ...), custom_call_target="tpu_custom_call" | custom-call | flops 536870912 | bytes 4194304 | tf_op jit(solution)/shard_map/pallas_call | solution.py:1066
  691.1 3.4 collective-permute-start.61
  698.2 12.3 %collective-permute-done.61 = bf16[512,768]{1,0:T(8,128)(2,1)S(1)} collective-permute-done((bf16[512,768]{1,0:T(8,128)(2,1)S(1)}, bf16[512,768]{1,0:T(8,128)(2,1)S(1)}, u32[]{:S(2)}, u32[]{:S(2)}) %collective-permute-start.61) | collective-permute-done | bytes 786464 | tf_op jit(solution)/shard_map/ppermute | solution.py:529
  714.5 4.7 collective-permute-start.67
  719.3 4.0 fusion.8
  726.5 6.9 collective-permute-done.67
  736.7 5.6 collective-permute-start.73
  751.5 5.0 collective-permute-done.76
  756.6 5.1 collective-permute-start.81
  763.1 7.0 collective-permute-done.81
  770.1 4.1 fusion.41
  774.9 4.6 all-to-all-start.2
  779.5 2.9 fusion.51
  783.9 4.1 collective-permute-start.83
  796.0 5.0 collective-permute-start.85
  813.6 2.9 convolution_convert_fusion
  824.3 3.5 collective-permute-start.89
  843.8 5.0 collective-permute-start.92
  860.3 4.0 maximum_select_fusion.1
  (660 shorter events, 251.0 us)
Async XLA Ops:
  28.8 21.9 %collective-permute-start.15 = (bf16[4,128,768]{2,1,0:T(8,128)(2,1)}, bf16[4,128,768]{2,1,0:T(8,128)(2,1)}, u32[]{:S(2)}, u32[]{:S(2)}) collective-permute-start(bf16[4,128,768]{2,1,0:T(8,128)(2,1)} %pad_maximum_fusion.15), channel_id=1, source_target_pairs={{8,0},{10,2},{12,4},{14,6},{16,8},{18,10},{20,12},{22,14},{24,16},... | collective-permute-start | bytes 2359304 | tf_op jit(solution)/shard_map/ppermute | solution.py:447
  30.0 21.9 %collective-permute-start.12 = (bf16[4,128,768]{2,1,0:T(8,128)(2,1)}, bf16[4,128,768]{2,1,0:T(8,128)(2,1)}, u32[]{:S(2)}, u32[]{:S(2)}) collective-permute-start(bf16[4,128,768]{2,1,0:T(8,128)(2,1)} %pad_maximum_fusion.15), channel_id=1, source_target_pairs={{0,8},{2,10},{4,12},{6,14},{8,16},{10,18},{12,20},{14,22},{16,24},... | collective-permute-start | bytes 2359304 | tf_op jit(solution)/shard_map/ppermute | solution.py:447
  38.2 19.7 %collective-permute-start.9 = (bf16[2,128,4,384]{3,1,2,0:T(8,128)(2,1)}, bf16[2,128,4,384]{3,1,2,0:T(8,128)(2,1)}, u32[]{:S(2)}, u32[]{:S(2)}) collective-permute-start(bf16[2,128,4,384]{3,1,2,0:T(8,128)(2,1)} %pad_maximum_fusion.16), channel_id=1, source_target_pairs={{0,4},{2,6},{4,0},{6,2},{8,12},{10,14},{12,8},{14,10},{16,20},{18,... | collective-permute-start | bytes 2359304 | tf_op jit(solution)/shard_map/ppermute | solution.py:412
  40.4 24.7 %collective-permute-start.7 = (bf16[2,128,2048]{2,1,0:T(8,128)(2,1)S(1)}, bf16[2,128,2048]{2,1,0:T(8,128)(2,1)S(1)}, u32[]{:S(2)}, u32[]{:S(2)}) collective-permute-start(bf16[2,128,2048]{2,1,0:T(8,128)(2,1)S(1)} %pad_maximum_fusion.13), channel_id=1, source_target_pairs={{0,2},{2,0},{4,6},{6,4},{8,10},{10,8},{12,14},{14,12},{16,18},{18,... | collective-permute-start | bytes 3145736 | tf_op jit(solution)/shard_map/ppermute | solution.py:412
  50.7 20.9 %collective-permute-start.16 = (bf16[4,128,768]{2,1,0:T(8,128)(2,1)}, bf16[4,128,768]{2,1,0:T(8,128)(2,1)}, u32[]{:S(2)}, u32[]{:S(2)}) collective-permute-start(bf16[4,128,768]{2,1,0:T(8,128)(2,1)} %collective-permute-done.15), channel_id=1, source_target_pairs={{8,0},{10,2},{12,4},{14,6},{16,8},{18,10},{20,12},{22,14},{24,16},... | collective-permute-start | bytes 2359304 | tf_op jit(solution)/shard_map/ppermute | solution.py:447
  52.0 20.9 %collective-permute-start.13 = (bf16[4,128,768]{2,1,0:T(8,128)(2,1)}, bf16[4,128,768]{2,1,0:T(8,128)(2,1)}, u32[]{:S(2)}, u32[]{:S(2)}) collective-permute-start(bf16[4,128,768]{2,1,0:T(8,128)(2,1)} %collective-permute-done.12), channel_id=1, source_target_pairs={{0,8},{2,10},{4,12},{6,14},{8,16},{10,18},{12,20},{14,22},{16,24},... | collective-permute-start | bytes 2359304 | tf_op jit(solution)/shard_map/ppermute | solution.py:447
  62.6 25.0 %collective-permute-start.10 = (bf16[16,64,768]{2,1,0:T(8,128)(2,1)}, bf16[16,64,768]{2,1,0:T(8,128)(2,1)}, u32[]{:S(2)}, u32[]{:S(2)}) collective-permute-start(bf16[16,64,768]{2,1,0:T(8,128)(2,1)} %pad_maximum_fusion.9), channel_id=1, source_target_pairs={{0,1},{1,0},{2,3},{3,2},{4,5},{5,4},{6,7},{7,6},{8,9},{9,8},{10,11... | collective-permute-start | bytes 4718600 | tf_op jit(solution)/shard_map/ppermute | solution.py:385
  66.9 28.8 %collective-permute-start.11 = (bf16[4,128,2048]{2,1,0:T(8,128)(2,1)}, bf16[4,128,2048]{2,1,0:T(8,128)(2,1)}, u32[]{:S(2)}, u32[]{:S(2)}) collective-permute-start(bf16[4,128,2048]{2,1,0:T(8,128)(2,1)} %pad_maximum_fusion.x_own), channel_id=1, source_target_pairs={{0,1},{1,0},{2,3},{3,2},{4,5},{5,4},{6,7},{7,6},{8,9},{9,8},{10,11... | collective-permute-start | bytes 6291464 | tf_op jit(solution)/shard_map/ppermute | solution.py:385
  71.5 23.2 %collective-permute-start.17 = (bf16[4,128,768]{2,1,0:T(8,128)(2,1)}, bf16[4,128,768]{2,1,0:T(8,128)(2,1)}, u32[]{:S(2)}, u32[]{:S(2)}) collective-permute-start(bf16[4,128,768]{2,1,0:T(8,128)(2,1)} %collective-permute-done.16), channel_id=1, source_target_pairs={{8,0},{10,2},{12,4},{14,6},{16,8},{18,10},{20,12},{22,14},{24,16},... | collective-permute-start | bytes 2359304 | tf_op jit(solution)/shard_map/ppermute | solution.py:447
  72.8 22.8 %collective-permute-start.14 = (bf16[4,128,768]{2,1,0:T(8,128)(2,1)}, bf16[4,128,768]{2,1,0:T(8,128)(2,1)}, u32[]{:S(2)}, u32[]{:S(2)}) collective-permute-start(bf16[4,128,768]{2,1,0:T(8,128)(2,1)} %collective-permute-done.13), channel_id=1, source_target_pairs={{0,8},{2,10},{4,12},{6,14},{8,16},{10,18},{12,20},{14,22},{16,24},... | collective-permute-start | bytes 2359304 | tf_op jit(solution)/shard_map/ppermute | solution.py:447
  100.4 31.2 %collective-permute-start.20 = (bf16[128,2048]{1,0:T(8,128)(2,1)}, bf16[128,2048]{1,0:T(8,128)(2,1)}, u32[]{:S(2)}, u32[]{:S(2)}) collective-permute-start(bf16[128,2048]{1,0:T(8,128)(2,1)} %constant_dynamic-slice_fusion.34), channel_id=1, source_target_pairs={{0,24},{2,26},{4,28},{6,30},{8,0},{10,2},{12,4},{14,6},{16,8},{18,... | collective-permute-start | bytes 1572872 | tf_op jit(solution)/shard_map/ppermute | solution.py:418
  106.7 43.7 %collective-permute-start.19 = (bf16[128,2048]{1,0:T(8,128)(2,1)}, bf16[128,2048]{1,0:T(8,128)(2,1)}, u32[]{:S(2)}, u32[]{:S(2)}) collective-permute-start(bf16[128,2048]{1,0:T(8,128)(2,1)} %constant_dynamic-slice_fusion.34), channel_id=1, source_target_pairs={{0,16},{2,18},{4,20},{6,22},{8,24},{10,26},{12,28},{14,30},{16,0},... | collective-permute-start | bytes 1572872 | tf_op jit(solution)/shard_map/ppermute | solution.py:418
  106.7 43.7 %collective-permute-start.18 = (bf16[128,2048]{1,0:T(8,128)(2,1)}, bf16[128,2048]{1,0:T(8,128)(2,1)}, u32[]{:S(2)}, u32[]{:S(2)}) collective-permute-start(bf16[128,2048]{1,0:T(8,128)(2,1)} %constant_dynamic-slice_fusion.34), channel_id=1, source_target_pairs={{0,8},{2,10},{4,12},{6,14},{8,16},{10,18},{12,20},{14,22},{16,24},... | collective-permute-start | bytes 1572872 | tf_op jit(solution)/shard_map/ppermute | solution.py:418
  161.5 25.2 %collective-permute-start.24 = (bf16[128,2048]{1,0:T(8,128)(2,1)S(1)}, bf16[128,2048]{1,0:T(8,128)(2,1)S(1)}, u32[]{:S(2)}, u32[]{:S(2)}) collective-permute-start(bf16[128,2048]{1,0:T(8,128)(2,1)S(1)} %get-tuple-element.604), channel_id=1, source_target_pairs={{0,6},{2,4},{4,2},{6,0},{8,14},{10,12},{12,10},{14,8},{16,22},{18,... | collective-permute-start | bytes 1572872 | tf_op jit(solution)/shard_map/ppermute | solution.py:412
  163.3 24.2 %collective-permute-start.23 = (bf16[128,2048]{1,0:T(8,128)(2,1)S(1)}, bf16[128,2048]{1,0:T(8,128)(2,1)S(1)}, u32[]{:S(2)}, u32[]{:S(2)}) collective-permute-start(bf16[128,2048]{1,0:T(8,128)(2,1)S(1)} %get-tuple-element.605), channel_id=1, source_target_pairs={{0,4},{2,6},{4,0},{6,2},{8,12},{10,14},{12,8},{14,10},{16,20},{18,... | collective-permute-start | bytes 1572872 | tf_op jit(solution)/shard_map/ppermute | solution.py:412
  169.1 28.8 %collective-permute-start.30 = (bf16[4,128,2048]{2,1,0:T(8,128)(2,1)}, bf16[4,128,2048]{2,1,0:T(8,128)(2,1)}, u32[]{:S(2)}, u32[]{:S(2)}) collective-permute-start(bf16[4,128,2048]{2,1,0:T(8,128)(2,1)} %pad_maximum_fusion.1.dy_own), channel_id=1, source_target_pairs={{0,1},{1,0},{2,3},{3,2},{4,5},{5,4},{6,7},{7,6},{8,9},{9,8},{10,11... | collective-permute-start | bytes 6291464 | tf_op jit(solution)/shard_map/ppermute | solution.py:385
  169.9 72.7 %collective-permute-start.29 = (bf16[4,128,2048]{2,1,0:T(8,128)(2,1)}, bf16[4,128,2048]{2,1,0:T(8,128)(2,1)}, u32[]{:S(2)}, u32[]{:S(2)}) collective-permute-start(bf16[4,128,2048]{2,1,0:T(8,128)(2,1)} %pad_maximum_fusion.1.dy_own), channel_id=1, source_target_pairs={{0,4},{2,6},{4,0},{6,2},{8,12},{10,14},{12,8},{14,10},{16,20},{18,... | collective-permute-start | bytes 6291464 | tf_op jit(solution)/shard_map/ppermute | solution.py:412
  174.4 68.2 %collective-permute-start.28 = (bf16[4,128,2048]{2,1,0:T(8,128)(2,1)}, bf16[4,128,2048]{2,1,0:T(8,128)(2,1)}, u32[]{:S(2)}, u32[]{:S(2)}) collective-permute-start(bf16[4,128,2048]{2,1,0:T(8,128)(2,1)} %pad_maximum_fusion.1.dy_own), channel_id=1, source_target_pairs={{0,2},{2,0},{4,6},{6,4},{8,10},{10,8},{12,14},{14,12},{16,18},{18,... | collective-permute-start | bytes 6291464 | tf_op jit(solution)/shard_map/ppermute | solution.py:412
  188.3 76.5 %all-to-all-start = ((bf16[16,264,128]{2,1,0:T(8,128)(2,1)}), bf16[16,264,128]{2,1,0:T(8,128)(2,1)}, u32[]{:S(2)}, u32[]{:S(2)}) async-start(bf16[16,264,128]{2,1,0:T(8,128)(2,1)} %bitcast.414), calls=%async_computation | async-start | bytes 2162688 | tf_op jit(solution)/shard_map/all_to_all | solution.py:1398
  193.4 49.2 %collective-permute-start.27 = (bf16[128,2048]{1,0:T(8,128)(2,1)S(1)}, bf16[128,2048]{1,0:T(8,128)(2,1)}, u32[]{:S(2)}, u32[]{:S(2)}) collective-permute-start(bf16[128,2048]{1,0:T(8,128)(2,1)S(1)} %multiply_convert_fusion), channel_id=1, source_target_pairs={{0,24},{2,26},{4,28},{6,30},{8,0},{10,2},{12,4},{14,6},{16,8},{18,... | collective-permute-start | bytes 1572872 | tf_op jit(solution)/shard_map/ppermute | solution.py:418
  196.6 68.2 %collective-permute-start.26 = (bf16[128,2048]{1,0:T(8,128)(2,1)S(1)}, bf16[128,2048]{1,0:T(8,128)(2,1)}, u32[]{:S(2)}, u32[]{:S(2)}) collective-permute-start(bf16[128,2048]{1,0:T(8,128)(2,1)S(1)} %multiply_convert_fusion), channel_id=1, source_target_pairs={{0,16},{2,18},{4,20},{6,22},{8,24},{10,26},{12,28},{14,30},{16,0},... | collective-permute-start | bytes 1572872 | tf_op jit(solution)/shard_map/ppermute | solution.py:418
  197.9 66.9 %collective-permute-start.25 = (bf16[128,2048]{1,0:T(8,128)(2,1)S(1)}, bf16[128,2048]{1,0:T(8,128)(2,1)}, u32[]{:S(2)}, u32[]{:S(2)}) collective-permute-start(bf16[128,2048]{1,0:T(8,128)(2,1)S(1)} %multiply_convert_fusion), channel_id=1, source_target_pairs={{0,8},{2,10},{4,12},{6,14},{8,16},{10,18},{12,20},{14,22},{16,24},... | collective-permute-start | bytes 1572872 | tf_op jit(solution)/shard_map/ppermute | solution.py:418
  274.0 77.1 %collective-permute-start.36 = (bf16[8,128,2048]{2,1,0:T(8,128)(2,1)}, bf16[8,128,2048]{2,1,0:T(8,128)(2,1)}, u32[]{:S(2)}, u32[]{:S(2)}) collective-permute-start(bf16[8,128,2048]{2,1,0:T(8,128)(2,1)} %constant_dynamic-update-slice_fusion.1.dy_own), channel_id=1, source_target_pairs={{0,1},{1,0},{2,3},{3,2},{4,5},{5,4},{6,7},{7,6},{8,9},{9,8},{10,11... | collective-permute-start | bytes 12582920 | tf_op jit(solution)/shard_map/ppermute | solution.py:385
  281.1 70.0 %collective-permute-start.32 = (bf16[4,128,2048]{2,1,0:T(8,128)(2,1)}, bf16[4,128,2048]{2,1,0:T(8,128)(2,1)S(1)}, u32[]{:S(2)}, u32[]{:S(2)}) collective-permute-start(bf16[4,128,2048]{2,1,0:T(8,128)(2,1)} %pad_maximum_fusion.2.hn_own), channel_id=1, source_target_pairs={{0,4},{2,6},{4,0},{6,2},{8,12},{10,14},{12,8},{14,10},{16,20},{18,... | collective-permute-start | bytes 6291464 | tf_op jit(solution)/shard_map/ppermute | solution.py:412
  281.9 69.2 %collective-permute-start.31 = (bf16[4,128,2048]{2,1,0:T(8,128)(2,1)}, bf16[4,128,2048]{2,1,0:T(8,128)(2,1)}, u32[]{:S(2)}, u32[]{:S(2)}) collective-permute-start(bf16[4,128,2048]{2,1,0:T(8,128)(2,1)} %pad_maximum_fusion.2.hn_own), channel_id=1, source_target_pairs={{0,2},{2,0},{4,6},{6,4},{8,10},{10,8},{12,14},{14,12},{16,18},{18,... | collective-permute-start | bytes 6291464 | tf_op jit(solution)/shard_map/ppermute | solution.py:412
  283.1 68.0 %collective-permute-start.34 = (bf16[4,64,2048]{2,1,0:T(8,128)(2,1)}, bf16[4,64,2048]{2,1,0:T(8,128)(2,1)}, u32[]{:S(2)}, u32[]{:S(2)}) collective-permute-start(bf16[4,64,2048]{2,1,0:T(8,128)(2,1)} %slice.705), channel_id=1, source_target_pairs={{0,2},{2,0},{4,6},{6,4},{8,10},{10,8},{12,14},{14,12},{16,18},{18,... | collective-permute-start | bytes 3145736 | tf_op jit(solution)/shard_map/ppermute | solution.py:412
  285.7 65.4 %collective-permute-start.33 = (bf16[4,64,2048]{2,1,0:T(8,128)(2,1)}, bf16[4,64,2048]{2,1,0:T(8,128)(2,1)}, u32[]{:S(2)}, u32[]{:S(2)}) collective-permute-start(bf16[4,64,2048]{2,1,0:T(8,128)(2,1)} %slice.704), channel_id=1, source_target_pairs={{0,4},{2,6},{4,0},{6,2},{8,12},{10,14},{12,8},{14,10},{16,20},{18,... | collective-permute-start | bytes 3145736 | tf_op jit(solution)/shard_map/ppermute | solution.py:412
  361.3 52.4 %collective-permute-start.41 = (bf16[4,128,2048]{2,1,0:T(8,128)(2,1)}, bf16[4,128,2048]{2,1,0:T(8,128)(2,1)}, u32[]{:S(2)}, u32[]{:S(2)}) collective-permute-start(bf16[4,128,2048]{2,1,0:T(8,128)(2,1)} %constant_dynamic-update-slice_fusion.5.dy_own), channel_id=1, source_target_pairs={{0,1},{1,0},{2,3},{3,2},{4,5},{5,4},{6,7},{7,6},{8,9},{9,8},{10,11... | collective-permute-start | bytes 6291464 | tf_op jit(solution)/shard_map/ppermute | solution.py:385
  364.8 48.9 %collective-permute-start.39 = (bf16[4,64,2048]{2,1,0:T(8,128)(2,1)}, bf16[4,64,2048]{2,1,0:T(8,128)(2,1)S(1)}, u32[]{:S(2)}, u32[]{:S(2)}) collective-permute-start(bf16[4,64,2048]{2,1,0:T(8,128)(2,1)} %slice.717), channel_id=1, source_target_pairs={{0,2},{2,0},{4,6},{6,4},{8,10},{10,8},{12,14},{14,12},{16,18},{18,... | collective-permute-start | bytes 3145736 | tf_op jit(solution)/shard_map/ppermute | solution.py:412
  366.0 47.7 %collective-permute-start.38 = (bf16[4,64,2048]{2,1,0:T(8,128)(2,1)}, bf16[4,64,2048]{2,1,0:T(8,128)(2,1)S(1)}, u32[]{:S(2)}, u32[]{:S(2)}) collective-permute-start(bf16[4,64,2048]{2,1,0:T(8,128)(2,1)} %slice.716), channel_id=1, source_target_pairs={{0,4},{2,6},{4,0},{6,2},{8,12},{10,14},{12,8},{14,10},{16,20},{18,... | collective-permute-start | bytes 3145736 | tf_op jit(solution)/shard_map/ppermute | solution.py:412
  415.0 48.4 %collective-permute-start.42 = (bf16[8,128,2048]{2,1,0:T(8,128)(2,1)}, bf16[8,128,2048]{2,1,0:T(8,128)(2,1)}, u32[]{:S(2)}, u32[]{:S(2)}) collective-permute-start(bf16[8,128,2048]{2,1,0:T(8,128)(2,1)} %get-tuple-element.304), channel_id=1, source_target_pairs={{0,1},{1,0},{2,3},{3,2},{4,5},{5,4},{6,7},{7,6},{8,9},{9,8},{10,11... | collective-permute-start | bytes 12582920 | tf_op jit(solution)/shard_map/ppermute | solution.py:385
  417.7 48.5 %collective-permute-start.37 = (bf16[4,128,2048]{2,1,0:T(8,128)(2,1)}, bf16[4,128,2048]{2,1,0:T(8,128)(2,1)}, u32[]{:S(2)}, u32[]{:S(2)}) collective-permute-start(bf16[4,128,2048]{2,1,0:T(8,128)(2,1)} %get-tuple-element.286), channel_id=1, source_target_pairs={{0,1},{1,0},{2,3},{3,2},{4,5},{5,4},{6,7},{7,6},{8,9},{9,8},{10,11... | collective-permute-start | bytes 6291464 | tf_op jit(solution)/shard_map/ppermute | solution.py:385
  473.9 59.9 %collective-permute-start.46 = (bf16[2,4,64,2048]{3,2,1,0:T(8,128)(2,1)}, bf16[2,4,64,2048]{3,2,1,0:T(8,128)(2,1)}, u32[]{:S(2)}, u32[]{:S(2)}) collective-permute-start(bf16[2,4,64,2048]{3,2,1,0:T(8,128)(2,1)} %pad_maximum_fusion.3), channel_id=1, source_target_pairs={{0,4},{2,6},{4,0},{6,2},{8,12},{10,14},{12,8},{14,10},{16,20},{18,... | collective-permute-start | bytes 6291464 | tf_op jit(solution)/shard_map/ppermute | solution.py:412
  475.1 58.7 %collective-permute-start.47 = (bf16[2,4,64,2048]{3,2,1,0:T(8,128)(2,1)}, bf16[2,4,64,2048]{3,2,1,0:T(8,128)(2,1)}, u32[]{:S(2)}, u32[]{:S(2)}) collective-permute-start(bf16[2,4,64,2048]{3,2,1,0:T(8,128)(2,1)} %pad_maximum_fusion.4), channel_id=1, source_target_pairs={{0,2},{2,0},{4,6},{6,4},{8,10},{10,8},{12,14},{14,12},{16,18},{18,... | collective-permute-start | bytes 6291464 | tf_op jit(solution)/shard_map/ppermute | solution.py:412
  476.4 57.3 %all-to-all-start.1 = ((bf16[266,16,128]{2,0,1:T(8,128)(2,1)}), bf16[266,16,128]{2,0,1:T(8,128)(2,1)S(1)}, u32[]{:S(2)}, u32[]{:S(2)}) async-start(bf16[266,16,128]{2,0,1:T(8,128)(2,1)} %pad_maximum_fusion.11), calls=%async_computation.1 | async-start | bytes 2228224 | tf_op jit(solution)/shard_map/all_to_all | solution.py:1486
  539.7 28.2 %collective-permute-start.50 = (bf16[8,128,2048]{2,1,0:T(8,128)(2,1)}, bf16[8,128,2048]{2,1,0:T(8,128)(2,1)}, u32[]{:S(2)}, u32[]{:S(2)}) collective-permute-start(bf16[8,128,2048]{2,1,0:T(8,128)(2,1)} %get-tuple-element.371), channel_id=1, source_target_pairs={{0,1},{1,0},{2,3},{3,2},{4,5},{5,4},{6,7},{7,6},{8,9},{9,8},{10,11... | collective-permute-start | bytes 12582920 | tf_op jit(solution)/shard_map/ppermute | solution.py:385
  541.2 24.7 %collective-permute-start.51 = (bf16[4,128,2048]{2,1,0:T(8,128)(2,1)}, bf16[4,128,2048]{2,1,0:T(8,128)(2,1)S(1)}, u32[]{:S(2)}, u32[]{:S(2)}) collective-permute-start(bf16[4,128,2048]{2,1,0:T(8,128)(2,1)} %get-tuple-element.373), channel_id=1, source_target_pairs={{0,1},{1,0},{2,3},{3,2},{4,5},{5,4},{6,7},{7,6},{8,9},{9,8},{10,11... | collective-permute-start | bytes 6291464 | tf_op jit(solution)/shard_map/ppermute | solution.py:385
  541.3 30.0 %collective-permute-start.48 = (bf16[4,64,2048]{2,1,0:T(8,128)(2,1)}, bf16[4,64,2048]{2,1,0:T(8,128)(2,1)}, u32[]{:S(2)}, u32[]{:S(2)}) collective-permute-start(bf16[4,64,2048]{2,1,0:T(8,128)(2,1)} %get-tuple-element.362), channel_id=1, source_target_pairs={{0,2},{2,0},{4,6},{6,4},{8,10},{10,8},{12,14},{14,12},{16,18},{18,... | collective-permute-start | bytes 3145736 | tf_op jit(solution)/shard_map/ppermute | solution.py:412
  542.0 29.3 %collective-permute-start.49 = (bf16[4,64,2048]{2,1,0:T(8,128)(2,1)}, bf16[4,64,2048]{2,1,0:T(8,128)(2,1)}, u32[]{:S(2)}, u32[]{:S(2)}) collective-permute-start(bf16[4,64,2048]{2,1,0:T(8,128)(2,1)} %get-tuple-element.363), channel_id=1, source_target_pairs={{0,4},{2,6},{4,0},{6,2},{8,12},{10,14},{12,8},{14,10},{16,20},{18,... | collective-permute-start | bytes 3145736 | tf_op jit(solution)/shard_map/ppermute | solution.py:412
  577.4 45.2 %collective-permute-start.53 = (bf16[128,2048]{1,0:T(8,128)(2,1)S(1)}, bf16[128,2048]{1,0:T(8,128)(2,1)S(1)}, u32[]{:S(2)}, u32[]{:S(2)}) collective-permute-start(bf16[128,2048]{1,0:T(8,128)(2,1)S(1)} %get-tuple-element.381), channel_id=1, source_target_pairs={{0,16},{2,18},{4,20},{6,22},{8,24},{10,26},{12,28},{14,30},{16,0},... | collective-permute-start | bytes 1572872 | tf_op jit(solution)/shard_map/ppermute | solution.py:418
  577.8 44.8 %collective-permute-start.54 = (bf16[128,2048]{1,0:T(8,128)(2,1)S(1)}, bf16[128,2048]{1,0:T(8,128)(2,1)S(1)}, u32[]{:S(2)}, u32[]{:S(2)}) collective-permute-start(bf16[128,2048]{1,0:T(8,128)(2,1)S(1)} %get-tuple-element.382), channel_id=1, source_target_pairs={{0,8},{2,10},{4,12},{6,14},{8,16},{10,18},{12,20},{14,22},{16,24},... | collective-permute-start | bytes 1572872 | tf_op jit(solution)/shard_map/ppermute | solution.py:418
  579.2 71.7 %collective-permute-start.58 = (bf16[2,4,64,2048]{3,2,1,0:T(8,128)(2,1)S(1)}, bf16[2,4,64,2048]{3,2,1,0:T(8,128)(2,1)S(1)}, u32[]{:S(2)}, u32[]{:S(2)}) collective-permute-start(bf16[2,4,64,2048]{3,2,1,0:T(8,128)(2,1)S(1)} %pad_maximum_fusion.5), channel_id=1, source_target_pairs={{0,4},{2,6},{4,0},{6,2},{8,12},{10,14},{12,8},{14,10},{16,20},{18,... | collective-permute-start | bytes 6291464 | tf_op jit(solution)/shard_map/ppermute | solution.py:412
  579.5 71.4 %collective-permute-start.59 = (bf16[2,4,64,2048]{3,2,1,0:T(8,128)(2,1)S(1)}, bf16[2,4,64,2048]{3,2,1,0:T(8,128)(2,1)S(1)}, u32[]{:S(2)}, u32[]{:S(2)}) collective-permute-start(bf16[2,4,64,2048]{3,2,1,0:T(8,128)(2,1)S(1)} %pad_maximum_fusion.6), channel_id=1, source_target_pairs={{0,2},{2,0},{4,6},{6,4},{8,10},{10,8},{12,14},{14,12},{16,18},{18,... | collective-permute-start | bytes 6291464 | tf_op jit(solution)/shard_map/ppermute | solution.py:412
  626.1 24.8 %collective-permute-start.56 = (bf16[128,2048]{1,0:T(8,128)(2,1)S(1)}, bf16[128,2048]{1,0:T(8,128)(2,1)S(1)}, u32[]{:S(2)}, u32[]{:S(2)}) collective-permute-start(bf16[128,2048]{1,0:T(8,128)(2,1)S(1)} %fusion.117), channel_id=1, source_target_pairs={{0,4},{2,6},{4,0},{6,2},{8,12},{10,14},{12,8},{14,10},{16,20},{18,... | collective-permute-start | bytes 1572872 | tf_op jit(solution)/shard_map/ppermute | solution.py:412
  626.5 24.4 %collective-permute-start.55 = (bf16[128,2048]{1,0:T(8,128)(2,1)S(1)}, bf16[128,2048]{1,0:T(8,128)(2,1)S(1)}, u32[]{:S(2)}, u32[]{:S(2)}) collective-permute-start(bf16[128,2048]{1,0:T(8,128)(2,1)S(1)} %fusion.117), channel_id=1, source_target_pairs={{0,2},{2,0},{4,6},{6,4},{8,10},{10,8},{12,14},{14,12},{16,18},{18,... | collective-permute-start | bytes 1572872 | tf_op jit(solution)/shard_map/ppermute | solution.py:412
  683.1 31.4 %collective-permute-start.72 = (bf16[4,128,2048]{2,1,0:T(8,128)(2,1)}, bf16[4,128,2048]{2,1,0:T(8,128)(2,1)}, u32[]{:S(2)}, u32[]{:S(2)}) collective-permute-start(bf16[4,128,2048]{2,1,0:T(8,128)(2,1)} %get-tuple-element.416), channel_id=1, source_target_pairs={{0,1},{1,0},{2,3},{3,2},{4,5},{5,4},{6,7},{7,6},{8,9},{9,8},{10,11... | collective-permute-start | bytes 6291464 | tf_op jit(solution)/shard_map/ppermute | solution.py:385
  683.9 26.6 %collective-permute-start.65 = (bf16[4,64,2048]{2,1,0:T(8,128)(2,1)}, bf16[4,64,2048]{2,1,0:T(8,128)(2,1)}, u32[]{:S(2)}, u32[]{:S(2)}) collective-permute-start(bf16[4,64,2048]{2,1,0:T(8,128)(2,1)} %get-tuple-element.410), channel_id=1, source_target_pairs={{0,2},{2,0},{4,6},{6,4},{8,10},{10,8},{12,14},{14,12},{16,18},{18,... | collective-permute-start | bytes 3145736 | tf_op jit(solution)/shard_map/ppermute | solution.py:412
  684.4 26.1 %collective-permute-start.66 = (bf16[4,64,2048]{2,1,0:T(8,128)(2,1)}, bf16[4,64,2048]{2,1,0:T(8,128)(2,1)}, u32[]{:S(2)}, u32[]{:S(2)}) collective-permute-start(bf16[4,64,2048]{2,1,0:T(8,128)(2,1)} %get-tuple-element.411), channel_id=1, source_target_pairs={{0,4},{2,6},{4,0},{6,2},{8,12},{10,14},{12,8},{14,10},{16,20},{18,... | collective-permute-start | bytes 3145736 | tf_op jit(solution)/shard_map/ppermute | solution.py:412
  691.1 19.3 %collective-permute-start.61 = (bf16[512,768]{1,0:T(8,128)(2,1)S(1)}, bf16[512,768]{1,0:T(8,128)(2,1)S(1)}, u32[]{:S(2)}, u32[]{:S(2)}) collective-permute-start(bf16[512,768]{1,0:T(8,128)(2,1)S(1)} %get-tuple-element.587), channel_id=1, source_target_pairs={{0,8},{2,10},{4,12},{6,14},{1,9},{3,11},{5,13},{7,15}} | collective-permute-start | bytes 2359304 | tf_op jit(solution)/shard_map/ppermute | solution.py:529
  714.5 18.9 %collective-permute-start.67 = (bf16[512,768]{1,0:T(8,128)(2,1)S(1)}, bf16[512,768]{1,0:T(8,128)(2,1)S(1)}, u32[]{:S(2)}, u32[]{:S(2)}) collective-permute-start(bf16[512,768]{1,0:T(8,128)(2,1)S(1)} %get-tuple-element.585), channel_id=1, source_target_pairs={{0,8},{2,10},{4,12},{6,14},{8,16},{10,18},{12,20},{14,22},{1,9},{3... | collective-permute-start | bytes 2359304 | tf_op jit(solution)/shard_map/ppermute | solution.py:529
  723.7 19.1 %collective-permute-start.78 = (bf16[128,2048]{1,0:T(8,128)(2,1)S(1)}, bf16[128,2048]{1,0:T(8,128)(2,1)S(1)}, u32[]{:S(2)}, u32[]{:S(2)}) collective-permute-start(bf16[128,2048]{1,0:T(8,128)(2,1)S(1)} %get-tuple-element.596), channel_id=1, source_target_pairs={{0,2},{2,0},{4,6},{6,4},{8,10},{10,8},{12,14},{14,12},{16,18},{18,... | collective-permute-start | bytes 1572872 | tf_op jit(solution)/shard_map/ppermute | solution.py:412
  724.4 21.6 %collective-permute-start.80 = (bf16[128,2048]{1,0:T(8,128)(2,1)S(1)}, bf16[128,2048]{1,0:T(8,128)(2,1)S(1)}, u32[]{:S(2)}, u32[]{:S(2)}) collective-permute-start(bf16[128,2048]{1,0:T(8,128)(2,1)S(1)} %get-tuple-element.597), channel_id=1, source_target_pairs={{0,6},{2,4},{4,2},{6,0},{8,14},{10,12},{12,10},{14,8},{16,22},{18,... | collective-permute-start | bytes 1572872 | tf_op jit(solution)/shard_map/ppermute | solution.py:412
  725.6 22.3 %collective-permute-start.79 = (bf16[128,2048]{1,0:T(8,128)(2,1)S(1)}, bf16[128,2048]{1,0:T(8,128)(2,1)S(1)}, u32[]{:S(2)}, u32[]{:S(2)}) collective-permute-start(bf16[128,2048]{1,0:T(8,128)(2,1)S(1)} %get-tuple-element.598), channel_id=1, source_target_pairs={{0,4},{2,6},{4,0},{6,2},{8,12},{10,14},{12,8},{14,10},{16,20},{18,... | collective-permute-start | bytes 1572872 | tf_op jit(solution)/shard_map/ppermute | solution.py:412
  735.4 34.7 %collective-permute-start.74 = (bf16[512,768]{1,0:T(8,128)(2,1)}, bf16[512,768]{1,0:T(8,128)(2,1)}, u32[]{:S(2)}, u32[]{:S(2)}) collective-permute-start(bf16[512,768]{1,0:T(8,128)(2,1)} %get-tuple-element.582), channel_id=1, source_target_pairs={{8,0},{10,2},{12,4},{14,6},{16,8},{18,10},{20,12},{22,14},{24,16},... | collective-permute-start | bytes 2359304 | tf_op jit(solution)/shard_map/ppermute | solution.py:529
  736.7 33.4 %collective-permute-start.73 = (bf16[512,768]{1,0:T(8,128)(2,1)}, bf16[512,768]{1,0:T(8,128)(2,1)}, u32[]{:S(2)}, u32[]{:S(2)}) collective-permute-start(bf16[512,768]{1,0:T(8,128)(2,1)} %get-tuple-element.583), channel_id=1, source_target_pairs={{0,8},{2,10},{4,12},{6,14},{8,16},{10,18},{12,20},{14,22},{16,24},... | collective-permute-start | bytes 2359304 | tf_op jit(solution)/shard_map/ppermute | solution.py:529
  747.9 15.2 %collective-permute-start.75 = (bf16[128,576]{1,0:T(8,128)(2,1)S(1)}, bf16[128,576]{1,0:T(8,128)(2,1)S(1)}, u32[]{:S(2)}, u32[]{:S(2)}) collective-permute-start(bf16[128,576]{1,0:T(8,128)(2,1)S(1)} %pad_maximum_fusion.22), channel_id=1, source_target_pairs={{0,2},{2,0},{4,6},{6,4},{8,10},{10,8},{12,14},{14,12},{16,18},{18,... | collective-permute-start | bytes 442376 | tf_op jit(solution)/shard_map/ppermute | solution.py:412
  774.9 20.1 %all-to-all-start.2 = ((f32[19,16,128]{2,0,1:T(8,128)}), f32[19,16,128]{2,0,1:T(8,128)S(1)}, u32[]{:S(2)}, u32[]{:S(2)}) async-start(f32[19,16,128]{2,0,1:T(8,128)} %pad_maximum_fusion.21), calls=%async_computation.2 | async-start | bytes 393216 | tf_op jit(solution)/shard_map/all_to_all | solution.py:1641
  782.5 27.7 %collective-permute-start.84 = (bf16[128,2048]{1,0:T(8,128)(2,1)}, bf16[128,2048]{1,0:T(8,128)(2,1)}, u32[]{:S(2)}, u32[]{:S(2)}) collective-permute-start(bf16[128,2048]{1,0:T(8,128)(2,1)} %get-tuple-element.592), channel_id=1, source_target_pairs={{16,8},{18,10},{20,12},{22,14},{24,16},{26,18},{28,20},{30,22},{17... | collective-permute-start | bytes 1572872 | tf_op jit(solution)/shard_map/ppermute | solution.py:529
  783.9 26.3 %collective-permute-start.83 = (bf16[128,2048]{1,0:T(8,128)(2,1)}, bf16[128,2048]{1,0:T(8,128)(2,1)}, u32[]{:S(2)}, u32[]{:S(2)}) collective-permute-start(bf16[128,2048]{1,0:T(8,128)(2,1)} %get-tuple-element.593), channel_id=1, source_target_pairs={{0,8},{2,10},{4,12},{6,14},{8,16},{10,18},{12,20},{14,22},{1,9},{3... | collective-permute-start | bytes 1572872 | tf_op jit(solution)/shard_map/ppermute | solution.py:529
  824.3 14.7 %collective-permute-start.89 = (bf16[128,2048]{1,0:T(8,128)(2,1)S(1)}, bf16[128,2048]{1,0:T(8,128)(2,1)S(1)}, u32[]{:S(2)}, u32[]{:S(2)}) collective-permute-start(bf16[128,2048]{1,0:T(8,128)(2,1)S(1)} %get-tuple-element.590), channel_id=1, source_target_pairs={{0,8},{2,10},{4,12},{6,14},{8,16},{10,18},{12,20},{14,22},{16,24},... | collective-permute-start | bytes 1572872 | tf_op jit(solution)/shard_map/ppermute | solution.py:529
  833.9 20.9 %collective-permute-start.96 = (bf16[128,288]{0,1:T(8,128)(2,1)}, bf16[128,288]{0,1:T(8,128)(2,1)}, u32[]{:S(2)}, u32[]{:S(2)}) collective-permute-start(bf16[128,288]{0,1:T(8,128)(2,1)} %bitcast.376), channel_id=1, source_target_pairs={{0,24},{2,26},{4,28},{6,30},{8,0},{10,2},{12,4},{14,6},{16,8},{18,... | collective-permute-start | bytes 221192 | tf_op jit(solution)/shard_map/ppermute | solution.py:418
  836.7 18.2 %collective-permute-start.94 = (bf16[128,288]{0,1:T(8,128)(2,1)}, bf16[128,288]{0,1:T(8,128)(2,1)}, u32[]{:S(2)}, u32[]{:S(2)}) collective-permute-start(bf16[128,288]{0,1:T(8,128)(2,1)} %bitcast.378), channel_id=1, source_target_pairs={{0,8},{2,10},{4,12},{6,14},{8,16},{10,18},{12,20},{14,22},{16,24},... | collective-permute-start | bytes 221192 | tf_op jit(solution)/shard_map/ppermute | solution.py:418
  836.7 18.2 %collective-permute-start.95 = (bf16[128,288]{0,1:T(8,128)(2,1)}, bf16[128,288]{0,1:T(8,128)(2,1)}, u32[]{:S(2)}, u32[]{:S(2)}) collective-permute-start(bf16[128,288]{0,1:T(8,128)(2,1)} %bitcast.377), channel_id=1, source_target_pairs={{0,16},{2,18},{4,20},{6,22},{8,24},{10,26},{12,28},{14,30},{16,0},... | collective-permute-start | bytes 221192 | tf_op jit(solution)/shard_map/ppermute | solution.py:418
  843.8 16.5 %collective-permute-start.92 = (f32[128,2048]{1,0:T(8,128)}, f32[128,2048]{1,0:T(8,128)}, u32[]{:S(2)}, u32[]{:S(2)}) collective-permute-start(f32[128,2048]{1,0:T(8,128)} %get-tuple-element.619), channel_id=1, source_target_pairs={{0,1},{1,0},{2,3},{3,2},{4,5},{5,4},{6,7},{7,6},{8,9},{9,8},{10,11... | collective-permute-start | bytes 3145736 | tf_op jit(solution)/shard_map/ppermute | solution.py:385
  (146 other events, 2323.2 us)
where the time goes:
time: 874 us; the launch traced here: 865 us
  waiting for transfers between devices  270 us (31%)
  Pallas kernels  204 us (23%)
  starting transfers between devices  154 us (18%)
  other arithmetic  114 us (13%)
  local copies, waits for them, and re-layouts  108 us (12%)
  matrix products  12.1 us (1%)
    ppermute x41, waiting for transfers between devices, to_partner(): lax.ppermute(value, 'expert', [(g, g ^ flips) for g in range(groups)])  123 us
    pallas_call x3, Pallas kernels, experts(): pl.pallas_call(functools.partial(expert_kernel, shared_cols, expert_count...  100 us
    ppermute x15, waiting for transfers between devices, to_deeper(): return lax.ppermute(value, 'expert', pairs)  80.7 us
    unnamed x261, local copies, waits for them, and re-layouts  42.7 us
    pallas_call x2, Pallas kernels, column_products(): pl.pallas_call(product_kernel, grid=(width // tile, count), in_specs=[*[p...  33.9 us
    ppermute x12, starting transfers between devices, hop(): arrived.append(lax.ppermute(gone, 'expert', pairs))  33.6 us
    ppermute x41, starting transfers between devices, to_partner(): lax.ppermute(value, 'expert', [(g, g ^ flips) for g in range(groups)])  33.1 us
    pallas_call x3, Pallas kernels, outputs(): pl.pallas_call(output_kernel, grid=(groups // per_step,), in_specs=[flat(...  29.3 us
  transfers between devices with their start and end apart: 101, of which 27 were waited for; matrix products, arithmetic and copies ran while one was open for 17% of the time, Pallas kernels for 21%

commit v1 on v0

--- a/solution.py
+++ b/solution.py
@@ -1439,21 +1439,22 @@
     dy_parts = {parts[0]: (dy_line, dy_line_other)}
     hn_line, dy_beside = tie(jnp.stack(hn_came), dy_beside)
     dy_near = jnp.concatenate(dy_beside, axis=0)
-    hn_beside, dy_far, done_line, *dy_parts[parts[1]] = tie(
+    hn_beside, dy_beside, done_line, *dy_parts[parts[1]] = tie(
         hn_gather.beside(hn_line),
-        dy_gather.far(dy_beside),
+        dy_beside,
         run_experts(parts[0], hn_line, swap_cores(hn_line)),
         dy_near,
         swap_cores(dy_near),
     )
     d_line_came = swap_cores(done_line[5])
-    hn_near, dy_far = jnp.concatenate(hn_beside, axis=0), jnp.concatenate(dy_far, axis=1)
-    hn_far, done_near, *dy_parts[parts[2]] = tie(
+    hn_near = jnp.concatenate(hn_beside, axis=0)
+    hn_far, dy_far, done_near = tie(
         hn_gather.far(hn_beside),
+        dy_gather.far(dy_beside),
         run_experts(parts[1], hn_near, swap_cores(hn_near)),
-        dy_far,
-        swap_cores(dy_far),
-    )
+    )
+    dy_far = jnp.concatenate(dy_far, axis=1)
+    dy_parts[parts[2]] = dy_far, swap_cores(dy_far)
     d_near_came = swap_cores(done_near[5])
     hn_far = jnp.concatenate(hn_far, axis=1)
     done_far = run_experts(parts[2], hn_far, swap_cores(hn_far))

time: 874 us -> 853 us (0.976)
  waiting for transfers between devices: 270 us -> 249 us
    ppermute x41, waiting for transfers between devices: 123 us -> 98.7 us  [to_partner(): lax.ppermute(value, 'expert', [(g, g ^ flips) for g in range(groups)])]
    unnamed x261 -> x269, local copies, waits for them, and re-layouts: 42.7 us -> 41.6 us
  transfers between devices with their start and end apart: 101 -> 101, of which waited for: 27 -> 30; matrix products, arithmetic and copies ran while one was open for 17% -> 17% of each run, Pallas kernels for 21% -> 22%
where the time goes in v1:
time: 853 us; the launch traced here: 843 us
  waiting for transfers between devices  249 us (29%)
  Pallas kernels  204 us (24%)
  starting transfers between devices  156 us (18%)
  other arithmetic  113 us (13%)
  local copies, waits for them, and re-layouts  106 us (12%)
  matrix products  12.1 us (1%)
    pallas_call x3, Pallas kernels, experts(): pl.pallas_call(functools.partial(expert_kernel, shared_cols, expert_count...  100 us
    ppermute x41, waiting for transfers between devices, to_partner(): lax.ppermute(value, 'expert', [(g, g ^ flips) for g in range(groups)])  98.7 us
    ppermute x15, waiting for transfers between devices, to_deeper(): return lax.ppermute(value, 'expert', pairs)  80.8 us
    unnamed x269, local copies, waits for them, and re-layouts  41.6 us
    ppermute x41, starting transfers between devices, to_partner(): lax.ppermute(value, 'expert', [(g, g ^ flips) for g in range(groups)])  34.9 us
    pallas_call x2, Pallas kernels, column_products(): pl.pallas_call(product_kernel, grid=(width // tile, count), in_specs=[*[p...  33.9 us
    ppermute x12, starting transfers between devices, hop(): arrived.append(lax.ppermute(gone, 'expert', pairs))  33.3 us
    pallas_call x3, Pallas kernels, outputs(): pl.pallas_call(output_kernel, grid=(groups // per_step,), in_specs=[flat(...  29.2 us
  transfers between devices with their start and end apart: 101, of which 30 were waited for; matrix products, arithmetic and copies ran while one was open for 17% of the time, Pallas kernels for 22%

profile of v1, /device:TPU:1, one launch (start us, length us, event | category | flops | bytes accessed | tf_op | source)
XLA Modules:
  0.0 843.4 jit_solution(16969594596747098443)
XLA Ops:
  7.7 3.1 collective-permute-start.4
  21.5 3.7 collective-permute-done.2
  30.0 7.2 collective-permute-start.12
  41.9 8.7 %collective-permute-done.15 = bf16[4,128,768]{2,1,0:T(8,128)(2,1)} collective-permute-done((bf16[4,128,768]{2,1,0:T(8,128)(2,1)}, bf16[4,128,768]{2,1,0:T(8,128)(2,1)}, u32[]{:S(2)}, u32[]{:S(2)}) %collective-permute-start.15) | collective-permute-done | bytes 786464 | tf_op jit(solution)/shard_map/ppermute | solution.py:447
  52.0 5.6 collective-permute-start.13
  68.4 3.1 fusion.91
  72.9 6.8 collective-permute-start.14
  81.3 3.3 pad_maximum_fusion.19.cosine
  84.7 2.9 pad_maximum_fusion.20.sine
  90.1 4.7 collective-permute-done.17
  100.4 6.3 collective-permute-start.20
  113.3 18.4 %shard_map.263 = (bf16[4,256,2048]{2,1,0:T(8,128)(2,1)}, bf16[4,256,512]{2,1,0:T(8,128)(2,1)}, bf16[4,256,384]{2,1,0:T(8,128)(2,1)}, bf16[4,256,512]{2,1,0:T(8,1...) custom-call(s32[1]{0:T(128)} %bitcast.core_ref, ...), custom_call_target="tpu_custom_call" | custom-call | flops 5368709120 | bytes 8388608 | tf_op jit(solution)/shard_map/pallas_call | solution.py:1023
  131.7 18.7 %collective-permute-done.19 = bf16[128,2048]{1,0:T(8,128)(2,1)} collective-permute-done((bf16[128,2048]{1,0:T(8,128)(2,1)}, bf16[128,2048]{1,0:T(8,128)(2,1)}, u32[]{:S(2)}, u32[]{:S(2)}) %collective-permute-start.19) | collective-permute-done | bytes 524320 | tf_op jit(solution)/shard_map/ppermute | solution.py:418
  157.7 3.0 add_convert_fusion.1
  165.9 3.2 pad_maximum_fusion.1.dy_own
  171.2 3.3 collective-permute-done.22
  175.0 11.7 %collective-permute-done.24 = bf16[128,2048]{1,0:T(8,128)(2,1)S(1)} collective-permute-done((bf16[128,2048]{1,0:T(8,128)(2,1)S(1)}, bf16[128,2048]{1,0:T(8,128)(2,1)S(1)}, u32[]{:S(2)}, u32[]{:S(2)}) %collective-permute-start.24) | collective-permute-done | bytes 524320 | tf_op jit(solution)/shard_map/ppermute | solution.py:412
  188.3 5.0 all-to-all-start
  193.4 3.1 collective-permute-start.27
  204.4 3.8 maximum_maximum_fusion.1
  208.2 34.5 %collective-permute-done.29 = bf16[4,128,2048]{2,1,0:T(8,128)(2,1)} collective-permute-done((bf16[4,128,2048]{2,1,0:T(8,128)(2,1)}, bf16[4,128,2048]{2,1,0:T(8,128)(2,1)}, u32[]{:S(2)}, u32[]{:S(2)}) %collective-permute-start.29) | collective-permute-done | bytes 2097184 | tf_op jit(solution)/shard_map/ppermute | solution.py:412
  242.6 22.1 %collective-permute-done.26 = bf16[128,2048]{1,0:T(8,128)(2,1)} collective-permute-done((bf16[128,2048]{1,0:T(8,128)(2,1)S(1)}, bf16[128,2048]{1,0:T(8,128)(2,1)}, u32[]{:S(2)}, u32[]{:S(2)}) %collective-permute-start.26) | collective-permute-done | bytes 524320 | tf_op jit(solution)/shard_map/ppermute | solution.py:418
  264.8 2.9 pad_maximum_fusion.2.hn_own
  267.7 3.2 constant_dynamic-update-slice_fusion.2
  270.8 3.2 constant_dynamic-update-slice_fusion.1.dy_own
  285.3 27.1 %shard_map.264 = (bf16[512,2048]{1,0:T(8,128)(2,1)}, bf16[512,2048]{1,0:T(8,128)(2,1)}, bf16[512,704]{1,0:T(8,128)(2,1)}, bf16[2,512,704]{2,1,0:T(8,128)(2,1)}, ...) custom-call(s32[1]{0:T(128)} %bitcast.68.me_ref, ...), custom_call_target="tpu_custom_call" | custom-call | flops 8192 | bytes 8192 | tf_op jit(solution)/shard_map/pallas_call | solution.py:777
  312.5 11.2 %collective-permute-done.32 = bf16[4,128,2048]{2,1,0:T(8,128)(2,1)S(1)} collective-permute-done((bf16[4,128,2048]{2,1,0:T(8,128)(2,1)}, bf16[4,128,2048]{2,1,0:T(8,128)(2,1)S(1)}, u32[]{:S(2)}, u32[]{:S(2)}) %collective-permute-start.32) | collective-permute-done | bytes 2097184 | tf_op jit(solution)/shard_map/ppermute | solution.py:412
  342.5 45.7 %shard_map.265 = (bf16[1024,2048]{1,0:T(8,128)(2,1)}, bf16[1024,2048]{1,0:T(8,128)(2,1)}, bf16[1024,704]{1,0:T(8,128)(2,1)}, bf16[2,1024,704]{2,1,0:T(8,128)(2,1...) custom-call(s32[1]{0:T(128)} %bitcast.68.me_ref, ...), custom_call_target="tpu_custom_call" | custom-call | flops 16384 | bytes 16384 | tf_op jit(solution)/shard_map/pallas_call | solution.py:777
  395.8 9.1 %collective-permute-done.43.dy_other = bf16[4,128,2048]{2,1,0:T(8,128)(2,1)S(1)} collective-permute-done((bf16[4,128,2048]{2,1,0:T(8,128)(2,1)S(1)}, bf16[4,128,2048]{2,1,0:T(8,128)(2,1)S(1)}, u32[]{:S(2)}, u32[]{:S(2)}) %collective-permute-start.43) | collective-permute-done | bytes 2097184 | tf_op jit(solution)/shard_map/ppermute | solution.py:385
  404.9 3.0 collective-permute-done.42.hn_other
  409.2 27.6 %shard_map.266 = (bf16[512,2048]{1,0:T(8,128)(2,1)}, bf16[512,2048]{1,0:T(8,128)(2,1)}, bf16[512,704]{1,0:T(8,128)(2,1)}, bf16[2,512,704]{2,1,0:T(8,128)(2,1)}, ...) custom-call(s32[1]{0:T(128)} %bitcast.68.me_ref, ...), custom_call_target="tpu_custom_call" | custom-call | flops 8192 | bytes 8192 | tf_op jit(solution)/shard_map/pallas_call | solution.py:777
  441.9 2.9 fusion.118
  455.0 4.1 all-to-all-start.1
  459.1 11.2 %shard_map.270 = f32[1,704,2048]{2,1,0:T(8,128)} custom-call(bf16[1,512,704]{2,1,0:T(8,128)(2,1)} %bitcast.419, bf16[1,1024,704]{2,1,0:T(8,128)(2,1)} %bitcast.412, bf16[1,512,704]{2,1,0:T(8,128)(2,1)} %bitcast.420, bf16[512,2048]{1,0:T(8,128)(2,1)} %get-tuple-element.345.refs_3_, bf16[1024,2048]{1,0:T(8,128)(2,1)} %get-tuple-element.346.refs_4_, ...), custom_call_target="tpu_custom_call" | custom-call | flops 2048 | bytes 2048 | tf_op jit(solution)/shard_map/pallas_call | solution.py:1126
  470.3 8.4 shard_map.267
  478.7 8.3 shard_map.269
  487.0 12.5 %shard_map.268 = (bf16[8,128,2048]{2,1,0:T(8,128)(2,1)}, bf16[8,128,2048]{2,1,0:T(8,128)(2,1)}) custom-call(bf16[1024,704]{1,0:T(8,128)(2,1)} %get-tuple-element.335.act, bf16[8,128,128]{2,1,0:T(8,128)(2,1)} %get-tuple-element.336.sact_own, bf16[8,128,128]{2,1,0:T(8,128)(2,1)} %get-tuple-element.337.sact_other, f32[8,128,128]{2,1,0:T(8,128)} %slice.718.meta_own, ...), custom_call_target="tpu_custom_call" | custom-call | flops 268435456 | bytes 2097152 | tf_op jit(solution)/shard_map/pallas_call | solution.py:1158
  499.5 12.2 %all-to-all-done.1 = bf16[266,16,128]{2,0,1:T(8,128)(2,1)S(1)} async-done(((bf16[266,16,128]{2,0,1:T(8,128)(2,1)}), bf16[266,16,128]{2,0,1:T(8,128)(2,1)S(1)}, u32[]{:S(2)}, u32[]{:S(2)}) %all-to-all-start.1) | async-done | bytes 1089568 | tf_op jit(solution)/shard_map/all_to_all | solution.py:1487
  511.8 5.9 fusion.13
  521.4 22.8 %shard_map.271 = f32[2,704,2048]{2,1,0:T(8,128)} custom-call(bf16[2,512,704]{2,1,0:T(8,128)(2,1)} %get-tuple-element.364.refs_0_, bf16[2,1024,704]{2,1,0:T(8,128)(2,1)} %get-tuple-element.365.refs_1_, bf16[2,512,704]{2,1,0:T(8,128)(2,1)} %get-tuple-element.366.refs_2_, bf16[512,2048]{1,0:T(8,128)(2,1)} %get-tuple-element.367.refs_3_, ...), custom_call_target="tpu_custom_call" | custom-call | flops 2048 | bytes 2048 | tf_op jit(solution)/shard_map/pallas_call | solution.py:1126
  551.2 4.6 fusion.12
  561.2 7.8 collective-permute-done.52
  568.9 32.1 %collective-permute-done.53 = bf16[128,2048]{1,0:T(8,128)(2,1)S(1)} collective-permute-done((bf16[128,2048]{1,0:T(8,128)(2,1)S(1)}, bf16[128,2048]{1,0:T(8,128)(2,1)S(1)}, u32[]{:S(2)}, u32[]{:S(2)}) %collective-permute-start.53) | collective-permute-done | bytes 524320 | tf_op jit(solution)/shard_map/ppermute | solution.py:418
  606.0 10.1 %collective-permute-done.57 = bf16[128,2048]{1,0:T(8,128)(2,1)S(1)} collective-permute-done((bf16[128,2048]{1,0:T(8,128)(2,1)S(1)}, bf16[128,2048]{1,0:T(8,128)(2,1)S(1)}, u32[]{:S(2)}, u32[]{:S(2)}) %collective-permute-start.57) | collective-permute-done | bytes 524320 | tf_op jit(solution)/shard_map/ppermute | solution.py:412
  616.1 13.3 %collective-permute-done.56 = bf16[128,2048]{1,0:T(8,128)(2,1)S(1)} collective-permute-done((bf16[128,2048]{1,0:T(8,128)(2,1)S(1)}, bf16[128,2048]{1,0:T(8,128)(2,1)S(1)}, u32[]{:S(2)}, u32[]{:S(2)}) %collective-permute-start.56) | collective-permute-done | bytes 524320 | tf_op jit(solution)/shard_map/ppermute | solution.py:412
  631.4 4.1 fusion.9
  636.8 22.1 %shard_map.272 = (bf16[2048,640]{1,0:T(8,128)(2,1)}, bf16[512,512]{1,0:T(8,128)(2,1)}, bf16[4,128,2048]{2,1,0:T(8,128)(2,1)}, bf16[4,128,2048]{2,1,0:T(8,128)(2,...) custom-call(s32[1]{0:T(128)} %bitcast.core_ref, bf16[4,128,2048]{2,1,0:T(8,128)(2,1)} %copy-done.22, ...), custom_call_target="tpu_custom_call" | custom-call | flops 536870912 | bytes 4194304 | tf_op jit(solution)/shard_map/pallas_call | solution.py:1066
  669.8 3.1 collective-permute-start.61
  676.6 12.3 %collective-permute-done.61 = bf16[512,768]{1,0:T(8,128)(2,1)S(1)} collective-permute-done((bf16[512,768]{1,0:T(8,128)(2,1)S(1)}, bf16[512,768]{1,0:T(8,128)(2,1)S(1)}, u32[]{:S(2)}, u32[]{:S(2)}) %collective-permute-start.61) | collective-permute-done | bytes 786464 | tf_op jit(solution)/shard_map/ppermute | solution.py:529
  693.0 4.7 collective-permute-start.67
  697.8 4.0 fusion.8
  705.0 6.9 collective-permute-done.67
  715.1 5.6 collective-permute-start.73
  729.9 5.1 collective-permute-done.76
  735.0 5.1 collective-permute-start.81
  741.5 6.8 collective-permute-done.81
  748.4 4.1 fusion.41
  753.2 5.3 all-to-all-start.2
  758.5 2.9 fusion.51
  762.9 4.1 collective-permute-start.83
  775.0 5.0 collective-permute-start.85
  803.0 3.5 collective-permute-start.89
  822.5 5.0 collective-permute-start.92
  839.0 4.0 maximum_select_fusion.1
  (668 shorter events, 255.1 us)
Async XLA Ops:
  28.8 21.9 %collective-permute-start.15 = (bf16[4,128,768]{2,1,0:T(8,128)(2,1)}, bf16[4,128,768]{2,1,0:T(8,128)(2,1)}, u32[]{:S(2)}, u32[]{:S(2)}) collective-permute-start(bf16[4,128,768]{2,1,0:T(8,128)(2,1)} %pad_maximum_fusion.15), channel_id=1, source_target_pairs={{8,0},{10,2},{12,4},{14,6},{16,8},{18,10},{20,12},{22,14},{24,16},... | collective-permute-start | bytes 2359304 | tf_op jit(solution)/shard_map/ppermute | solution.py:447
  30.0 21.9 %collective-permute-start.12 = (bf16[4,128,768]{2,1,0:T(8,128)(2,1)}, bf16[4,128,768]{2,1,0:T(8,128)(2,1)}, u32[]{:S(2)}, u32[]{:S(2)}) collective-permute-start(bf16[4,128,768]{2,1,0:T(8,128)(2,1)} %pad_maximum_fusion.15), channel_id=1, source_target_pairs={{0,8},{2,10},{4,12},{6,14},{8,16},{10,18},{12,20},{14,22},{16,24},... | collective-permute-start | bytes 2359304 | tf_op jit(solution)/shard_map/ppermute | solution.py:447
  38.2 19.7 %collective-permute-start.9 = (bf16[2,128,4,384]{3,1,2,0:T(8,128)(2,1)}, bf16[2,128,4,384]{3,1,2,0:T(8,128)(2,1)}, u32[]{:S(2)}, u32[]{:S(2)}) collective-permute-start(bf16[2,128,4,384]{3,1,2,0:T(8,128)(2,1)} %pad_maximum_fusion.16), channel_id=1, source_target_pairs={{0,4},{2,6},{4,0},{6,2},{8,12},{10,14},{12,8},{14,10},{16,20},{18,... | collective-permute-start | bytes 2359304 | tf_op jit(solution)/shard_map/ppermute | solution.py:412
  40.4 24.8 %collective-permute-start.7 = (bf16[2,128,2048]{2,1,0:T(8,128)(2,1)S(1)}, bf16[2,128,2048]{2,1,0:T(8,128)(2,1)S(1)}, u32[]{:S(2)}, u32[]{:S(2)}) collective-permute-start(bf16[2,128,2048]{2,1,0:T(8,128)(2,1)S(1)} %pad_maximum_fusion.13), channel_id=1, source_target_pairs={{0,2},{2,0},{4,6},{6,4},{8,10},{10,8},{12,14},{14,12},{16,18},{18,... | collective-permute-start | bytes 3145736 | tf_op jit(solution)/shard_map/ppermute | solution.py:412
  50.7 20.9 %collective-permute-start.16 = (bf16[4,128,768]{2,1,0:T(8,128)(2,1)}, bf16[4,128,768]{2,1,0:T(8,128)(2,1)}, u32[]{:S(2)}, u32[]{:S(2)}) collective-permute-start(bf16[4,128,768]{2,1,0:T(8,128)(2,1)} %collective-permute-done.15), channel_id=1, source_target_pairs={{8,0},{10,2},{12,4},{14,6},{16,8},{18,10},{20,12},{22,14},{24,16},... | collective-permute-start | bytes 2359304 | tf_op jit(solution)/shard_map/ppermute | solution.py:447
  52.0 20.9 %collective-permute-start.13 = (bf16[4,128,768]{2,1,0:T(8,128)(2,1)}, bf16[4,128,768]{2,1,0:T(8,128)(2,1)}, u32[]{:S(2)}, u32[]{:S(2)}) collective-permute-start(bf16[4,128,768]{2,1,0:T(8,128)(2,1)} %collective-permute-done.12), channel_id=1, source_target_pairs={{0,8},{2,10},{4,12},{6,14},{8,16},{10,18},{12,20},{14,22},{16,24},... | collective-permute-start | bytes 2359304 | tf_op jit(solution)/shard_map/ppermute | solution.py:447
  62.6 24.9 %collective-permute-start.10 = (bf16[16,64,768]{2,1,0:T(8,128)(2,1)}, bf16[16,64,768]{2,1,0:T(8,128)(2,1)}, u32[]{:S(2)}, u32[]{:S(2)}) collective-permute-start(bf16[16,64,768]{2,1,0:T(8,128)(2,1)} %pad_maximum_fusion.9), channel_id=1, source_target_pairs={{0,1},{1,0},{2,3},{3,2},{4,5},{5,4},{6,7},{7,6},{8,9},{9,8},{10,11... | collective-permute-start | bytes 4718600 | tf_op jit(solution)/shard_map/ppermute | solution.py:385
  66.9 28.8 %collective-permute-start.11 = (bf16[4,128,2048]{2,1,0:T(8,128)(2,1)}, bf16[4,128,2048]{2,1,0:T(8,128)(2,1)}, u32[]{:S(2)}, u32[]{:S(2)}) collective-permute-start(bf16[4,128,2048]{2,1,0:T(8,128)(2,1)} %pad_maximum_fusion.x_own), channel_id=1, source_target_pairs={{0,1},{1,0},{2,3},{3,2},{4,5},{5,4},{6,7},{7,6},{8,9},{9,8},{10,11... | collective-permute-start | bytes 6291464 | tf_op jit(solution)/shard_map/ppermute | solution.py:385
  71.6 23.2 %collective-permute-start.17 = (bf16[4,128,768]{2,1,0:T(8,128)(2,1)}, bf16[4,128,768]{2,1,0:T(8,128)(2,1)}, u32[]{:S(2)}, u32[]{:S(2)}) collective-permute-start(bf16[4,128,768]{2,1,0:T(8,128)(2,1)} %collective-permute-done.16), channel_id=1, source_target_pairs={{8,0},{10,2},{12,4},{14,6},{16,8},{18,10},{20,12},{22,14},{24,16},... | collective-permute-start | bytes 2359304 | tf_op jit(solution)/shard_map/ppermute | solution.py:447
  72.9 22.8 %collective-permute-start.14 = (bf16[4,128,768]{2,1,0:T(8,128)(2,1)}, bf16[4,128,768]{2,1,0:T(8,128)(2,1)}, u32[]{:S(2)}, u32[]{:S(2)}) collective-permute-start(bf16[4,128,768]{2,1,0:T(8,128)(2,1)} %collective-permute-done.13), channel_id=1, source_target_pairs={{0,8},{2,10},{4,12},{6,14},{8,16},{10,18},{12,20},{14,22},{16,24},... | collective-permute-start | bytes 2359304 | tf_op jit(solution)/shard_map/ppermute | solution.py:447
  100.4 31.3 %collective-permute-start.20 = (bf16[128,2048]{1,0:T(8,128)(2,1)}, bf16[128,2048]{1,0:T(8,128)(2,1)}, u32[]{:S(2)}, u32[]{:S(2)}) collective-permute-start(bf16[128,2048]{1,0:T(8,128)(2,1)} %constant_dynamic-slice_fusion.34), channel_id=1, source_target_pairs={{0,24},{2,26},{4,28},{6,30},{8,0},{10,2},{12,4},{14,6},{16,8},{18,... | collective-permute-start | bytes 1572872 | tf_op jit(solution)/shard_map/ppermute | solution.py:418
  106.7 43.7 %collective-permute-start.19 = (bf16[128,2048]{1,0:T(8,128)(2,1)}, bf16[128,2048]{1,0:T(8,128)(2,1)}, u32[]{:S(2)}, u32[]{:S(2)}) collective-permute-start(bf16[128,2048]{1,0:T(8,128)(2,1)} %constant_dynamic-slice_fusion.34), channel_id=1, source_target_pairs={{0,16},{2,18},{4,20},{6,22},{8,24},{10,26},{12,28},{14,30},{16,0},... | collective-permute-start | bytes 1572872 | tf_op jit(solution)/shard_map/ppermute | solution.py:418
  106.7 43.7 %collective-permute-start.18 = (bf16[128,2048]{1,0:T(8,128)(2,1)}, bf16[128,2048]{1,0:T(8,128)(2,1)}, u32[]{:S(2)}, u32[]{:S(2)}) collective-permute-start(bf16[128,2048]{1,0:T(8,128)(2,1)} %constant_dynamic-slice_fusion.34), channel_id=1, source_target_pairs={{0,8},{2,10},{4,12},{6,14},{8,16},{10,18},{12,20},{14,22},{16,24},... | collective-permute-start | bytes 1572872 | tf_op jit(solution)/shard_map/ppermute | solution.py:418
  161.5 25.2 %collective-permute-start.24 = (bf16[128,2048]{1,0:T(8,128)(2,1)S(1)}, bf16[128,2048]{1,0:T(8,128)(2,1)S(1)}, u32[]{:S(2)}, u32[]{:S(2)}) collective-permute-start(bf16[128,2048]{1,0:T(8,128)(2,1)S(1)} %get-tuple-element.604), channel_id=1, source_target_pairs={{0,6},{2,4},{4,2},{6,0},{8,14},{10,12},{12,10},{14,8},{16,22},{18,... | collective-permute-start | bytes 1572872 | tf_op jit(solution)/shard_map/ppermute | solution.py:412
  163.3 24.2 %collective-permute-start.23 = (bf16[128,2048]{1,0:T(8,128)(2,1)S(1)}, bf16[128,2048]{1,0:T(8,128)(2,1)S(1)}, u32[]{:S(2)}, u32[]{:S(2)}) collective-permute-start(bf16[128,2048]{1,0:T(8,128)(2,1)S(1)} %get-tuple-element.605), channel_id=1, source_target_pairs={{0,4},{2,6},{4,0},{6,2},{8,12},{10,14},{12,8},{14,10},{16,20},{18,... | collective-permute-start | bytes 1572872 | tf_op jit(solution)/shard_map/ppermute | solution.py:412
  169.1 28.8 %collective-permute-start.30 = (bf16[4,128,2048]{2,1,0:T(8,128)(2,1)}, bf16[4,128,2048]{2,1,0:T(8,128)(2,1)}, u32[]{:S(2)}, u32[]{:S(2)}) collective-permute-start(bf16[4,128,2048]{2,1,0:T(8,128)(2,1)} %pad_maximum_fusion.1.dy_own), channel_id=1, source_target_pairs={{0,1},{1,0},{2,3},{3,2},{4,5},{5,4},{6,7},{7,6},{8,9},{9,8},{10,11... | collective-permute-start | bytes 6291464 | tf_op jit(solution)/shard_map/ppermute | solution.py:385
  169.9 72.7 %collective-permute-start.29 = (bf16[4,128,2048]{2,1,0:T(8,128)(2,1)}, bf16[4,128,2048]{2,1,0:T(8,128)(2,1)}, u32[]{:S(2)}, u32[]{:S(2)}) collective-permute-start(bf16[4,128,2048]{2,1,0:T(8,128)(2,1)} %pad_maximum_fusion.1.dy_own), channel_id=1, source_target_pairs={{0,4},{2,6},{4,0},{6,2},{8,12},{10,14},{12,8},{14,10},{16,20},{18,... | collective-permute-start | bytes 6291464 | tf_op jit(solution)/shard_map/ppermute | solution.py:412
  174.4 68.2 %collective-permute-start.28 = (bf16[4,128,2048]{2,1,0:T(8,128)(2,1)}, bf16[4,128,2048]{2,1,0:T(8,128)(2,1)}, u32[]{:S(2)}, u32[]{:S(2)}) collective-permute-start(bf16[4,128,2048]{2,1,0:T(8,128)(2,1)} %pad_maximum_fusion.1.dy_own), channel_id=1, source_target_pairs={{0,2},{2,0},{4,6},{6,4},{8,10},{10,8},{12,14},{14,12},{16,18},{18,... | collective-permute-start | bytes 6291464 | tf_op jit(solution)/shard_map/ppermute | solution.py:412
  188.3 76.4 %all-to-all-start = ((bf16[16,264,128]{2,1,0:T(8,128)(2,1)}), bf16[16,264,128]{2,1,0:T(8,128)(2,1)}, u32[]{:S(2)}, u32[]{:S(2)}) async-start(bf16[16,264,128]{2,1,0:T(8,128)(2,1)} %bitcast.414), calls=%async_computation | async-start | bytes 2162688 | tf_op jit(solution)/shard_map/all_to_all | solution.py:1398
  193.4 49.2 %collective-permute-start.27 = (bf16[128,2048]{1,0:T(8,128)(2,1)S(1)}, bf16[128,2048]{1,0:T(8,128)(2,1)}, u32[]{:S(2)}, u32[]{:S(2)}) collective-permute-start(bf16[128,2048]{1,0:T(8,128)(2,1)S(1)} %multiply_convert_fusion), channel_id=1, source_target_pairs={{0,24},{2,26},{4,28},{6,30},{8,0},{10,2},{12,4},{14,6},{16,8},{18,... | collective-permute-start | bytes 1572872 | tf_op jit(solution)/shard_map/ppermute | solution.py:418
  196.6 68.2 %collective-permute-start.26 = (bf16[128,2048]{1,0:T(8,128)(2,1)S(1)}, bf16[128,2048]{1,0:T(8,128)(2,1)}, u32[]{:S(2)}, u32[]{:S(2)}) collective-permute-start(bf16[128,2048]{1,0:T(8,128)(2,1)S(1)} %multiply_convert_fusion), channel_id=1, source_target_pairs={{0,16},{2,18},{4,20},{6,22},{8,24},{10,26},{12,28},{14,30},{16,0},... | collective-permute-start | bytes 1572872 | tf_op jit(solution)/shard_map/ppermute | solution.py:418
  197.9 66.9 %collective-permute-start.25 = (bf16[128,2048]{1,0:T(8,128)(2,1)S(1)}, bf16[128,2048]{1,0:T(8,128)(2,1)}, u32[]{:S(2)}, u32[]{:S(2)}) collective-permute-start(bf16[128,2048]{1,0:T(8,128)(2,1)S(1)} %multiply_convert_fusion), channel_id=1, source_target_pairs={{0,8},{2,10},{4,12},{6,14},{8,16},{10,18},{12,20},{14,22},{16,24},... | collective-permute-start | bytes 1572872 | tf_op jit(solution)/shard_map/ppermute | solution.py:418
  274.0 50.2 %collective-permute-start.34 = (bf16[8,128,2048]{2,1,0:T(8,128)(2,1)}, bf16[8,128,2048]{2,1,0:T(8,128)(2,1)}, u32[]{:S(2)}, u32[]{:S(2)}) collective-permute-start(bf16[8,128,2048]{2,1,0:T(8,128)(2,1)} %constant_dynamic-update-slice_fusion.1.dy_own), channel_id=1, source_target_pairs={{0,1},{1,0},{2,3},{3,2},{4,5},{5,4},{6,7},{7,6},{8,9},{9,8},{10,11... | collective-permute-start | bytes 12582920 | tf_op jit(solution)/shard_map/ppermute | solution.py:385
  276.5 47.2 %collective-permute-start.32 = (bf16[4,128,2048]{2,1,0:T(8,128)(2,1)}, bf16[4,128,2048]{2,1,0:T(8,128)(2,1)S(1)}, u32[]{:S(2)}, u32[]{:S(2)}) collective-permute-start(bf16[4,128,2048]{2,1,0:T(8,128)(2,1)} %pad_maximum_fusion.2.hn_own), channel_id=1, source_target_pairs={{0,4},{2,6},{4,0},{6,2},{8,12},{10,14},{12,8},{14,10},{16,20},{18,... | collective-permute-start | bytes 6291464 | tf_op jit(solution)/shard_map/ppermute | solution.py:412
  277.4 46.8 %collective-permute-start.31 = (bf16[4,128,2048]{2,1,0:T(8,128)(2,1)}, bf16[4,128,2048]{2,1,0:T(8,128)(2,1)}, u32[]{:S(2)}, u32[]{:S(2)}) collective-permute-start(bf16[4,128,2048]{2,1,0:T(8,128)(2,1)} %pad_maximum_fusion.2.hn_own), channel_id=1, source_target_pairs={{0,2},{2,0},{4,6},{6,4},{8,10},{10,8},{12,14},{14,12},{16,18},{18,... | collective-permute-start | bytes 6291464 | tf_op jit(solution)/shard_map/ppermute | solution.py:412
  328.1 14.4 %collective-permute-start.40 = (bf16[8,128,2048]{2,1,0:T(8,128)(2,1)S(1)}, bf16[8,128,2048]{2,1,0:T(8,128)(2,1)}, u32[]{:S(2)}, u32[]{:S(2)}) collective-permute-start(bf16[8,128,2048]{2,1,0:T(8,128)(2,1)S(1)} %constant_dynamic-update-slice_fusion.3.hn_own), channel_id=1, source_target_pairs={{0,1},{1,0},{2,3},{3,2},{4,5},{5,4},{6,7},{7,6},{8,9},{9,8},{10,11... | collective-permute-start | bytes 12582920 | tf_op jit(solution)/shard_map/ppermute | solution.py:385
  337.9 50.3 %collective-permute-start.37 = (bf16[4,64,2048]{2,1,0:T(8,128)(2,1)}, bf16[4,64,2048]{2,1,0:T(8,128)(2,1)S(1)}, u32[]{:S(2)}, u32[]{:S(2)}) collective-permute-start(bf16[4,64,2048]{2,1,0:T(8,128)(2,1)} %slice.715), channel_id=1, source_target_pairs={{0,2},{2,0},{4,6},{6,4},{8,10},{10,8},{12,14},{14,12},{16,18},{18,... | collective-permute-start | bytes 3145736 | tf_op jit(solution)/shard_map/ppermute | solution.py:412
  339.1 49.1 %collective-permute-start.36 = (bf16[4,64,2048]{2,1,0:T(8,128)(2,1)}, bf16[4,64,2048]{2,1,0:T(8,128)(2,1)S(1)}, u32[]{:S(2)}, u32[]{:S(2)}) collective-permute-start(bf16[4,64,2048]{2,1,0:T(8,128)(2,1)} %slice.714), channel_id=1, source_target_pairs={{0,4},{2,6},{4,0},{6,2},{8,12},{10,14},{12,8},{14,10},{16,20},{18,... | collective-permute-start | bytes 3145736 | tf_op jit(solution)/shard_map/ppermute | solution.py:412
  339.4 48.8 %collective-permute-start.39 = (bf16[4,64,2048]{2,1,0:T(8,128)(2,1)}, bf16[4,64,2048]{2,1,0:T(8,128)(2,1)}, u32[]{:S(2)}, u32[]{:S(2)}) collective-permute-start(bf16[4,64,2048]{2,1,0:T(8,128)(2,1)} %slice.717), channel_id=1, source_target_pairs={{0,2},{2,0},{4,6},{6,4},{8,10},{10,8},{12,14},{14,12},{16,18},{18,... | collective-permute-start | bytes 3145736 | tf_op jit(solution)/shard_map/ppermute | solution.py:412
  340.0 48.2 %collective-permute-start.38 = (bf16[4,64,2048]{2,1,0:T(8,128)(2,1)}, bf16[4,64,2048]{2,1,0:T(8,128)(2,1)}, u32[]{:S(2)}, u32[]{:S(2)}) collective-permute-start(bf16[4,64,2048]{2,1,0:T(8,128)(2,1)} %slice.716), channel_id=1, source_target_pairs={{0,4},{2,6},{4,0},{6,2},{8,12},{10,14},{12,8},{14,10},{16,20},{18,... | collective-permute-start | bytes 3145736 | tf_op jit(solution)/shard_map/ppermute | solution.py:412
  390.9 51.0 %collective-permute-start.41 = (bf16[8,128,2048]{2,1,0:T(8,128)(2,1)}, bf16[8,128,2048]{2,1,0:T(8,128)(2,1)}, u32[]{:S(2)}, u32[]{:S(2)}) collective-permute-start(bf16[8,128,2048]{2,1,0:T(8,128)(2,1)} %get-tuple-element.304), channel_id=1, source_target_pairs={{0,1},{1,0},{2,3},{3,2},{4,5},{5,4},{6,7},{7,6},{8,9},{9,8},{10,11... | collective-permute-start | bytes 12582920 | tf_op jit(solution)/shard_map/ppermute | solution.py:385
  394.9 49.9 %collective-permute-start.35 = (bf16[4,128,2048]{2,1,0:T(8,128)(2,1)}, bf16[4,128,2048]{2,1,0:T(8,128)(2,1)}, u32[]{:S(2)}, u32[]{:S(2)}) collective-permute-start(bf16[4,128,2048]{2,1,0:T(8,128)(2,1)} %get-tuple-element.286), channel_id=1, source_target_pairs={{0,1},{1,0},{2,3},{3,2},{4,5},{5,4},{6,7},{7,6},{8,9},{9,8},{10,11... | collective-permute-start | bytes 6291464 | tf_op jit(solution)/shard_map/ppermute | solution.py:385
  452.4 59.4 %collective-permute-start.46 = (bf16[2,4,64,2048]{3,2,1,0:T(8,128)(2,1)}, bf16[2,4,64,2048]{3,2,1,0:T(8,128)(2,1)}, u32[]{:S(2)}, u32[]{:S(2)}) collective-permute-start(bf16[2,4,64,2048]{3,2,1,0:T(8,128)(2,1)} %pad_maximum_fusion.3), channel_id=1, source_target_pairs={{0,4},{2,6},{4,0},{6,2},{8,12},{10,14},{12,8},{14,10},{16,20},{18,... | collective-permute-start | bytes 6291464 | tf_op jit(solution)/shard_map/ppermute | solution.py:412
  453.0 58.7 %collective-permute-start.47 = (bf16[2,4,64,2048]{3,2,1,0:T(8,128)(2,1)}, bf16[2,4,64,2048]{3,2,1,0:T(8,128)(2,1)}, u32[]{:S(2)}, u32[]{:S(2)}) collective-permute-start(bf16[2,4,64,2048]{3,2,1,0:T(8,128)(2,1)} %pad_maximum_fusion.4), channel_id=1, source_target_pairs={{0,2},{2,0},{4,6},{6,4},{8,10},{10,8},{12,14},{14,12},{16,18},{18,... | collective-permute-start | bytes 6291464 | tf_op jit(solution)/shard_map/ppermute | solution.py:412
  455.0 56.7 %all-to-all-start.1 = ((bf16[266,16,128]{2,0,1:T(8,128)(2,1)}), bf16[266,16,128]{2,0,1:T(8,128)(2,1)S(1)}, u32[]{:S(2)}, u32[]{:S(2)}) async-start(bf16[266,16,128]{2,0,1:T(8,128)(2,1)} %pad_maximum_fusion.11), calls=%async_computation.1 | async-start | bytes 2228224 | tf_op jit(solution)/shard_map/all_to_all | solution.py:1487
  517.7 28.8 %collective-permute-start.50 = (bf16[8,128,2048]{2,1,0:T(8,128)(2,1)}, bf16[8,128,2048]{2,1,0:T(8,128)(2,1)}, u32[]{:S(2)}, u32[]{:S(2)}) collective-permute-start(bf16[8,128,2048]{2,1,0:T(8,128)(2,1)} %get-tuple-element.371), channel_id=1, source_target_pairs={{0,1},{1,0},{2,3},{3,2},{4,5},{5,4},{6,7},{7,6},{8,9},{9,8},{10,11... | collective-permute-start | bytes 12582920 | tf_op jit(solution)/shard_map/ppermute | solution.py:385
  519.2 25.3 %collective-permute-start.51 = (bf16[4,128,2048]{2,1,0:T(8,128)(2,1)}, bf16[4,128,2048]{2,1,0:T(8,128)(2,1)S(1)}, u32[]{:S(2)}, u32[]{:S(2)}) collective-permute-start(bf16[4,128,2048]{2,1,0:T(8,128)(2,1)} %get-tuple-element.373), channel_id=1, source_target_pairs={{0,1},{1,0},{2,3},{3,2},{4,5},{5,4},{6,7},{7,6},{8,9},{9,8},{10,11... | collective-permute-start | bytes 6291464 | tf_op jit(solution)/shard_map/ppermute | solution.py:385
  519.2 30.6 %collective-permute-start.48 = (bf16[4,64,2048]{2,1,0:T(8,128)(2,1)}, bf16[4,64,2048]{2,1,0:T(8,128)(2,1)}, u32[]{:S(2)}, u32[]{:S(2)}) collective-permute-start(bf16[4,64,2048]{2,1,0:T(8,128)(2,1)} %get-tuple-element.362), channel_id=1, source_target_pairs={{0,2},{2,0},{4,6},{6,4},{8,10},{10,8},{12,14},{14,12},{16,18},{18,... | collective-permute-start | bytes 3145736 | tf_op jit(solution)/shard_map/ppermute | solution.py:412
  521.1 28.7 %collective-permute-start.49 = (bf16[4,64,2048]{2,1,0:T(8,128)(2,1)}, bf16[4,64,2048]{2,1,0:T(8,128)(2,1)}, u32[]{:S(2)}, u32[]{:S(2)}) collective-permute-start(bf16[4,64,2048]{2,1,0:T(8,128)(2,1)} %get-tuple-element.363), channel_id=1, source_target_pairs={{0,4},{2,6},{4,0},{6,2},{8,12},{10,14},{12,8},{14,10},{16,20},{18,... | collective-permute-start | bytes 3145736 | tf_op jit(solution)/shard_map/ppermute | solution.py:412
  556.0 45.1 %collective-permute-start.53 = (bf16[128,2048]{1,0:T(8,128)(2,1)S(1)}, bf16[128,2048]{1,0:T(8,128)(2,1)S(1)}, u32[]{:S(2)}, u32[]{:S(2)}) collective-permute-start(bf16[128,2048]{1,0:T(8,128)(2,1)S(1)} %get-tuple-element.381), channel_id=1, source_target_pairs={{0,16},{2,18},{4,20},{6,22},{8,24},{10,26},{12,28},{14,30},{16,0},... | collective-permute-start | bytes 1572872 | tf_op jit(solution)/shard_map/ppermute | solution.py:418
  556.2 44.8 %collective-permute-start.54 = (bf16[128,2048]{1,0:T(8,128)(2,1)S(1)}, bf16[128,2048]{1,0:T(8,128)(2,1)S(1)}, u32[]{:S(2)}, u32[]{:S(2)}) collective-permute-start(bf16[128,2048]{1,0:T(8,128)(2,1)S(1)} %get-tuple-element.382), channel_id=1, source_target_pairs={{0,8},{2,10},{4,12},{6,14},{8,16},{10,18},{12,20},{14,22},{16,24},... | collective-permute-start | bytes 1572872 | tf_op jit(solution)/shard_map/ppermute | solution.py:418
  557.6 71.7 %collective-permute-start.58 = (bf16[2,4,64,2048]{3,2,1,0:T(8,128)(2,1)S(1)}, bf16[2,4,64,2048]{3,2,1,0:T(8,128)(2,1)S(1)}, u32[]{:S(2)}, u32[]{:S(2)}) collective-permute-start(bf16[2,4,64,2048]{3,2,1,0:T(8,128)(2,1)S(1)} %pad_maximum_fusion.5), channel_id=1, source_target_pairs={{0,4},{2,6},{4,0},{6,2},{8,12},{10,14},{12,8},{14,10},{16,20},{18,... | collective-permute-start | bytes 6291464 | tf_op jit(solution)/shard_map/ppermute | solution.py:412
  558.9 70.5 %collective-permute-start.59 = (bf16[2,4,64,2048]{3,2,1,0:T(8,128)(2,1)S(1)}, bf16[2,4,64,2048]{3,2,1,0:T(8,128)(2,1)S(1)}, u32[]{:S(2)}, u32[]{:S(2)}) collective-permute-start(bf16[2,4,64,2048]{3,2,1,0:T(8,128)(2,1)S(1)} %pad_maximum_fusion.6), channel_id=1, source_target_pairs={{0,2},{2,0},{4,6},{6,4},{8,10},{10,8},{12,14},{14,12},{16,18},{18,... | collective-permute-start | bytes 6291464 | tf_op jit(solution)/shard_map/ppermute | solution.py:412
  604.7 24.6 %collective-permute-start.56 = (bf16[128,2048]{1,0:T(8,128)(2,1)S(1)}, bf16[128,2048]{1,0:T(8,128)(2,1)S(1)}, u32[]{:S(2)}, u32[]{:S(2)}) collective-permute-start(bf16[128,2048]{1,0:T(8,128)(2,1)S(1)} %fusion.117), channel_id=1, source_target_pairs={{0,4},{2,6},{4,0},{6,2},{8,12},{10,14},{12,8},{14,10},{16,20},{18,... | collective-permute-start | bytes 1572872 | tf_op jit(solution)/shard_map/ppermute | solution.py:412
  604.9 24.5 %collective-permute-start.55 = (bf16[128,2048]{1,0:T(8,128)(2,1)S(1)}, bf16[128,2048]{1,0:T(8,128)(2,1)S(1)}, u32[]{:S(2)}, u32[]{:S(2)}) collective-permute-start(bf16[128,2048]{1,0:T(8,128)(2,1)S(1)} %fusion.117), channel_id=1, source_target_pairs={{0,2},{2,0},{4,6},{6,4},{8,10},{10,8},{12,14},{14,12},{16,18},{18,... | collective-permute-start | bytes 1572872 | tf_op jit(solution)/shard_map/ppermute | solution.py:412
  661.8 31.2 %collective-permute-start.72 = (bf16[4,128,2048]{2,1,0:T(8,128)(2,1)}, bf16[4,128,2048]{2,1,0:T(8,128)(2,1)}, u32[]{:S(2)}, u32[]{:S(2)}) collective-permute-start(bf16[4,128,2048]{2,1,0:T(8,128)(2,1)} %get-tuple-element.416), channel_id=1, source_target_pairs={{0,1},{1,0},{2,3},{3,2},{4,5},{5,4},{6,7},{7,6},{8,9},{9,8},{10,11... | collective-permute-start | bytes 6291464 | tf_op jit(solution)/shard_map/ppermute | solution.py:385
  662.5 26.3 %collective-permute-start.65 = (bf16[4,64,2048]{2,1,0:T(8,128)(2,1)}, bf16[4,64,2048]{2,1,0:T(8,128)(2,1)}, u32[]{:S(2)}, u32[]{:S(2)}) collective-permute-start(bf16[4,64,2048]{2,1,0:T(8,128)(2,1)} %get-tuple-element.410), channel_id=1, source_target_pairs={{0,2},{2,0},{4,6},{6,4},{8,10},{10,8},{12,14},{14,12},{16,18},{18,... | collective-permute-start | bytes 3145736 | tf_op jit(solution)/shard_map/ppermute | solution.py:412
  663.0 25.9 %collective-permute-start.66 = (bf16[4,64,2048]{2,1,0:T(8,128)(2,1)}, bf16[4,64,2048]{2,1,0:T(8,128)(2,1)}, u32[]{:S(2)}, u32[]{:S(2)}) collective-permute-start(bf16[4,64,2048]{2,1,0:T(8,128)(2,1)} %get-tuple-element.411), channel_id=1, source_target_pairs={{0,4},{2,6},{4,0},{6,2},{8,12},{10,14},{12,8},{14,10},{16,20},{18,... | collective-permute-start | bytes 3145736 | tf_op jit(solution)/shard_map/ppermute | solution.py:412
  669.8 19.0 %collective-permute-start.61 = (bf16[512,768]{1,0:T(8,128)(2,1)S(1)}, bf16[512,768]{1,0:T(8,128)(2,1)S(1)}, u32[]{:S(2)}, u32[]{:S(2)}) collective-permute-start(bf16[512,768]{1,0:T(8,128)(2,1)S(1)} %get-tuple-element.587), channel_id=1, source_target_pairs={{0,8},{2,10},{4,12},{6,14},{1,9},{3,11},{5,13},{7,15}} | collective-permute-start | bytes 2359304 | tf_op jit(solution)/shard_map/ppermute | solution.py:529
  693.0 18.9 %collective-permute-start.67 = (bf16[512,768]{1,0:T(8,128)(2,1)S(1)}, bf16[512,768]{1,0:T(8,128)(2,1)S(1)}, u32[]{:S(2)}, u32[]{:S(2)}) collective-permute-start(bf16[512,768]{1,0:T(8,128)(2,1)S(1)} %get-tuple-element.585), channel_id=1, source_target_pairs={{0,8},{2,10},{4,12},{6,14},{8,16},{10,18},{12,20},{14,22},{1,9},{3... | collective-permute-start | bytes 2359304 | tf_op jit(solution)/shard_map/ppermute | solution.py:529
  702.2 19.1 %collective-permute-start.78 = (bf16[128,2048]{1,0:T(8,128)(2,1)S(1)}, bf16[128,2048]{1,0:T(8,128)(2,1)S(1)}, u32[]{:S(2)}, u32[]{:S(2)}) collective-permute-start(bf16[128,2048]{1,0:T(8,128)(2,1)S(1)} %get-tuple-element.596), channel_id=1, source_target_pairs={{0,2},{2,0},{4,6},{6,4},{8,10},{10,8},{12,14},{14,12},{16,18},{18,... | collective-permute-start | bytes 1572872 | tf_op jit(solution)/shard_map/ppermute | solution.py:412
  703.1 21.4 %collective-permute-start.80 = (bf16[128,2048]{1,0:T(8,128)(2,1)S(1)}, bf16[128,2048]{1,0:T(8,128)(2,1)S(1)}, u32[]{:S(2)}, u32[]{:S(2)}) collective-permute-start(bf16[128,2048]{1,0:T(8,128)(2,1)S(1)} %get-tuple-element.597), channel_id=1, source_target_pairs={{0,6},{2,4},{4,2},{6,0},{8,14},{10,12},{12,10},{14,8},{16,22},{18,... | collective-permute-start | bytes 1572872 | tf_op jit(solution)/shard_map/ppermute | solution.py:412
  704.0 22.3 %collective-permute-start.79 = (bf16[128,2048]{1,0:T(8,128)(2,1)S(1)}, bf16[128,2048]{1,0:T(8,128)(2,1)S(1)}, u32[]{:S(2)}, u32[]{:S(2)}) collective-permute-start(bf16[128,2048]{1,0:T(8,128)(2,1)S(1)} %get-tuple-element.598), channel_id=1, source_target_pairs={{0,4},{2,6},{4,0},{6,2},{8,12},{10,14},{12,8},{14,10},{16,20},{18,... | collective-permute-start | bytes 1572872 | tf_op jit(solution)/shard_map/ppermute | solution.py:412
  713.8 34.5 %collective-permute-start.74 = (bf16[512,768]{1,0:T(8,128)(2,1)}, bf16[512,768]{1,0:T(8,128)(2,1)}, u32[]{:S(2)}, u32[]{:S(2)}) collective-permute-start(bf16[512,768]{1,0:T(8,128)(2,1)} %get-tuple-element.582), channel_id=1, source_target_pairs={{8,0},{10,2},{12,4},{14,6},{16,8},{18,10},{20,12},{22,14},{24,16},... | collective-permute-start | bytes 2359304 | tf_op jit(solution)/shard_map/ppermute | solution.py:529
  715.1 33.2 %collective-permute-start.73 = (bf16[512,768]{1,0:T(8,128)(2,1)}, bf16[512,768]{1,0:T(8,128)(2,1)}, u32[]{:S(2)}, u32[]{:S(2)}) collective-permute-start(bf16[512,768]{1,0:T(8,128)(2,1)} %get-tuple-element.583), channel_id=1, source_target_pairs={{0,8},{2,10},{4,12},{6,14},{8,16},{10,18},{12,20},{14,22},{16,24},... | collective-permute-start | bytes 2359304 | tf_op jit(solution)/shard_map/ppermute | solution.py:529
  726.3 15.2 %collective-permute-start.75 = (bf16[128,576]{1,0:T(8,128)(2,1)S(1)}, bf16[128,576]{1,0:T(8,128)(2,1)S(1)}, u32[]{:S(2)}, u32[]{:S(2)}) collective-permute-start(bf16[128,576]{1,0:T(8,128)(2,1)S(1)} %pad_maximum_fusion.22), channel_id=1, source_target_pairs={{0,2},{2,0},{4,6},{6,4},{8,10},{10,8},{12,14},{14,12},{16,18},{18,... | collective-permute-start | bytes 442376 | tf_op jit(solution)/shard_map/ppermute | solution.py:412
  753.2 20.8 %all-to-all-start.2 = ((f32[19,16,128]{2,0,1:T(8,128)}), f32[19,16,128]{2,0,1:T(8,128)S(1)}, u32[]{:S(2)}, u32[]{:S(2)}) async-start(f32[19,16,128]{2,0,1:T(8,128)} %pad_maximum_fusion.21), calls=%async_computation.2 | async-start | bytes 393216 | tf_op jit(solution)/shard_map/all_to_all | solution.py:1642
  761.4 27.5 %collective-permute-start.84 = (bf16[128,2048]{1,0:T(8,128)(2,1)}, bf16[128,2048]{1,0:T(8,128)(2,1)}, u32[]{:S(2)}, u32[]{:S(2)}) collective-permute-start(bf16[128,2048]{1,0:T(8,128)(2,1)} %get-tuple-element.592), channel_id=1, source_target_pairs={{16,8},{18,10},{20,12},{22,14},{24,16},{26,18},{28,20},{30,22},{17... | collective-permute-start | bytes 1572872 | tf_op jit(solution)/shard_map/ppermute | solution.py:529
  762.9 26.0 %collective-permute-start.83 = (bf16[128,2048]{1,0:T(8,128)(2,1)}, bf16[128,2048]{1,0:T(8,128)(2,1)}, u32[]{:S(2)}, u32[]{:S(2)}) collective-permute-start(bf16[128,2048]{1,0:T(8,128)(2,1)} %get-tuple-element.593), channel_id=1, source_target_pairs={{0,8},{2,10},{4,12},{6,14},{8,16},{10,18},{12,20},{14,22},{1,9},{3... | collective-permute-start | bytes 1572872 | tf_op jit(solution)/shard_map/ppermute | solution.py:529
  803.0 14.7 %collective-permute-start.89 = (bf16[128,2048]{1,0:T(8,128)(2,1)S(1)}, bf16[128,2048]{1,0:T(8,128)(2,1)S(1)}, u32[]{:S(2)}, u32[]{:S(2)}) collective-permute-start(bf16[128,2048]{1,0:T(8,128)(2,1)S(1)} %get-tuple-element.590), channel_id=1, source_target_pairs={{0,8},{2,10},{4,12},{6,14},{8,16},{10,18},{12,20},{14,22},{16,24},... | collective-permute-start | bytes 1572872 | tf_op jit(solution)/shard_map/ppermute | solution.py:529
  812.6 20.9 %collective-permute-start.96 = (bf16[128,288]{0,1:T(8,128)(2,1)}, bf16[128,288]{0,1:T(8,128)(2,1)}, u32[]{:S(2)}, u32[]{:S(2)}) collective-permute-start(bf16[128,288]{0,1:T(8,128)(2,1)} %bitcast.376), channel_id=1, source_target_pairs={{0,24},{2,26},{4,28},{6,30},{8,0},{10,2},{12,4},{14,6},{16,8},{18,... | collective-permute-start | bytes 221192 | tf_op jit(solution)/shard_map/ppermute | solution.py:418
  815.3 18.2 %collective-permute-start.94 = (bf16[128,288]{0,1:T(8,128)(2,1)}, bf16[128,288]{0,1:T(8,128)(2,1)}, u32[]{:S(2)}, u32[]{:S(2)}) collective-permute-start(bf16[128,288]{0,1:T(8,128)(2,1)} %bitcast.378), channel_id=1, source_target_pairs={{0,8},{2,10},{4,12},{6,14},{8,16},{10,18},{12,20},{14,22},{16,24},... | collective-permute-start | bytes 221192 | tf_op jit(solution)/shard_map/ppermute | solution.py:418
  815.4 18.2 %collective-permute-start.95 = (bf16[128,288]{0,1:T(8,128)(2,1)}, bf16[128,288]{0,1:T(8,128)(2,1)}, u32[]{:S(2)}, u32[]{:S(2)}) collective-permute-start(bf16[128,288]{0,1:T(8,128)(2,1)} %bitcast.377), channel_id=1, source_target_pairs={{0,16},{2,18},{4,20},{6,22},{8,24},{10,26},{12,28},{14,30},{16,0},... | collective-permute-start | bytes 221192 | tf_op jit(solution)/shard_map/ppermute | solution.py:418
  822.5 16.5 %collective-permute-start.92 = (f32[128,2048]{1,0:T(8,128)}, f32[128,2048]{1,0:T(8,128)}, u32[]{:S(2)}, u32[]{:S(2)}) collective-permute-start(f32[128,2048]{1,0:T(8,128)} %get-tuple-element.619), channel_id=1, source_target_pairs={{0,1},{1,0},{2,3},{3,2},{4,5},{5,4},{6,7},{7,6},{8,9},{9,8},{10,11... | collective-permute-start | bytes 3145736 | tf_op jit(solution)/shard_map/ppermute | solution.py:385
  (150 other events, 2315.9 us)

commit v2 on v1

--- a/solution.py
+++ b/solution.py
@@ -1575,8 +1575,13 @@
     latent_near_own = jnp.stack(latent_parts)
     latent_near = in_order(core, latent_near_own, swap_cores(latent_near_own), axis=1)
     head_sums = head_hops.total(came).astype(bf16).reshape(PLANE, block_rows, -1)
-    out_z, latent_near, head_shared, grads_came = tie(
-        out_hops.hop(2, out_z), latent_near, share_columns(head_sums, place), grads_came
+    out_z, latent_near, head_shared, grads_came, grad_normed, grad_latent = tie(
+        out_hops.hop(2, out_z),
+        latent_near,
+        share_columns(head_sums, place),
+        grads_came,
+        grad_normed,
+        grad_latent,
     )
     out_z = out_hops.hop(3, out_z)
     latent_cut = latent_cols // 2

time: 853 us -> 875 us (1.026)
  local copies, waits for them, and re-layouts: 106 us -> 119 us
  waiting for transfers between devices: 249 us -> 258 us
  transfers between devices with their start and end apart: 101 -> 101, of which waited for: 30 -> 32; matrix products, arithmetic and copies ran while one was open for 17% -> 18% of each run, Pallas kernels for 22% -> 21%
where the time goes in v2:
time: 875 us; the launch traced here: 866 us
  waiting for transfers between devices  258 us (29%)
  Pallas kernels  204 us (23%)
  starting transfers between devices  156 us (18%)
  local copies, waits for them, and re-layouts  119 us (14%)
  other arithmetic  114 us (13%)
  matrix products  12 us (1%)
    pallas_call x3, Pallas kernels, experts(): pl.pallas_call(functools.partial(expert_kernel, shared_cols, expert_count...  100 us
    ppermute x41, waiting for transfers between devices, to_partner(): lax.ppermute(value, 'expert', [(g, g ^ flips) for g in range(groups)])  97.8 us
    ppermute x15, waiting for transfers between devices, to_deeper(): return lax.ppermute(value, 'expert', pairs)  89.3 us
    unnamed x269, local copies, waits for them, and re-layouts  49.3 us
    ppermute x41, starting transfers between devices, to_partner(): lax.ppermute(value, 'expert', [(g, g ^ flips) for g in range(groups)])  35.1 us
    pallas_call x2, Pallas kernels, column_products(): pl.pallas_call(product_kernel, grid=(width // tile, count), in_specs=[*[p...  33.9 us
    ppermute x12, starting transfers between devices, hop(): arrived.append(lax.ppermute(gone, 'expert', pairs))  33.7 us
    ppermute x12, waiting for transfers between devices, hop(): arrived.append(lax.ppermute(gone, 'expert', pairs))  29.5 us
  transfers between devices with their start and end apart: 101, of which 32 were waited for; matrix products, arithmetic and copies ran while one was open for 18% of the time, Pallas kernels for 21%

profile of v2, /device:TPU:1, one launch (start us, length us, event | category | flops | bytes accessed | tf_op | source)
XLA Modules:
  0.0 865.7 jit_solution(5935534984053080438)
XLA Ops:
  7.7 3.1 collective-permute-start.4
  21.5 3.7 collective-permute-done.2
  30.0 7.2 collective-permute-start.12
  41.9 8.7 %collective-permute-done.15 = bf16[4,128,768]{2,1,0:T(8,128)(2,1)} collective-permute-done((bf16[4,128,768]{2,1,0:T(8,128)(2,1)}, bf16[4,128,768]{2,1,0:T(8,128)(2,1)}, u32[]{:S(2)}, u32[]{:S(2)}) %collective-permute-start.15) | collective-permute-done | bytes 786464 | tf_op jit(solution)/shard_map/ppermute | solution.py:447
  52.0 5.6 collective-permute-start.13
  68.4 3.1 fusion.88
  72.9 6.8 collective-permute-start.14
  81.3 3.4 pad_maximum_fusion.19.cosine
  90.1 4.7 collective-permute-done.17
  100.4 6.3 collective-permute-start.20
  113.3 18.3 %shard_map.263 = (bf16[4,256,2048]{2,1,0:T(8,128)(2,1)}, bf16[4,256,512]{2,1,0:T(8,128)(2,1)}, bf16[4,256,384]{2,1,0:T(8,128)(2,1)}, bf16[4,256,512]{2,1,0:T(8,1...) custom-call(s32[1]{0:T(128)} %bitcast.core_ref, ...), custom_call_target="tpu_custom_call" | custom-call | flops 5368709120 | bytes 8388608 | tf_op jit(solution)/shard_map/pallas_call | solution.py:1023
  131.7 18.8 %collective-permute-done.19 = bf16[128,2048]{1,0:T(8,128)(2,1)} collective-permute-done((bf16[128,2048]{1,0:T(8,128)(2,1)}, bf16[128,2048]{1,0:T(8,128)(2,1)}, u32[]{:S(2)}, u32[]{:S(2)}) %collective-permute-start.19) | collective-permute-done | bytes 524320 | tf_op jit(solution)/shard_map/ppermute | solution.py:418
  157.7 3.0 add_convert_fusion.1
  165.9 3.2 pad_maximum_fusion.1.dy_own
  171.2 3.3 collective-permute-done.22
  175.0 11.7 %collective-permute-done.24 = bf16[128,2048]{1,0:T(8,128)(2,1)S(1)} collective-permute-done((bf16[128,2048]{1,0:T(8,128)(2,1)S(1)}, bf16[128,2048]{1,0:T(8,128)(2,1)S(1)}, u32[]{:S(2)}, u32[]{:S(2)}) %collective-permute-start.24) | collective-permute-done | bytes 524320 | tf_op jit(solution)/shard_map/ppermute | solution.py:412
  188.3 5.0 all-to-all-start
  193.4 3.1 collective-permute-start.27
  204.4 3.8 maximum_maximum_fusion.1
  208.2 34.5 %collective-permute-done.29 = bf16[4,128,2048]{2,1,0:T(8,128)(2,1)} collective-permute-done((bf16[4,128,2048]{2,1,0:T(8,128)(2,1)}, bf16[4,128,2048]{2,1,0:T(8,128)(2,1)}, u32[]{:S(2)}, u32[]{:S(2)}) %collective-permute-start.29) | collective-permute-done | bytes 2097184 | tf_op jit(solution)/shard_map/ppermute | solution.py:412
  242.6 22.1 %collective-permute-done.26 = bf16[128,2048]{1,0:T(8,128)(2,1)} collective-permute-done((bf16[128,2048]{1,0:T(8,128)(2,1)S(1)}, bf16[128,2048]{1,0:T(8,128)(2,1)}, u32[]{:S(2)}, u32[]{:S(2)}) %collective-permute-start.26) | collective-permute-done | bytes 524320 | tf_op jit(solution)/shard_map/ppermute | solution.py:418
  267.7 3.2 constant_dynamic-update-slice_fusion.2
  270.9 3.2 constant_dynamic-update-slice_fusion.1.dy_own
  285.4 27.1 %shard_map.264 = (bf16[512,2048]{1,0:T(8,128)(2,1)}, bf16[512,2048]{1,0:T(8,128)(2,1)}, bf16[512,704]{1,0:T(8,128)(2,1)}, bf16[2,512,704]{2,1,0:T(8,128)(2,1)}, ...) custom-call(s32[1]{0:T(128)} %bitcast.68.me_ref, ...), custom_call_target="tpu_custom_call" | custom-call | flops 8192 | bytes 8192 | tf_op jit(solution)/shard_map/pallas_call | solution.py:777
  312.5 11.2 %collective-permute-done.32 = bf16[4,128,2048]{2,1,0:T(8,128)(2,1)S(1)} collective-permute-done((bf16[4,128,2048]{2,1,0:T(8,128)(2,1)}, bf16[4,128,2048]{2,1,0:T(8,128)(2,1)S(1)}, u32[]{:S(2)}, u32[]{:S(2)}) %collective-permute-start.32) | collective-permute-done | bytes 2097184 | tf_op jit(solution)/shard_map/ppermute | solution.py:412
  342.5 45.6 %shard_map.265 = (bf16[1024,2048]{1,0:T(8,128)(2,1)}, bf16[1024,2048]{1,0:T(8,128)(2,1)}, bf16[1024,704]{1,0:T(8,128)(2,1)}, bf16[2,1024,704]{2,1,0:T(8,128)(2,1...) custom-call(s32[1]{0:T(128)} %bitcast.68.me_ref, ...), custom_call_target="tpu_custom_call" | custom-call | flops 16384 | bytes 16384 | tf_op jit(solution)/shard_map/pallas_call | solution.py:777
  395.8 9.1 %collective-permute-done.43.dy_other = bf16[4,128,2048]{2,1,0:T(8,128)(2,1)S(1)} collective-permute-done((bf16[4,128,2048]{2,1,0:T(8,128)(2,1)S(1)}, bf16[4,128,2048]{2,1,0:T(8,128)(2,1)S(1)}, u32[]{:S(2)}, u32[]{:S(2)}) %collective-permute-start.43) | collective-permute-done | bytes 2097184 | tf_op jit(solution)/shard_map/ppermute | solution.py:385
  404.8 3.0 collective-permute-done.42.hn_other
  409.2 27.5 %shard_map.266 = (bf16[512,2048]{1,0:T(8,128)(2,1)}, bf16[512,2048]{1,0:T(8,128)(2,1)}, bf16[512,704]{1,0:T(8,128)(2,1)}, bf16[2,512,704]{2,1,0:T(8,128)(2,1)}, ...) custom-call(s32[1]{0:T(128)} %bitcast.68.me_ref, ...), custom_call_target="tpu_custom_call" | custom-call | flops 8192 | bytes 8192 | tf_op jit(solution)/shard_map/pallas_call | solution.py:777
  455.0 4.1 all-to-all-start.1
  459.1 11.2 %shard_map.270 = f32[1,704,2048]{2,1,0:T(8,128)} custom-call(bf16[1,512,704]{2,1,0:T(8,128)(2,1)} %bitcast.419, bf16[1,1024,704]{2,1,0:T(8,128)(2,1)} %bitcast.412, bf16[1,512,704]{2,1,0:T(8,128)(2,1)} %bitcast.420, bf16[512,2048]{1,0:T(8,128)(2,1)} %get-tuple-element.347.refs_3_, bf16[1024,2048]{1,0:T(8,128)(2,1)} %get-tuple-element.348.refs_4_, ...), custom_call_target="tpu_custom_call" | custom-call | flops 2048 | bytes 2048 | tf_op jit(solution)/shard_map/pallas_call | solution.py:1126
  470.2 8.4 shard_map.267
  478.7 8.4 shard_map.269
  487.0 12.5 %shard_map.268 = (bf16[8,128,2048]{2,1,0:T(8,128)(2,1)}, bf16[8,128,2048]{2,1,0:T(8,128)(2,1)}) custom-call(bf16[1024,704]{1,0:T(8,128)(2,1)} %get-tuple-element.337.act, bf16[8,128,128]{2,1,0:T(8,128)(2,1)} %get-tuple-element.338.sact_own, bf16[8,128,128]{2,1,0:T(8,128)(2,1)} %get-tuple-element.339.sact_other, f32[8,128,128]{2,1,0:T(8,128)} %slice.718.meta_own, ...), custom_call_target="tpu_custom_call" | custom-call | flops 268435456 | bytes 2097152 | tf_op jit(solution)/shard_map/pallas_call | solution.py:1158
  499.5 12.2 %all-to-all-done.1 = bf16[266,16,128]{2,0,1:T(8,128)(2,1)S(1)} async-done(((bf16[266,16,128]{2,0,1:T(8,128)(2,1)}), bf16[266,16,128]{2,0,1:T(8,128)(2,1)S(1)}, u32[]{:S(2)}, u32[]{:S(2)}) %all-to-all-start.1) | async-done | bytes 1089568 | tf_op jit(solution)/shard_map/all_to_all | solution.py:1487
  511.7 5.9 fusion.10
  521.3 22.8 %shard_map.271 = f32[2,704,2048]{2,1,0:T(8,128)} custom-call(bf16[2,512,704]{2,1,0:T(8,128)(2,1)} %get-tuple-element.366.refs_0_, bf16[2,1024,704]{2,1,0:T(8,128)(2,1)} %get-tuple-element.367.refs_1_, bf16[2,512,704]{2,1,0:T(8,128)(2,1)} %get-tuple-element.368.refs_2_, bf16[512,2048]{1,0:T(8,128)(2,1)} %get-tuple-element.369.refs_3_, ...), custom_call_target="tpu_custom_call" | custom-call | flops 2048 | bytes 2048 | tf_op jit(solution)/shard_map/pallas_call | solution.py:1126
  551.1 4.6 fusion.9
  561.2 7.7 collective-permute-done.52
  568.9 32.1 %collective-permute-done.53 = bf16[128,2048]{1,0:T(8,128)(2,1)S(1)} collective-permute-done((bf16[128,2048]{1,0:T(8,128)(2,1)S(1)}, bf16[128,2048]{1,0:T(8,128)(2,1)S(1)}, u32[]{:S(2)}, u32[]{:S(2)}) %collective-permute-start.53) | collective-permute-done | bytes 524320 | tf_op jit(solution)/shard_map/ppermute | solution.py:418
  606.6 10.1 %collective-permute-done.57 = bf16[128,2048]{1,0:T(8,128)(2,1)S(1)} collective-permute-done((bf16[128,2048]{1,0:T(8,128)(2,1)S(1)}, bf16[128,2048]{1,0:T(8,128)(2,1)S(1)}, u32[]{:S(2)}, u32[]{:S(2)}) %collective-permute-start.57) | collective-permute-done | bytes 524320 | tf_op jit(solution)/shard_map/ppermute | solution.py:412
  616.6 13.3 %collective-permute-done.56 = bf16[128,2048]{1,0:T(8,128)(2,1)S(1)} collective-permute-done((bf16[128,2048]{1,0:T(8,128)(2,1)S(1)}, bf16[128,2048]{1,0:T(8,128)(2,1)S(1)}, u32[]{:S(2)}, u32[]{:S(2)}) %collective-permute-start.56) | collective-permute-done | bytes 524320 | tf_op jit(solution)/shard_map/ppermute | solution.py:412
  632.0 4.1 fusion.6
  637.4 22.0 %shard_map.272 = (bf16[2048,640]{1,0:T(8,128)(2,1)}, bf16[512,512]{1,0:T(8,128)(2,1)}, bf16[4,128,2048]{2,1,0:T(8,128)(2,1)}, bf16[4,128,2048]{2,1,0:T(8,128)(2,...) custom-call(s32[1]{0:T(128)} %bitcast.core_ref, bf16[4,128,2048]{2,1,0:T(8,128)(2,1)} %copy-done.21, ...), custom_call_target="tpu_custom_call" | custom-call | flops 536870912 | bytes 4194304 | tf_op jit(solution)/shard_map/pallas_call | solution.py:1066
  670.9 3.0 collective-permute-start.61
  677.6 12.3 %collective-permute-done.61 = bf16[512,768]{1,0:T(8,128)(2,1)S(1)} collective-permute-done((bf16[512,768]{1,0:T(8,128)(2,1)S(1)}, bf16[512,768]{1,0:T(8,128)(2,1)S(1)}, u32[]{:S(2)}, u32[]{:S(2)}) %collective-permute-start.61) | collective-permute-done | bytes 786464 | tf_op jit(solution)/shard_map/ppermute | solution.py:529
  694.0 4.7 collective-permute-start.67
  698.8 4.0 fusion.5
  706.0 7.0 collective-permute-done.67
  716.2 5.6 collective-permute-start.73
  731.0 5.1 collective-permute-done.76
  736.1 5.1 collective-permute-start.81
  743.2 6.3 collective-permute-done.81
  759.8 3.7 collective-permute-start.85
  767.5 4.8 collective-permute-start.83
  779.2 4.0 collective-permute-done.83
  793.3 4.6 fusion.38
  798.6 6.3 all-to-all-start.2
  820.4 3.3 collective-permute-start.89
  827.0 3.9 collective-permute-start.96
  833.2 5.5 collective-permute-done.96
  838.6 3.1 collective-permute-done.94
  841.8 5.5 collective-permute-start.97
  861.2 4.0 maximum_select_fusion.1
  (669 shorter events, 272.0 us)
Async XLA Ops:
  28.8 21.9 %collective-permute-start.15 = (bf16[4,128,768]{2,1,0:T(8,128)(2,1)}, bf16[4,128,768]{2,1,0:T(8,128)(2,1)}, u32[]{:S(2)}, u32[]{:S(2)}) collective-permute-start(bf16[4,128,768]{2,1,0:T(8,128)(2,1)} %pad_maximum_fusion.15), channel_id=1, source_target_pairs={{8,0},{10,2},{12,4},{14,6},{16,8},{18,10},{20,12},{22,14},{24,16},... | collective-permute-start | bytes 2359304 | tf_op jit(solution)/shard_map/ppermute | solution.py:447
  30.0 21.9 %collective-permute-start.12 = (bf16[4,128,768]{2,1,0:T(8,128)(2,1)}, bf16[4,128,768]{2,1,0:T(8,128)(2,1)}, u32[]{:S(2)}, u32[]{:S(2)}) collective-permute-start(bf16[4,128,768]{2,1,0:T(8,128)(2,1)} %pad_maximum_fusion.15), channel_id=1, source_target_pairs={{0,8},{2,10},{4,12},{6,14},{8,16},{10,18},{12,20},{14,22},{16,24},... | collective-permute-start | bytes 2359304 | tf_op jit(solution)/shard_map/ppermute | solution.py:447
  38.2 19.7 %collective-permute-start.9 = (bf16[2,128,4,384]{3,1,2,0:T(8,128)(2,1)}, bf16[2,128,4,384]{3,1,2,0:T(8,128)(2,1)}, u32[]{:S(2)}, u32[]{:S(2)}) collective-permute-start(bf16[2,128,4,384]{3,1,2,0:T(8,128)(2,1)} %pad_maximum_fusion.16), channel_id=1, source_target_pairs={{0,4},{2,6},{4,0},{6,2},{8,12},{10,14},{12,8},{14,10},{16,20},{18,... | collective-permute-start | bytes 2359304 | tf_op jit(solution)/shard_map/ppermute | solution.py:412
  40.4 24.8 %collective-permute-start.7 = (bf16[2,128,2048]{2,1,0:T(8,128)(2,1)S(1)}, bf16[2,128,2048]{2,1,0:T(8,128)(2,1)S(1)}, u32[]{:S(2)}, u32[]{:S(2)}) collective-permute-start(bf16[2,128,2048]{2,1,0:T(8,128)(2,1)S(1)} %pad_maximum_fusion.13), channel_id=1, source_target_pairs={{0,2},{2,0},{4,6},{6,4},{8,10},{10,8},{12,14},{14,12},{16,18},{18,... | collective-permute-start | bytes 3145736 | tf_op jit(solution)/shard_map/ppermute | solution.py:412
  50.7 20.9 %collective-permute-start.16 = (bf16[4,128,768]{2,1,0:T(8,128)(2,1)}, bf16[4,128,768]{2,1,0:T(8,128)(2,1)}, u32[]{:S(2)}, u32[]{:S(2)}) collective-permute-start(bf16[4,128,768]{2,1,0:T(8,128)(2,1)} %collective-permute-done.15), channel_id=1, source_target_pairs={{8,0},{10,2},{12,4},{14,6},{16,8},{18,10},{20,12},{22,14},{24,16},... | collective-permute-start | bytes 2359304 | tf_op jit(solution)/shard_map/ppermute | solution.py:447
  52.0 20.9 %collective-permute-start.13 = (bf16[4,128,768]{2,1,0:T(8,128)(2,1)}, bf16[4,128,768]{2,1,0:T(8,128)(2,1)}, u32[]{:S(2)}, u32[]{:S(2)}) collective-permute-start(bf16[4,128,768]{2,1,0:T(8,128)(2,1)} %collective-permute-done.12), channel_id=1, source_target_pairs={{0,8},{2,10},{4,12},{6,14},{8,16},{10,18},{12,20},{14,22},{16,24},... | collective-permute-start | bytes 2359304 | tf_op jit(solution)/shard_map/ppermute | solution.py:447
  62.6 25.0 %collective-permute-start.10 = (bf16[16,64,768]{2,1,0:T(8,128)(2,1)}, bf16[16,64,768]{2,1,0:T(8,128)(2,1)}, u32[]{:S(2)}, u32[]{:S(2)}) collective-permute-start(bf16[16,64,768]{2,1,0:T(8,128)(2,1)} %pad_maximum_fusion.9), channel_id=1, source_target_pairs={{0,1},{1,0},{2,3},{3,2},{4,5},{5,4},{6,7},{7,6},{8,9},{9,8},{10,11... | collective-permute-start | bytes 4718600 | tf_op jit(solution)/shard_map/ppermute | solution.py:385
  66.9 28.7 %collective-permute-start.11 = (bf16[4,128,2048]{2,1,0:T(8,128)(2,1)}, bf16[4,128,2048]{2,1,0:T(8,128)(2,1)}, u32[]{:S(2)}, u32[]{:S(2)}) collective-permute-start(bf16[4,128,2048]{2,1,0:T(8,128)(2,1)} %pad_maximum_fusion.x_own), channel_id=1, source_target_pairs={{0,1},{1,0},{2,3},{3,2},{4,5},{5,4},{6,7},{7,6},{8,9},{9,8},{10,11... | collective-permute-start | bytes 6291464 | tf_op jit(solution)/shard_map/ppermute | solution.py:385
  71.6 23.2 %collective-permute-start.17 = (bf16[4,128,768]{2,1,0:T(8,128)(2,1)}, bf16[4,128,768]{2,1,0:T(8,128)(2,1)}, u32[]{:S(2)}, u32[]{:S(2)}) collective-permute-start(bf16[4,128,768]{2,1,0:T(8,128)(2,1)} %collective-permute-done.16), channel_id=1, source_target_pairs={{8,0},{10,2},{12,4},{14,6},{16,8},{18,10},{20,12},{22,14},{24,16},... | collective-permute-start | bytes 2359304 | tf_op jit(solution)/shard_map/ppermute | solution.py:447
  72.9 22.8 %collective-permute-start.14 = (bf16[4,128,768]{2,1,0:T(8,128)(2,1)}, bf16[4,128,768]{2,1,0:T(8,128)(2,1)}, u32[]{:S(2)}, u32[]{:S(2)}) collective-permute-start(bf16[4,128,768]{2,1,0:T(8,128)(2,1)} %collective-permute-done.13), channel_id=1, source_target_pairs={{0,8},{2,10},{4,12},{6,14},{8,16},{10,18},{12,20},{14,22},{16,24},... | collective-permute-start | bytes 2359304 | tf_op jit(solution)/shard_map/ppermute | solution.py:447
  100.4 31.2 %collective-permute-start.20 = (bf16[128,2048]{1,0:T(8,128)(2,1)}, bf16[128,2048]{1,0:T(8,128)(2,1)}, u32[]{:S(2)}, u32[]{:S(2)}) collective-permute-start(bf16[128,2048]{1,0:T(8,128)(2,1)} %constant_dynamic-slice_fusion.34), channel_id=1, source_target_pairs={{0,24},{2,26},{4,28},{6,30},{8,0},{10,2},{12,4},{14,6},{16,8},{18,... | collective-permute-start | bytes 1572872 | tf_op jit(solution)/shard_map/ppermute | solution.py:418
  106.7 43.7 %collective-permute-start.19 = (bf16[128,2048]{1,0:T(8,128)(2,1)}, bf16[128,2048]{1,0:T(8,128)(2,1)}, u32[]{:S(2)}, u32[]{:S(2)}) collective-permute-start(bf16[128,2048]{1,0:T(8,128)(2,1)} %constant_dynamic-slice_fusion.34), channel_id=1, source_target_pairs={{0,16},{2,18},{4,20},{6,22},{8,24},{10,26},{12,28},{14,30},{16,0},... | collective-permute-start | bytes 1572872 | tf_op jit(solution)/shard_map/ppermute | solution.py:418
  106.7 43.7 %collective-permute-start.18 = (bf16[128,2048]{1,0:T(8,128)(2,1)}, bf16[128,2048]{1,0:T(8,128)(2,1)}, u32[]{:S(2)}, u32[]{:S(2)}) collective-permute-start(bf16[128,2048]{1,0:T(8,128)(2,1)} %constant_dynamic-slice_fusion.34), channel_id=1, source_target_pairs={{0,8},{2,10},{4,12},{6,14},{8,16},{10,18},{12,20},{14,22},{16,24},... | collective-permute-start | bytes 1572872 | tf_op jit(solution)/shard_map/ppermute | solution.py:418
  161.4 25.2 %collective-permute-start.24 = (bf16[128,2048]{1,0:T(8,128)(2,1)S(1)}, bf16[128,2048]{1,0:T(8,128)(2,1)S(1)}, u32[]{:S(2)}, u32[]{:S(2)}) collective-permute-start(bf16[128,2048]{1,0:T(8,128)(2,1)S(1)} %get-tuple-element.608), channel_id=1, source_target_pairs={{0,6},{2,4},{4,2},{6,0},{8,14},{10,12},{12,10},{14,8},{16,22},{18,... | collective-permute-start | bytes 1572872 | tf_op jit(solution)/shard_map/ppermute | solution.py:412
  163.3 24.2 %collective-permute-start.23 = (bf16[128,2048]{1,0:T(8,128)(2,1)S(1)}, bf16[128,2048]{1,0:T(8,128)(2,1)S(1)}, u32[]{:S(2)}, u32[]{:S(2)}) collective-permute-start(bf16[128,2048]{1,0:T(8,128)(2,1)S(1)} %get-tuple-element.609), channel_id=1, source_target_pairs={{0,4},{2,6},{4,0},{6,2},{8,12},{10,14},{12,8},{14,10},{16,20},{18,... | collective-permute-start | bytes 1572872 | tf_op jit(solution)/shard_map/ppermute | solution.py:412
  169.1 28.8 %collective-permute-start.30 = (bf16[4,128,2048]{2,1,0:T(8,128)(2,1)}, bf16[4,128,2048]{2,1,0:T(8,128)(2,1)}, u32[]{:S(2)}, u32[]{:S(2)}) collective-permute-start(bf16[4,128,2048]{2,1,0:T(8,128)(2,1)} %pad_maximum_fusion.1.dy_own), channel_id=1, source_target_pairs={{0,1},{1,0},{2,3},{3,2},{4,5},{5,4},{6,7},{7,6},{8,9},{9,8},{10,11... | collective-permute-start | bytes 6291464 | tf_op jit(solution)/shard_map/ppermute | solution.py:385
  169.9 72.7 %collective-permute-start.29 = (bf16[4,128,2048]{2,1,0:T(8,128)(2,1)}, bf16[4,128,2048]{2,1,0:T(8,128)(2,1)}, u32[]{:S(2)}, u32[]{:S(2)}) collective-permute-start(bf16[4,128,2048]{2,1,0:T(8,128)(2,1)} %pad_maximum_fusion.1.dy_own), channel_id=1, source_target_pairs={{0,4},{2,6},{4,0},{6,2},{8,12},{10,14},{12,8},{14,10},{16,20},{18,... | collective-permute-start | bytes 6291464 | tf_op jit(solution)/shard_map/ppermute | solution.py:412
  174.4 68.2 %collective-permute-start.28 = (bf16[4,128,2048]{2,1,0:T(8,128)(2,1)}, bf16[4,128,2048]{2,1,0:T(8,128)(2,1)}, u32[]{:S(2)}, u32[]{:S(2)}) collective-permute-start(bf16[4,128,2048]{2,1,0:T(8,128)(2,1)} %pad_maximum_fusion.1.dy_own), channel_id=1, source_target_pairs={{0,2},{2,0},{4,6},{6,4},{8,10},{10,8},{12,14},{14,12},{16,18},{18,... | collective-permute-start | bytes 6291464 | tf_op jit(solution)/shard_map/ppermute | solution.py:412
  188.3 76.5 %all-to-all-start = ((bf16[16,264,128]{2,1,0:T(8,128)(2,1)}), bf16[16,264,128]{2,1,0:T(8,128)(2,1)}, u32[]{:S(2)}, u32[]{:S(2)}) async-start(bf16[16,264,128]{2,1,0:T(8,128)(2,1)} %bitcast.414), calls=%async_computation | async-start | bytes 2162688 | tf_op jit(solution)/shard_map/all_to_all | solution.py:1398
  193.4 49.2 %collective-permute-start.27 = (bf16[128,2048]{1,0:T(8,128)(2,1)S(1)}, bf16[128,2048]{1,0:T(8,128)(2,1)}, u32[]{:S(2)}, u32[]{:S(2)}) collective-permute-start(bf16[128,2048]{1,0:T(8,128)(2,1)S(1)} %multiply_convert_fusion), channel_id=1, source_target_pairs={{0,24},{2,26},{4,28},{6,30},{8,0},{10,2},{12,4},{14,6},{16,8},{18,... | collective-permute-start | bytes 1572872 | tf_op jit(solution)/shard_map/ppermute | solution.py:418
  196.6 68.2 %collective-permute-start.26 = (bf16[128,2048]{1,0:T(8,128)(2,1)S(1)}, bf16[128,2048]{1,0:T(8,128)(2,1)}, u32[]{:S(2)}, u32[]{:S(2)}) collective-permute-start(bf16[128,2048]{1,0:T(8,128)(2,1)S(1)} %multiply_convert_fusion), channel_id=1, source_target_pairs={{0,16},{2,18},{4,20},{6,22},{8,24},{10,26},{12,28},{14,30},{16,0},... | collective-permute-start | bytes 1572872 | tf_op jit(solution)/shard_map/ppermute | solution.py:418
  197.9 66.9 %collective-permute-start.25 = (bf16[128,2048]{1,0:T(8,128)(2,1)S(1)}, bf16[128,2048]{1,0:T(8,128)(2,1)}, u32[]{:S(2)}, u32[]{:S(2)}) collective-permute-start(bf16[128,2048]{1,0:T(8,128)(2,1)S(1)} %multiply_convert_fusion), channel_id=1, source_target_pairs={{0,8},{2,10},{4,12},{6,14},{8,16},{10,18},{12,20},{14,22},{16,24},... | collective-permute-start | bytes 1572872 | tf_op jit(solution)/shard_map/ppermute | solution.py:418
  274.0 50.2 %collective-permute-start.34 = (bf16[8,128,2048]{2,1,0:T(8,128)(2,1)}, bf16[8,128,2048]{2,1,0:T(8,128)(2,1)}, u32[]{:S(2)}, u32[]{:S(2)}) collective-permute-start(bf16[8,128,2048]{2,1,0:T(8,128)(2,1)} %constant_dynamic-update-slice_fusion.1.dy_own), channel_id=1, source_target_pairs={{0,1},{1,0},{2,3},{3,2},{4,5},{5,4},{6,7},{7,6},{8,9},{9,8},{10,11... | collective-permute-start | bytes 12582920 | tf_op jit(solution)/shard_map/ppermute | solution.py:385
  276.5 47.2 %collective-permute-start.32 = (bf16[4,128,2048]{2,1,0:T(8,128)(2,1)}, bf16[4,128,2048]{2,1,0:T(8,128)(2,1)S(1)}, u32[]{:S(2)}, u32[]{:S(2)}) collective-permute-start(bf16[4,128,2048]{2,1,0:T(8,128)(2,1)} %pad_maximum_fusion.2.hn_own), channel_id=1, source_target_pairs={{0,4},{2,6},{4,0},{6,2},{8,12},{10,14},{12,8},{14,10},{16,20},{18,... | collective-permute-start | bytes 6291464 | tf_op jit(solution)/shard_map/ppermute | solution.py:412
  277.4 46.8 %collective-permute-start.31 = (bf16[4,128,2048]{2,1,0:T(8,128)(2,1)}, bf16[4,128,2048]{2,1,0:T(8,128)(2,1)}, u32[]{:S(2)}, u32[]{:S(2)}) collective-permute-start(bf16[4,128,2048]{2,1,0:T(8,128)(2,1)} %pad_maximum_fusion.2.hn_own), channel_id=1, source_target_pairs={{0,2},{2,0},{4,6},{6,4},{8,10},{10,8},{12,14},{14,12},{16,18},{18,... | collective-permute-start | bytes 6291464 | tf_op jit(solution)/shard_map/ppermute | solution.py:412
  337.9 50.2 %collective-permute-start.37 = (bf16[4,64,2048]{2,1,0:T(8,128)(2,1)}, bf16[4,64,2048]{2,1,0:T(8,128)(2,1)S(1)}, u32[]{:S(2)}, u32[]{:S(2)}) collective-permute-start(bf16[4,64,2048]{2,1,0:T(8,128)(2,1)} %slice.715), channel_id=1, source_target_pairs={{0,2},{2,0},{4,6},{6,4},{8,10},{10,8},{12,14},{14,12},{16,18},{18,... | collective-permute-start | bytes 3145736 | tf_op jit(solution)/shard_map/ppermute | solution.py:412
  339.1 49.1 %collective-permute-start.36 = (bf16[4,64,2048]{2,1,0:T(8,128)(2,1)}, bf16[4,64,2048]{2,1,0:T(8,128)(2,1)S(1)}, u32[]{:S(2)}, u32[]{:S(2)}) collective-permute-start(bf16[4,64,2048]{2,1,0:T(8,128)(2,1)} %slice.714), channel_id=1, source_target_pairs={{0,4},{2,6},{4,0},{6,2},{8,12},{10,14},{12,8},{14,10},{16,20},{18,... | collective-permute-start | bytes 3145736 | tf_op jit(solution)/shard_map/ppermute | solution.py:412
  339.4 48.8 %collective-permute-start.39 = (bf16[4,64,2048]{2,1,0:T(8,128)(2,1)}, bf16[4,64,2048]{2,1,0:T(8,128)(2,1)}, u32[]{:S(2)}, u32[]{:S(2)}) collective-permute-start(bf16[4,64,2048]{2,1,0:T(8,128)(2,1)} %slice.717), channel_id=1, source_target_pairs={{0,2},{2,0},{4,6},{6,4},{8,10},{10,8},{12,14},{14,12},{16,18},{18,... | collective-permute-start | bytes 3145736 | tf_op jit(solution)/shard_map/ppermute | solution.py:412
  340.0 48.2 %collective-permute-start.38 = (bf16[4,64,2048]{2,1,0:T(8,128)(2,1)}, bf16[4,64,2048]{2,1,0:T(8,128)(2,1)}, u32[]{:S(2)}, u32[]{:S(2)}) collective-permute-start(bf16[4,64,2048]{2,1,0:T(8,128)(2,1)} %slice.716), channel_id=1, source_target_pairs={{0,4},{2,6},{4,0},{6,2},{8,12},{10,14},{12,8},{14,10},{16,20},{18,... | collective-permute-start | bytes 3145736 | tf_op jit(solution)/shard_map/ppermute | solution.py:412
  390.9 51.0 %collective-permute-start.41 = (bf16[8,128,2048]{2,1,0:T(8,128)(2,1)}, bf16[8,128,2048]{2,1,0:T(8,128)(2,1)}, u32[]{:S(2)}, u32[]{:S(2)}) collective-permute-start(bf16[8,128,2048]{2,1,0:T(8,128)(2,1)} %get-tuple-element.306), channel_id=1, source_target_pairs={{0,1},{1,0},{2,3},{3,2},{4,5},{5,4},{6,7},{7,6},{8,9},{9,8},{10,11... | collective-permute-start | bytes 12582920 | tf_op jit(solution)/shard_map/ppermute | solution.py:385
  394.9 49.9 %collective-permute-start.35 = (bf16[4,128,2048]{2,1,0:T(8,128)(2,1)}, bf16[4,128,2048]{2,1,0:T(8,128)(2,1)}, u32[]{:S(2)}, u32[]{:S(2)}) collective-permute-start(bf16[4,128,2048]{2,1,0:T(8,128)(2,1)} %get-tuple-element.288), channel_id=1, source_target_pairs={{0,1},{1,0},{2,3},{3,2},{4,5},{5,4},{6,7},{7,6},{8,9},{9,8},{10,11... | collective-permute-start | bytes 6291464 | tf_op jit(solution)/shard_map/ppermute | solution.py:385
  452.3 59.4 %collective-permute-start.46 = (bf16[2,4,64,2048]{3,2,1,0:T(8,128)(2,1)}, bf16[2,4,64,2048]{3,2,1,0:T(8,128)(2,1)}, u32[]{:S(2)}, u32[]{:S(2)}) collective-permute-start(bf16[2,4,64,2048]{3,2,1,0:T(8,128)(2,1)} %pad_maximum_fusion.3), channel_id=1, source_target_pairs={{0,4},{2,6},{4,0},{6,2},{8,12},{10,14},{12,8},{14,10},{16,20},{18,... | collective-permute-start | bytes 6291464 | tf_op jit(solution)/shard_map/ppermute | solution.py:412
  453.0 58.7 %collective-permute-start.47 = (bf16[2,4,64,2048]{3,2,1,0:T(8,128)(2,1)}, bf16[2,4,64,2048]{3,2,1,0:T(8,128)(2,1)}, u32[]{:S(2)}, u32[]{:S(2)}) collective-permute-start(bf16[2,4,64,2048]{3,2,1,0:T(8,128)(2,1)} %pad_maximum_fusion.4), channel_id=1, source_target_pairs={{0,2},{2,0},{4,6},{6,4},{8,10},{10,8},{12,14},{14,12},{16,18},{18,... | collective-permute-start | bytes 6291464 | tf_op jit(solution)/shard_map/ppermute | solution.py:412
  455.0 56.7 %all-to-all-start.1 = ((bf16[266,16,128]{2,0,1:T(8,128)(2,1)}), bf16[266,16,128]{2,0,1:T(8,128)(2,1)S(1)}, u32[]{:S(2)}, u32[]{:S(2)}) async-start(bf16[266,16,128]{2,0,1:T(8,128)(2,1)} %pad_maximum_fusion.11), calls=%async_computation.1 | async-start | bytes 2228224 | tf_op jit(solution)/shard_map/all_to_all | solution.py:1487
  517.6 28.8 %collective-permute-start.50 = (bf16[8,128,2048]{2,1,0:T(8,128)(2,1)}, bf16[8,128,2048]{2,1,0:T(8,128)(2,1)}, u32[]{:S(2)}, u32[]{:S(2)}) collective-permute-start(bf16[8,128,2048]{2,1,0:T(8,128)(2,1)} %get-tuple-element.373), channel_id=1, source_target_pairs={{0,1},{1,0},{2,3},{3,2},{4,5},{5,4},{6,7},{7,6},{8,9},{9,8},{10,11... | collective-permute-start | bytes 12582920 | tf_op jit(solution)/shard_map/ppermute | solution.py:385
  519.2 25.2 %collective-permute-start.51 = (bf16[4,128,2048]{2,1,0:T(8,128)(2,1)}, bf16[4,128,2048]{2,1,0:T(8,128)(2,1)S(1)}, u32[]{:S(2)}, u32[]{:S(2)}) collective-permute-start(bf16[4,128,2048]{2,1,0:T(8,128)(2,1)} %get-tuple-element.375), channel_id=1, source_target_pairs={{0,1},{1,0},{2,3},{3,2},{4,5},{5,4},{6,7},{7,6},{8,9},{9,8},{10,11... | collective-permute-start | bytes 6291464 | tf_op jit(solution)/shard_map/ppermute | solution.py:385
  519.2 30.6 %collective-permute-start.48 = (bf16[4,64,2048]{2,1,0:T(8,128)(2,1)}, bf16[4,64,2048]{2,1,0:T(8,128)(2,1)}, u32[]{:S(2)}, u32[]{:S(2)}) collective-permute-start(bf16[4,64,2048]{2,1,0:T(8,128)(2,1)} %get-tuple-element.364), channel_id=1, source_target_pairs={{0,2},{2,0},{4,6},{6,4},{8,10},{10,8},{12,14},{14,12},{16,18},{18,... | collective-permute-start | bytes 3145736 | tf_op jit(solution)/shard_map/ppermute | solution.py:412
  521.0 28.8 %collective-permute-start.49 = (bf16[4,64,2048]{2,1,0:T(8,128)(2,1)}, bf16[4,64,2048]{2,1,0:T(8,128)(2,1)}, u32[]{:S(2)}, u32[]{:S(2)}) collective-permute-start(bf16[4,64,2048]{2,1,0:T(8,128)(2,1)} %get-tuple-element.365), channel_id=1, source_target_pairs={{0,4},{2,6},{4,0},{6,2},{8,12},{10,14},{12,8},{14,10},{16,20},{18,... | collective-permute-start | bytes 3145736 | tf_op jit(solution)/shard_map/ppermute | solution.py:412
  556.0 45.1 %collective-permute-start.53 = (bf16[128,2048]{1,0:T(8,128)(2,1)S(1)}, bf16[128,2048]{1,0:T(8,128)(2,1)S(1)}, u32[]{:S(2)}, u32[]{:S(2)}) collective-permute-start(bf16[128,2048]{1,0:T(8,128)(2,1)S(1)} %get-tuple-element.383), channel_id=1, source_target_pairs={{0,16},{2,18},{4,20},{6,22},{8,24},{10,26},{12,28},{14,30},{16,0},... | collective-permute-start | bytes 1572872 | tf_op jit(solution)/shard_map/ppermute | solution.py:418
  556.2 44.8 %collective-permute-start.54 = (bf16[128,2048]{1,0:T(8,128)(2,1)S(1)}, bf16[128,2048]{1,0:T(8,128)(2,1)S(1)}, u32[]{:S(2)}, u32[]{:S(2)}) collective-permute-start(bf16[128,2048]{1,0:T(8,128)(2,1)S(1)} %get-tuple-element.384), channel_id=1, source_target_pairs={{0,8},{2,10},{4,12},{6,14},{8,16},{10,18},{12,20},{14,22},{16,24},... | collective-permute-start | bytes 1572872 | tf_op jit(solution)/shard_map/ppermute | solution.py:418
  557.6 72.3 %collective-permute-start.58 = (bf16[2,4,64,2048]{3,2,1,0:T(8,128)(2,1)S(1)}, bf16[2,4,64,2048]{3,2,1,0:T(8,128)(2,1)S(1)}, u32[]{:S(2)}, u32[]{:S(2)}) collective-permute-start(bf16[2,4,64,2048]{3,2,1,0:T(8,128)(2,1)S(1)} %pad_maximum_fusion.5), channel_id=1, source_target_pairs={{0,4},{2,6},{4,0},{6,2},{8,12},{10,14},{12,8},{14,10},{16,20},{18,... | collective-permute-start | bytes 6291464 | tf_op jit(solution)/shard_map/ppermute | solution.py:412
  558.8 71.1 %collective-permute-start.59 = (bf16[2,4,64,2048]{3,2,1,0:T(8,128)(2,1)S(1)}, bf16[2,4,64,2048]{3,2,1,0:T(8,128)(2,1)S(1)}, u32[]{:S(2)}, u32[]{:S(2)}) collective-permute-start(bf16[2,4,64,2048]{3,2,1,0:T(8,128)(2,1)S(1)} %pad_maximum_fusion.6), channel_id=1, source_target_pairs={{0,2},{2,0},{4,6},{6,4},{8,10},{10,8},{12,14},{14,12},{16,18},{18,... | collective-permute-start | bytes 6291464 | tf_op jit(solution)/shard_map/ppermute | solution.py:412
  605.2 24.6 %collective-permute-start.56 = (bf16[128,2048]{1,0:T(8,128)(2,1)S(1)}, bf16[128,2048]{1,0:T(8,128)(2,1)S(1)}, u32[]{:S(2)}, u32[]{:S(2)}) collective-permute-start(bf16[128,2048]{1,0:T(8,128)(2,1)S(1)} %fusion.114), channel_id=1, source_target_pairs={{0,4},{2,6},{4,0},{6,2},{8,12},{10,14},{12,8},{14,10},{16,20},{18,... | collective-permute-start | bytes 1572872 | tf_op jit(solution)/shard_map/ppermute | solution.py:412
  605.4 24.5 %collective-permute-start.55 = (bf16[128,2048]{1,0:T(8,128)(2,1)S(1)}, bf16[128,2048]{1,0:T(8,128)(2,1)S(1)}, u32[]{:S(2)}, u32[]{:S(2)}) collective-permute-start(bf16[128,2048]{1,0:T(8,128)(2,1)S(1)} %fusion.114), channel_id=1, source_target_pairs={{0,2},{2,0},{4,6},{6,4},{8,10},{10,8},{12,14},{14,12},{16,18},{18,... | collective-permute-start | bytes 1572872 | tf_op jit(solution)/shard_map/ppermute | solution.py:412
  662.8 31.2 %collective-permute-start.72 = (bf16[4,128,2048]{2,1,0:T(8,128)(2,1)}, bf16[4,128,2048]{2,1,0:T(8,128)(2,1)}, u32[]{:S(2)}, u32[]{:S(2)}) collective-permute-start(bf16[4,128,2048]{2,1,0:T(8,128)(2,1)} %get-tuple-element.418), channel_id=1, source_target_pairs={{0,1},{1,0},{2,3},{3,2},{4,5},{5,4},{6,7},{7,6},{8,9},{9,8},{10,11... | collective-permute-start | bytes 6291464 | tf_op jit(solution)/shard_map/ppermute | solution.py:385
  663.6 26.3 %collective-permute-start.65 = (bf16[4,64,2048]{2,1,0:T(8,128)(2,1)}, bf16[4,64,2048]{2,1,0:T(8,128)(2,1)}, u32[]{:S(2)}, u32[]{:S(2)}) collective-permute-start(bf16[4,64,2048]{2,1,0:T(8,128)(2,1)} %get-tuple-element.412), channel_id=1, source_target_pairs={{0,2},{2,0},{4,6},{6,4},{8,10},{10,8},{12,14},{14,12},{16,18},{18,... | collective-permute-start | bytes 3145736 | tf_op jit(solution)/shard_map/ppermute | solution.py:412
  664.0 25.9 %collective-permute-start.66 = (bf16[4,64,2048]{2,1,0:T(8,128)(2,1)}, bf16[4,64,2048]{2,1,0:T(8,128)(2,1)}, u32[]{:S(2)}, u32[]{:S(2)}) collective-permute-start(bf16[4,64,2048]{2,1,0:T(8,128)(2,1)} %get-tuple-element.413), channel_id=1, source_target_pairs={{0,4},{2,6},{4,0},{6,2},{8,12},{10,14},{12,8},{14,10},{16,20},{18,... | collective-permute-start | bytes 3145736 | tf_op jit(solution)/shard_map/ppermute | solution.py:412
  670.9 19.0 %collective-permute-start.61 = (bf16[512,768]{1,0:T(8,128)(2,1)S(1)}, bf16[512,768]{1,0:T(8,128)(2,1)S(1)}, u32[]{:S(2)}, u32[]{:S(2)}) collective-permute-start(bf16[512,768]{1,0:T(8,128)(2,1)S(1)} %get-tuple-element.591), channel_id=1, source_target_pairs={{0,8},{2,10},{4,12},{6,14},{1,9},{3,11},{5,13},{7,15}} | collective-permute-start | bytes 2359304 | tf_op jit(solution)/shard_map/ppermute | solution.py:529
  694.0 19.0 %collective-permute-start.67 = (bf16[512,768]{1,0:T(8,128)(2,1)S(1)}, bf16[512,768]{1,0:T(8,128)(2,1)S(1)}, u32[]{:S(2)}, u32[]{:S(2)}) collective-permute-start(bf16[512,768]{1,0:T(8,128)(2,1)S(1)} %get-tuple-element.589), channel_id=1, source_target_pairs={{0,8},{2,10},{4,12},{6,14},{8,16},{10,18},{12,20},{14,22},{1,9},{3... | collective-permute-start | bytes 2359304 | tf_op jit(solution)/shard_map/ppermute | solution.py:529
  703.2 19.1 %collective-permute-start.78 = (bf16[128,2048]{1,0:T(8,128)(2,1)S(1)}, bf16[128,2048]{1,0:T(8,128)(2,1)S(1)}, u32[]{:S(2)}, u32[]{:S(2)}) collective-permute-start(bf16[128,2048]{1,0:T(8,128)(2,1)S(1)} %get-tuple-element.600), channel_id=1, source_target_pairs={{0,2},{2,0},{4,6},{6,4},{8,10},{10,8},{12,14},{14,12},{16,18},{18,... | collective-permute-start | bytes 1572872 | tf_op jit(solution)/shard_map/ppermute | solution.py:412
  704.2 21.4 %collective-permute-start.80 = (bf16[128,2048]{1,0:T(8,128)(2,1)S(1)}, bf16[128,2048]{1,0:T(8,128)(2,1)S(1)}, u32[]{:S(2)}, u32[]{:S(2)}) collective-permute-start(bf16[128,2048]{1,0:T(8,128)(2,1)S(1)} %get-tuple-element.601), channel_id=1, source_target_pairs={{0,6},{2,4},{4,2},{6,0},{8,14},{10,12},{12,10},{14,8},{16,22},{18,... | collective-permute-start | bytes 1572872 | tf_op jit(solution)/shard_map/ppermute | solution.py:412
  705.1 22.3 %collective-permute-start.79 = (bf16[128,2048]{1,0:T(8,128)(2,1)S(1)}, bf16[128,2048]{1,0:T(8,128)(2,1)S(1)}, u32[]{:S(2)}, u32[]{:S(2)}) collective-permute-start(bf16[128,2048]{1,0:T(8,128)(2,1)S(1)} %get-tuple-element.602), channel_id=1, source_target_pairs={{0,4},{2,6},{4,0},{6,2},{8,12},{10,14},{12,8},{14,10},{16,20},{18,... | collective-permute-start | bytes 1572872 | tf_op jit(solution)/shard_map/ppermute | solution.py:412
  714.9 34.6 %collective-permute-start.74 = (bf16[512,768]{1,0:T(8,128)(2,1)}, bf16[512,768]{1,0:T(8,128)(2,1)}, u32[]{:S(2)}, u32[]{:S(2)}) collective-permute-start(bf16[512,768]{1,0:T(8,128)(2,1)} %get-tuple-element.586), channel_id=1, source_target_pairs={{8,0},{10,2},{12,4},{14,6},{16,8},{18,10},{20,12},{22,14},{24,16},... | collective-permute-start | bytes 2359304 | tf_op jit(solution)/shard_map/ppermute | solution.py:529
  716.2 33.3 %collective-permute-start.73 = (bf16[512,768]{1,0:T(8,128)(2,1)}, bf16[512,768]{1,0:T(8,128)(2,1)}, u32[]{:S(2)}, u32[]{:S(2)}) collective-permute-start(bf16[512,768]{1,0:T(8,128)(2,1)} %get-tuple-element.587), channel_id=1, source_target_pairs={{0,8},{2,10},{4,12},{6,14},{8,16},{10,18},{12,20},{14,22},{16,24},... | collective-permute-start | bytes 2359304 | tf_op jit(solution)/shard_map/ppermute | solution.py:529
  727.4 15.8 %collective-permute-start.75 = (bf16[128,576]{1,0:T(8,128)(2,1)S(1)}, bf16[128,576]{1,0:T(8,128)(2,1)}, u32[]{:S(2)}, u32[]{:S(2)}) collective-permute-start(bf16[128,576]{1,0:T(8,128)(2,1)S(1)} %pad_maximum_fusion.22), channel_id=1, source_target_pairs={{0,2},{2,0},{4,6},{6,4},{8,10},{10,8},{12,14},{14,12},{16,18},{18,... | collective-permute-start | bytes 442376 | tf_op jit(solution)/shard_map/ppermute | solution.py:412
  752.8 14.7 %collective-permute-start.88 = (bf16[128,768]{1,0:T(8,128)(2,1)}, bf16[128,768]{1,0:T(8,128)(2,1)S(1)}, u32[]{:S(2)}, u32[]{:S(2)}) collective-permute-start(bf16[128,768]{1,0:T(8,128)(2,1)} %get-tuple-element.631), channel_id=1, source_target_pairs={{0,2},{2,0},{4,6},{6,4},{8,10},{10,8},{12,14},{14,12},{16,18},{18,... | collective-permute-start | bytes 589832 | tf_op jit(solution)/shard_map/ppermute | solution.py:412
  754.5 17.7 %collective-permute-start.87 = (bf16[128,768]{1,0:T(8,128)(2,1)}, bf16[128,768]{1,0:T(8,128)(2,1)S(1)}, u32[]{:S(2)}, u32[]{:S(2)}) collective-permute-start(bf16[128,768]{1,0:T(8,128)(2,1)} %get-tuple-element.632), channel_id=1, source_target_pairs={{0,4},{2,6},{4,0},{6,2},{8,12},{10,14},{12,8},{14,10},{16,20},{18,... | collective-permute-start | bytes 589832 | tf_op jit(solution)/shard_map/ppermute | solution.py:412
  755.1 17.8 %collective-permute-start.86 = (bf16[128,768]{1,0:T(8,128)(2,1)}, bf16[128,768]{1,0:T(8,128)(2,1)}, u32[]{:S(2)}, u32[]{:S(2)}) collective-permute-start(bf16[128,768]{1,0:T(8,128)(2,1)} %get-tuple-element.633), channel_id=1, source_target_pairs={{0,6},{2,4},{4,2},{6,0},{8,14},{10,12},{12,10},{14,8},{16,22},{18,... | collective-permute-start | bytes 589832 | tf_op jit(solution)/shard_map/ppermute | solution.py:412
  759.8 15.2 %collective-permute-start.85 = (bf16[4,128,576]{1,2,0:T(8,128)(2,1)}, bf16[4,128,576]{1,2,0:T(8,128)(2,1)}, u32[]{:S(2)}, u32[]{:S(2)}) collective-permute-start(bf16[4,128,576]{1,2,0:T(8,128)(2,1)} %copy.357), channel_id=1, source_target_pairs={{0,1},{1,0},{2,3},{3,2},{4,5},{5,4},{6,7},{7,6},{8,9},{9,8},{10,11... | collective-permute-start | bytes 1769480 | tf_op jit(solution)/shard_map/ppermute | solution.py:385
  767.5 15.6 %collective-permute-start.83 = (bf16[128,2048]{1,0:T(8,128)(2,1)}, bf16[128,2048]{1,0:T(8,128)(2,1)}, u32[]{:S(2)}, u32[]{:S(2)}) collective-permute-start(bf16[128,2048]{1,0:T(8,128)(2,1)} %get-tuple-element.597), channel_id=1, source_target_pairs={{0,8},{2,10},{4,12},{6,14},{8,16},{10,18},{12,20},{14,22},{1,9},{3... | collective-permute-start | bytes 1572872 | tf_op jit(solution)/shard_map/ppermute | solution.py:529
  798.6 56.2 %all-to-all-start.2 = ((f32[19,16,128]{2,0,1:T(8,128)}), f32[19,16,128]{2,0,1:T(8,128)}, u32[]{:S(2)}, u32[]{:S(2)}) async-start(f32[19,16,128]{2,0,1:T(8,128)} %pad_maximum_fusion.21), calls=%async_computation.2 | async-start | bytes 393216 | tf_op jit(solution)/shard_map/all_to_all | solution.py:1647
  820.4 26.8 %collective-permute-start.89 = (bf16[128,2048]{1,0:T(8,128)(2,1)S(1)}, bf16[128,2048]{1,0:T(8,128)(2,1)S(1)}, u32[]{:S(2)}, u32[]{:S(2)}) collective-permute-start(bf16[128,2048]{1,0:T(8,128)(2,1)S(1)} %get-tuple-element.594), channel_id=1, source_target_pairs={{0,8},{2,10},{4,12},{6,14},{8,16},{10,18},{12,20},{14,22},{16,24},... | collective-permute-start | bytes 1572872 | tf_op jit(solution)/shard_map/ppermute | solution.py:529
  823.7 23.5 %collective-permute-start.90 = (bf16[128,2048]{1,0:T(8,128)(2,1)S(1)}, bf16[128,2048]{1,0:T(8,128)(2,1)S(1)}, u32[]{:S(2)}, u32[]{:S(2)}) collective-permute-start(bf16[128,2048]{1,0:T(8,128)(2,1)S(1)} %get-tuple-element.595), channel_id=1, source_target_pairs={{8,0},{10,2},{12,4},{14,6},{16,8},{18,10},{20,12},{22,14},{24,16},... | collective-permute-start | bytes 1572872 | tf_op jit(solution)/shard_map/ppermute | solution.py:529
  841.8 14.5 %collective-permute-start.97 = (f32[128,288]{0,1:T(8,128)S(1)}, f32[128,288]{0,1:T(8,128)}, u32[]{:S(2)}, u32[]{:S(2)}) collective-permute-start(f32[128,288]{0,1:T(8,128)S(1)} %fusion.90), channel_id=1, source_target_pairs={{0,1},{1,0},{2,3},{3,2},{4,5},{5,4},{6,7},{7,6},{8,9},{9,8},{10,11... | collective-permute-start | bytes 442376 | tf_op jit(solution)/shard_map/ppermute | solution.py:385
  (151 other events, 2297.4 us)
